TPU v7x, 128 devices: a whole 4x4x4 slice. The times are simulated.
128 devices in a mesh: seq: 16 (over z, y), expert: 8 (over x, core).
Axes of the slice: x: 4, y: 4, z: 4, core: 2. Of those that a mesh axis runs over, the one named last changes fastest.
Arguments:
- tokens: bfloat16 [2048, 4096], P(('seq', 'expert')), may hold values from -6 to 6
- gain_mamba: float32 [4096], replicated, may hold values from 0.1 to 1.9
- in_weight: bfloat16 [2, 4096, 8192], P(None, 'seq', 'expert'), may hold values from -0.09375 to 0.09375
- conv_weight: float32 [4, 8192], P(None, 'expert'), may hold values from -3 to 3
- conv_bias: float32 [8192], P('expert'), may hold values from -3 to 3
- xproj_weight: bfloat16 [8192, 288], P('expert'), may hold values from -0.0625 to 0.0625
- dt_weight: bfloat16 [256, 8192], P(None, 'expert'), may hold values from -0.375 to 0.375
- dt_bias: float32 [8192], P('expert'), may hold values from -7 to -2
- a_rate: float32 [16, 8192], P(None, 'expert'), may hold values from 0.01 to 8
- skip_d: float32 [8192], P('expert'), may hold values from 0.5 to 1.5
- out_weight: bfloat16 [8192, 4096], P('expert', 'seq'), may hold values from -0.0625 to 0.0625
- gain_moe: float32 [4096], replicated, may hold values from 0.1 to 1.9
- expert_ids: int32 [2048, 2], P(('seq', 'expert')), may hold values from 0 to 15, all different within a row; in each aligned block of 16 rows (0 to 15, 16 to 31, ...) at most 4 rows name the same one
- gate_weights: float32 [2048, 2], P(('seq', 'expert')), may hold values from 0.2 to 1
- w_gate: bfloat16 [16, 4096, 7168], P('seq', None, 'expert'), may hold values from -0.09375 to 0.09375
- w_up: bfloat16 [16, 4096, 7168], P('seq', None, 'expert'), may hold values from -0.09375 to 0.09375
- w_down: bfloat16 [16, 7168, 4096], P('seq', 'expert'), may hold values from -0.0625 to 0.0625
Outputs:
- mixed: bfloat16 [2048, 4096], P(('seq', 'expert'))
Inputs may be any that keep to these rules, and one draw needn't show every extreme that they name: `expert_ids`: each row names 2 different experts. In each aligned block of 16 rows (the rows of one device) no expert is named by more than 4 rows, a bound that some block reaches.
All inputs are finite; a program needn't handle non-finite values.
Results may differ from a plain program's by a relative error of at most 0.03.
Values may be sent and summed in bfloat16 or wider, within the bound.
A program may use at most 192 MiB of HBM per device.

v0:
```python
import jax
import jax.numpy as jnp
from jax import lax
from jax.sharding import PartitionSpec as P

STATE = 16
CONV = 4
RANK = 256
TOP = 2


def from_behind(block, axis, distance):
    devices = range(lax.axis_size(axis))
    route = [(i - distance, i) for i in devices if i - distance in devices]
    return lax.ppermute(block, axis, route)


def rms_norm(values, gain):
    wide = values.astype(jnp.float32)
    return wide * lax.rsqrt(jnp.mean(wide * wide, axis=-1, keepdims=True) + 1e-05) * gain


def combine_states(earlier, later):
    return (earlier[0] * later[0], later[0] * earlier[1] + later[1])


def per_device(
    tokens,
    gain_mamba,
    in_weight,
    conv_weight,
    conv_bias,
    xproj_weight,
    dt_weight,
    dt_bias,
    a_rate,
    skip_d,
    out_weight,
    gain_moe,
    expert_ids,
    gate_weights,
    w_gate,
    w_up,
    w_down,
):
    rows, dim = tokens.shape
    n_seq = lax.axis_size("seq")
    n_exp = lax.axis_size("expert")
    group = lax.all_gather(tokens, "expert", axis=0, tiled=True)
    local_tok = group.shape[0]
    normed = rms_norm(group, gain_mamba).astype(jnp.bfloat16)
    both = jnp.einsum(
        "td,kdc->tkc",
        normed,
        lax.all_gather(in_weight, "seq", axis=1, tiled=True),
        preferred_element_type=jnp.float32,
    )
    xpart = both[:, 0]
    zpart = both[:, 1]
    edge = from_behind(xpart[local_tok - (CONV - 1) :], "seq", 1)
    padded = jnp.concatenate([edge, xpart], axis=0)
    conv = conv_bias
    for tap in range(CONV):
        conv = conv + conv_weight[tap] * padded[tap : tap + local_tok]
    inner = jax.nn.silu(conv).astype(jnp.bfloat16)
    partial_value = jnp.dot(inner, xproj_weight, preferred_element_type=jnp.float32)
    low_part, edge_part = (
        lax.psum(partial_value[:, :RANK].astype(jnp.bfloat16), "expert").astype(jnp.float32),
        lax.psum(partial_value[:, RANK:].astype(jnp.bfloat16), "expert").astype(jnp.float32),
    )
    dt_low = low_part.astype(jnp.bfloat16)
    bmat = edge_part[:, :STATE]
    cmat = edge_part[:, STATE:]
    step = jax.nn.softplus(jnp.dot(dt_low, dt_weight, preferred_element_type=jnp.float32) + dt_bias)
    inner_f = inner.astype(jnp.float32)
    decay = jnp.exp(-step[:, None, :] * a_rate[None, :, :])
    source = bmat[:, :, None] * (step * inner_f)[:, None, :]
    cumulative, states = lax.associative_scan(combine_states, (decay, source), axis=0)
    total = cumulative[-1]
    final = states[-1]

    def relay(turn, incoming):
        return from_behind((total * incoming + final).astype(jnp.bfloat16), "seq", 1).astype(
            jnp.float32
        )

    arriving = lax.fori_loop(0, n_seq - 1, relay, jnp.zeros_like(final))
    states = states + cumulative * arriving[None, :, :]
    readout = jnp.sum(cmat[:, :, None] * states, axis=1)
    gated = ((readout + skip_d * inner_f) * jax.nn.silu(zpart)).astype(jnp.bfloat16)
    terms = jnp.dot(
        gated,
        lax.all_gather(out_weight, "seq", axis=1, tiled=True),
        preferred_element_type=jnp.float32,
    )
    mixer = lax.psum_scatter(
        terms.astype(jnp.bfloat16), "expert", scatter_dimension=0, tiled=True
    ).astype(jnp.float32)
    resid = (tokens.astype(jnp.float32) + mixer).astype(jnp.bfloat16)
    normed2 = rms_norm(resid, gain_moe).astype(jnp.bfloat16)
    capacity = max(2, 4 * rows // n_seq)
    slots_all = n_seq * capacity
    flat_ids = expert_ids.reshape(-1)
    onehot = (flat_ids[:, None] == jnp.arange(n_seq, dtype=jnp.int32)[None, :]).astype(jnp.int32)
    before = jnp.cumsum(onehot, axis=0) - onehot
    slot = jnp.sum(before * onehot, axis=1)
    target = flat_ids * capacity + slot
    places = target[:, None] == jnp.arange(slots_all, dtype=jnp.int32)[None, :]
    dispatch_mat = jnp.any(places.reshape(rows, TOP, slots_all), axis=1).astype(jnp.bfloat16)
    send = jnp.einsum(
        "rp,rd->pd", dispatch_mat, normed2, preferred_element_type=jnp.float32
    ).astype(jnp.bfloat16)
    received = lax.all_to_all(
        send.reshape(n_seq, capacity, dim), "seq", split_axis=0, concat_axis=0, tiled=True
    )
    pooled = lax.all_gather(
        received.reshape(1, slots_all, dim), "expert", axis=0, tiled=True
    ).reshape(n_exp * slots_all, dim)
    gate = jnp.dot(pooled, w_gate[0], preferred_element_type=jnp.float32)
    upper = jnp.dot(pooled, w_up[0], preferred_element_type=jnp.float32)
    act = (jax.nn.silu(gate) * upper).astype(jnp.bfloat16)
    outputs = lax.psum_scatter(
        jnp.dot(act, w_down[0], preferred_element_type=jnp.float32).astype(jnp.bfloat16),
        "expert",
        scatter_dimension=0,
        tiled=True,
    )
    returned = lax.all_to_all(
        outputs.reshape(n_seq, capacity, dim), "seq", split_axis=0, concat_axis=0, tiled=True
    ).reshape(slots_all, dim)
    weighting = jnp.where(places, gate_weights.reshape(-1)[:, None], 0.0)
    weighting = jnp.sum(weighting.reshape(rows, TOP, slots_all), axis=1)
    moe = jnp.dot(weighting, returned.astype(jnp.float32), precision=lax.Precision.HIGHEST)
    return (resid.astype(jnp.float32) + moe).astype(jnp.bfloat16)


def solution(mesh):
    placed = (
        P(("seq", "expert"), None),
        P(),
        P(None, "seq", "expert"),
        P(None, "expert"),
        P("expert"),
        P("expert", None),
        P(None, "expert"),
        P("expert"),
        P(None, "expert"),
        P("expert"),
        P("expert", "seq"),
        P(),
        P(("seq", "expert"), None),
        P(("seq", "expert"), None),
        P("seq", None, "expert"),
        P("seq", None, "expert"),
        P("seq", "expert", None),
    )
    return jax.shard_map(
        per_device,
        mesh=mesh,
        in_specs=placed,
        out_specs=P(("seq", "expert"), None),
        check_vma=False,
    )
```

profile of v0, /device:TPU:0, one launch (start us, length us, event | category | flops | bytes accessed | tf_op | source)
XLA Modules:
  0.0 908.5 jit_solution(7577490913799089768)
XLA Ops:
  8.9 26.0 %all-gather.5.cloned.1.call-done = bf16[128,4096]{1,0:T(8,128)(2,1)} async-done(((bf16[16,4096]{1,0:T(8,128)(2,1)}), bf16[128,4096]{1,0:T(8,128)(2,1)}) %all-gather.5.cloned.1.call-update) | async-done | bytes 1048592 | tf_op jit(solution)/shard_map/all_gather | solution.py:49
  36.5 111.9 %all-gather.7.cloned.1.call-done = bf16[2,4096,1024]{2,1,0:T(8,128)(2,1)} async-done(((bf16[2,256,1024]{2,1,0:T(8,128)(2,1)}), bf16[2,4096,1024]{2,1,0:T(8,128)(2,1)}) %all-gather.7.cloned.1.call-update) | async-done | bytes 16777232 | tf_op jit(solution)/shard_map/all_gather | solution.py:55
  148.4 8.5 fusion.20
  163.9 14.0 %psum.14 = bf16[128,32]{0,1:T(8,128)(2,1)S(1)} all-reduce(bf16[128,32]{0,1:T(8,128)(2,1)S(1)} %slice.341), channel_id=1, replica_groups=mesh['seq'=16,'expert'=8] {'expert'}, use_global_device_ids=true, to_apply=%region_1.2 | all-reduce | flops 4096 | bytes 16384 | tf_op jit(solution)/shard_map/psum | solution.py:69
  178.7 44.8 %all-reduce.30.cloned.1.call-done = bf16[128,256]{0,1:T(8,128)(2,1)} async-done(((bf16[128,256]{0,1:T(8,128)(2,1)}), bf16[128,256]{0,1:T(8,128)(2,1)}) %all-reduce.30.cloned.1.call-update) | async-done | bytes 65552 | tf_op jit(solution)/shard_map/psum | solution.py:68
  233.5 10.9 %slice_add_fusion = (f32[64,16,1024]{2,1,0:T(8,128)S(1)}, f32[64,16,1024]{2,1,0:T(8,128)}) fusion(f32[128,16,1024]{2,1,0:T(8,128)} %copy-done.3, f32[128,16,1024]{2,1,0:T(8,128)} %copy-done.2), kind=kLoop, calls=%fused_computation.19 | loop fusion | flops 3145728 | bytes 25165824 | tf_op jit(solution)/shard_map/add | solution.py:24
  308.4 7.0 pad.108
  315.3 10.2 %pad.109 = f32[32,16,1024]{2,1,0:T(8,128)} pad(f32[16,16,1024]{2,1,0:T(8,128)} %add.263, f32[]{:T(128)} %constant.13.clone.1), padding=1_0_1x0_0_0x0_0_0 | pad | bytes 3145732 | tf_op jit(solution)/shard_map/pad | solution.py:78
  325.5 10.1 %pad.95 = f32[32,16,1024]{2,1,0:T(8,128)} pad(f32[16,16,1024]{2,1,0:T(8,128)} %add.253, f32[]{:T(128)} %constant.13.clone.1), padding=1_0_1x0_0_0x0_0_0 | pad | bytes 3145732 | tf_op jit(solution)/shard_map/pad | solution.py:78
  337.9 10.2 %pad.94 = f32[32,16,1024]{2,1,0:T(8,128)} pad(f32[16,16,1024]{2,1,0:T(8,128)} %pad_maximum_fusion.4, f32[]{:T(128)} %constant.13.clone.1), padding=0_1_1x0_0_0x0_0_0 | pad | bytes 3145732 | tf_op jit(solution)/shard_map/pad | solution.py:78
  348.1 4.3 add.255
  355.3 5.0 fusion.16
  362.0 18.6 %pad.96 = f32[64,16,1024]{2,1,0:T(8,128)} pad(f32[32,16,1024]{2,1,0:T(8,128)} %pad_maximum_fusion.2, f32[]{:T(128)} %constant.13.clone.1), padding=0_1_1x0_0_0x0_0_0 | pad | bytes 6291460 | tf_op jit(solution)/shard_map/pad | solution.py:78
  380.6 12.0 %pad.97 = f32[64,16,1024]{2,1,0:T(8,128)} pad(f32[32,16,1024]{2,1,0:T(8,128)S(1)} %copy-done.16, f32[]{:T(128)} %constant.13.clone.1), padding=1_0_1x0_0_0x0_0_0 | pad | bytes 6291460 | tf_op jit(solution)/shard_map/pad | solution.py:78
  392.5 6.8 add.257
  399.4 35.6 %pad.99 = f32[128,16,1024]{2,1,0:T(8,128)} pad(f32[64,16,1024]{2,1,0:T(8,128)} %add.257, f32[]{:T(128)} %constant.13.clone.1), padding=1_0_1x0_0_0x0_0_0 | pad | bytes 12582916 | tf_op jit(solution)/shard_map/pad | solution.py:78
  436.5 18.6 %pad.110 = f32[64,16,1024]{2,1,0:T(8,128)} pad(f32[32,16,1024]{2,1,0:T(8,128)} %pad_maximum_fusion.3, f32[]{:T(128)} %constant.13.clone.1), padding=0_1_1x0_0_0x0_0_0 | pad | bytes 6291460 | tf_op jit(solution)/shard_map/pad | solution.py:78
  455.1 11.9 %pad.111 = f32[64,16,1024]{2,1,0:T(8,128)} pad(f32[32,16,1024]{2,1,0:T(8,128)S(1)} %copy-done.15, f32[]{:T(128)} %constant.13.clone.1), padding=1_0_1x0_0_0x0_0_0 | pad | bytes 6291460 | tf_op jit(solution)/shard_map/pad | solution.py:78
  467.0 7.1 add.265
  475.6 7.6 fusion.12
  485.7 35.5 %pad.98 = f32[128,16,1024]{2,1,0:T(8,128)} pad(f32[64,16,1024]{2,1,0:T(8,128)} %pad_maximum_fusion, f32[]{:T(128)} %constant.13.clone.1), padding=0_1_1x0_0_0x0_0_0 | pad | bytes 12582916 | tf_op jit(solution)/shard_map/pad | solution.py:78
  521.2 35.5 %pad.113 = f32[128,16,1024]{2,1,0:T(8,128)} pad(f32[64,16,1024]{2,1,0:T(8,128)} %add.265, f32[]{:T(128)} %constant.13.clone.1), padding=1_0_1x0_0_0x0_0_0 | pad | bytes 12582916 | tf_op jit(solution)/shard_map/pad | solution.py:78
  556.8 4.8 pad_maximum_fusion.1
  561.5 35.5 %pad.112 = f32[128,16,1024]{2,1,0:T(8,128)} pad(f32[64,16,1024]{2,1,0:T(8,128)} %pad_maximum_fusion.1, f32[]{:T(128)} %constant.13.clone.1), padding=0_1_1x0_0_0x0_0_0 | pad | bytes 12582916 | tf_op jit(solution)/shard_map/pad | solution.py:78
  598.8 107.7 %while.11 = (s32[]{:T(128)}, f32[16,1024]{1,0:T(8,128)S(1)}, f32[16,1024]{1,0:T(8,128)S(1)}, f32[16,1024]{1,0:T(8,128)S(1)}, s32[]{:T(128)}, /*index=5*/s32[]{:T(128)}) while((s32[]{:T(128)}, f32[16,1024]{1,0:T(8,128)S(1)}, f32[16,1024]{1,0:T(8,128)S(1)}, f32[16,1024]{1,0:T(8,128)S(1)}, s32[]{:T(128)}, /*index=5*/s32[]{:T(128)}) %tuple.47), condition=%wide.region_4.5_spmd.clone, body=%wide.region_3.4_spmd.clone.sunk | while | flops 81923 | bytes 458871 | solution.py:87
  603.9 4.2 collective-permute-start
  609.7 4.3 collective-permute-start
  621.5 4.2 collective-permute-start
  627.3 5.6 collective-permute-start
  634.5 6.5 collective-permute-start
  642.6 6.5 collective-permute-start
  650.7 6.3 collective-permute-start
  658.6 6.3 collective-permute-start
  666.6 6.3 collective-permute-start
  674.6 6.2 collective-permute-start
  682.5 6.3 collective-permute-start
  690.4 6.5 collective-permute-start
  698.5 6.3 collective-permute-start
  706.5 14.0 %multiply_reduce_fusion = f32[128,1024]{1,0:T(8,128)S(1)} fusion(f32[128,16,1024]{2,1,0:T(8,128)} %pad.112, f32[128,16,1024]{2,1,0:T(8,128)} %pad.113, f32[128,16,1024]{2,1,0:T(8,128)} %pad.98, f32[128,16,1024]{2,1,0:T(8,128)} %pad.99, f32[16,1024]{1,0:T(8,128)S(1)} %get-tuple-element.27, f32[128,16]{1,0:T(8,128)S(1)} %copy-done.28), kind=kLoop, calls=%fused_computation.3 | loop fusion | flops 12451840 | bytes 34152448 | tf_op jit(solution)/shard_map/reduce_sum | solution.py:89
  720.5 5.7 convolution_convert_fusion
  727.1 39.7 %reduce-scatter.3.cloned.1.call-done = bf16[16,4096]{1,0:T(8,128)(2,1)} async-done(((bf16[128,4096]{1,0:T(8,128)(2,1)}), bf16[16,4096]{1,0:T(8,128)(2,1)}) %reduce-scatter.3.cloned.1.call-update) | async-done | bytes 131088 | tf_op jit(solution)/shard_map/reduce_scatter | solution.py:96
  769.3 16.9 %all_to_all.10 = bf16[16,4,4096]{2,1,0:T(4,128)(2,1)S(1)} all-to-all(bf16[16,4,4096]{2,1,0:T(4,128)(2,1)S(1)} %reshape.78), channel_id=1, replica_groups=mesh['seq'=16,'expert'=8] {'seq'}, dimensions={0} | all-to-all | bytes 1048576 | tf_op jit(solution)/shard_map/all_to_all | solution.py:113
  787.2 29.3 %all-gather.11.cloned.1.call-done = bf16[8,64,4096]{2,1,0:T(8,128)(2,1)} async-done(((bf16[1,64,4096]{2,1,0:T(8,128)(2,1)}), bf16[8,64,4096]{2,1,0:T(8,128)(2,1)}) %all-gather.11.cloned.1.call-update) | async-done | bytes 4194320 | tf_op jit(solution)/shard_map/all_gather | solution.py:116
  816.5 10.1 %fusion.6 = f32[512,896]{1,0:T(8,128)} fusion(bf16[512,4096]{1,0:T(8,128)(2,1)} %bitcast.51, bf16[1,4096,896]{2,1,0:T(8,128)(2,1)} %param.33), kind=kOutput, calls=%fused_computation.9 | convolution fusion | flops 3758096384 | bytes 13369344 | tf_op jit(solution)/shard_map/dot_general | solution.py:119
  826.6 16.7 %fusion.8 = bf16[512,4096]{1,0:T(8,128)(2,1)} fusion(bf16[1,896,4096]{2,1,0:T(8,128)(2,1)} %param.35, f32[512,896]{1,0:T(8,128)} %fusion.6, bf16[512,4096]{1,0:T(8,128)(2,1)} %bitcast.52, bf16[1,4096,896]{2,1,0:T(8,128)(2,1)} %param.34), kind=kOutput, calls=%fused_computation.11 | convolution fusion | flops 7521042432 | bytes 24903680 | tf_op jit(solution)/shard_map/dot_general | solution.py:123
  843.3 38.0 %reduce-scatter.5.cloned.1.call-done = bf16[64,4096]{1,0:T(8,128)(2,1)} async-done(((bf16[512,4096]{1,0:T(8,128)(2,1)}), bf16[64,4096]{1,0:T(8,128)(2,1)}) %reduce-scatter.5.cloned.1.call-update) | async-done | bytes 524304 | tf_op jit(solution)/shard_map/reduce_scatter | solution.py:122
  883.3 7.1 all-to-all-start.1
  890.5 10.1 %all-to-all-done.1 = bf16[16,4,4096]{2,1,0:T(4,128)(2,1)S(1)} async-done(((bf16[16,4,4096]{2,1,0:T(4,128)(2,1)}), bf16[16,4,4096]{2,1,0:T(4,128)(2,1)S(1)}, u32[]{:S(2)}, u32[]{:S(2)}) %all-to-all-start.1) | async-done | bytes 524320 | tf_op jit(solution)/shard_map/all_to_all | solution.py:128
  (241 shorter events, 138.8 us)
Async XLA Ops:
  6.5 155.7 %copy-start = (bf16[1024,288]{0,1:T(8,128)(2,1)S(1)}, bf16[1024,288]{0,1:T(8,128)(2,1)}, u32[]{:S(2)}) copy-start(bf16[1024,288]{0,1:T(8,128)(2,1)} %param.24) | copy-start | bytes 1769476
  6.5 28.4 %all-gather.5.cloned.1.call-start = ((), (), s32[]{:S(2)}) async-start(), calls=%async_computation.4 | async-start | bytes 1179648 | tf_op jit(solution)/shard_map/all_gather | solution.py:49
  7.3 141.1 %all-gather.7.cloned.1.call-start = ((), (), s32[]{:S(2)}) async-start(), calls=%async_computation.5 | async-start | bytes 17825792 | tf_op jit(solution)/shard_map/all_gather | solution.py:55
  8.0 215.6 %all-reduce.30.cloned.1.call-start = ((), (), s32[]{:S(2)}) async-start(), calls=%async_computation.6 | async-start | bytes 131072 | tf_op jit(solution)/shard_map/psum | solution.py:68
  36.4 125.5 %copy-start.39 = (f32[1024]{0:T(1024)S(1)}, f32[1024]{0:T(1024)}, u32[]{:S(2)}) copy-start(f32[1024]{0:T(1024)} %param.23) | copy-start | bytes 12292
  36.4 187.1 %copy-start.42 = (bf16[256,1024]{1,0:T(8,128)(2,1)S(1)}, bf16[256,1024]{1,0:T(8,128)(2,1)}, u32[]{:S(2)}) copy-start(bf16[256,1024]{1,0:T(8,128)(2,1)} %param.25) | copy-start | bytes 1572868
  36.4 187.1 %copy-start.43 = (f32[1024]{0:T(1024)S(1)}, f32[1024]{0:T(1024)}, u32[]{:S(2)}) copy-start(f32[1024]{0:T(1024)} %param.26) | copy-start | bytes 12292
  156.9 68.0 %copy-start.37 = (f32[16,1024]{1,0:T(8,128)S(1)}, f32[16,1024]{1,0:T(8,128)}, u32[]{:S(2)}) copy-start(f32[16,1024]{1,0:T(8,128)} %param.27) | copy-start | bytes 196612
  156.9 5.0 collective-permute-start.1
  162.2 64.8 %copy-start.23 = (bf16[128,1024]{1,0:T(8,128)(2,1)}, bf16[128,1024]{1,0:T(8,128)(2,1)S(1)}, u32[]{:S(2)}) copy-start(bf16[128,1024]{1,0:T(8,128)(2,1)S(1)} %multiply_convert_fusion.1) | copy-start | bytes 786436
  163.2 557.3 %all-gather.9.cloned.1.call-start = ((), (), s32[]{:S(2)}) async-start(), calls=%async_computation.7 | async-start | bytes 8912896 | tf_op jit(solution)/shard_map/all_gather | solution.py:93
  163.8 602.9 %reduce-scatter.3.cloned.1.call-start = ((), (), s32[]{:S(2)}) async-start(), calls=%async_computation.8 | async-start | bytes 1179648 | tf_op jit(solution)/shard_map/reduce_scatter | solution.py:96
  280.3 8.2 copy-start.36
  288.5 8.3 copy-start.20
  308.4 27.3 %copy-start.33 = (f32[1,16,1024]{2,1,0:T(8,128)S(1)}, f32[1,16,1024]{2,1,0:T(8,128)}, u32[]{:S(2)}) copy-start(f32[1,16,1024]{2,1,0:T(8,128)} %slice.347) | copy-start | bytes 196612
  362.0 18.6 %copy-start.16 = (f32[32,16,1024]{2,1,0:T(8,128)S(1)}, f32[32,16,1024]{2,1,0:T(8,128)}, u32[]{:S(2)}) copy-start(f32[32,16,1024]{2,1,0:T(8,128)} %add.255) | copy-start | bytes 6291460
  399.4 35.6 %copy-start.17 = (f32[31,16,1024]{2,1,0:T(8,128)S(1)}, f32[31,16,1024]{2,1,0:T(8,128)}, u32[]{:S(2)}) copy-start(f32[31,16,1024]{2,1,0:T(8,128)} %get-tuple-element.56) | copy-start | bytes 6094852
  399.4 35.6 %copy-start.31 = (f32[1,16,1024]{2,1,0:T(8,128)S(1)}, f32[1,16,1024]{2,1,0:T(8,128)}, u32[]{:S(2)}) copy-start(f32[1,16,1024]{2,1,0:T(8,128)} %slice.369) | copy-start | bytes 196612
  436.5 18.6 %copy-start.15 = (f32[32,16,1024]{2,1,0:T(8,128)S(1)}, f32[32,16,1024]{2,1,0:T(8,128)}, u32[]{:S(2)}) copy-start(f32[32,16,1024]{2,1,0:T(8,128)} %add.264) | copy-start | bytes 6291460
  467.0 8.6 copy-start.6
  521.2 35.5 %copy-start.29 = (f32[1,16,1024]{2,1,0:T(8,128)S(1)}, f32[1,16,1024]{2,1,0:T(8,128)}, u32[]{:S(2)}) copy-start(f32[1,16,1024]{2,1,0:T(8,128)} %slice.368) | copy-start | bytes 196612
  561.5 144.9 %copy-start.28 = (f32[128,16]{1,0:T(8,128)S(1)}, f32[128,16]{1,0:T(8,128)}, u32[]{:S(2)}) copy-start(f32[128,16]{1,0:T(8,128)} %copy.42) | copy-start | bytes 24580
  598.8 5.0 collective-permute-start
  603.9 5.8 collective-permute-start
  609.7 5.9 collective-permute-start
  615.6 5.8 collective-permute-start
  621.5 5.8 collective-permute-start
  627.3 7.2 collective-permute-start
  634.5 8.1 collective-permute-start
  642.6 8.1 collective-permute-start
  650.7 7.9 collective-permute-start
  658.6 7.9 collective-permute-start
  666.6 8.0 collective-permute-start
  674.6 7.8 collective-permute-start
  682.5 7.9 collective-permute-start
  690.4 8.1 collective-permute-start
  698.5 7.9 collective-permute-start
  706.5 14.1 %copy-start.19 = (f32[128,2,1024]{2,0,1:T(8,128)S(1)}, f32[128,2,1024]{2,0,1:T(8,128)}, u32[]{:S(2)}) copy-start(f32[128,2,1024]{2,0,1:T(8,128)} %copy-done.18) | copy-start | bytes 3145732
  706.5 14.1 %copy-start.24 = (bf16[128,1024]{1,0:T(8,128)(2,1)S(1)}, bf16[128,1024]{1,0:T(8,128)(2,1)}, u32[]{:S(2)}) copy-start(bf16[128,1024]{1,0:T(8,128)(2,1)} %copy-done.23) | copy-start | bytes 786436
  706.5 14.1 %copy-start.44 = (f32[1024]{0:T(1024)S(1)}, f32[1024]{0:T(1024)}, u32[]{:S(2)}) copy-start(f32[1024]{0:T(1024)} %param.28) | copy-start | bytes 12292
  720.5 46.3 %copy-start.21 = (bf16[16,4096]{1,0:T(8,128)(2,1)S(1)}, bf16[16,4096]{1,0:T(8,128)(2,1)}, u32[]{:S(2)}) copy-start(bf16[16,4096]{1,0:T(8,128)(2,1)} %param.19) | copy-start | bytes 393220
  720.5 47.3 %copy-start.38 = (f32[4096]{0:T(1024)S(1)}, f32[4096]{0:T(1024)}, u32[]{:S(2)}) copy-start(f32[4096]{0:T(1024)} %param.30) | copy-start | bytes 49156
  726.3 90.2 %all-gather.11.cloned.1.call-start = ((), (), s32[]{:S(2)}) async-start(), calls=%async_computation.9 | async-start | bytes 4718592 | tf_op jit(solution)/shard_map/all_gather | solution.py:116
  787.1 94.2 %reduce-scatter.5.cloned.1.call-start = ((), (), s32[]{:S(2)}) async-start(), calls=%async_computation.10 | async-start | bytes 4718592 | tf_op jit(solution)/shard_map/reduce_scatter | solution.py:122
  826.6 75.1 %copy-start.1 = (bf16[1024,288]{0,1:T(8,128)(2,1)S(1)}, bf16[1024,288]{0,1:T(8,128)(2,1)}, u32[]{:S(2)}) copy-start(bf16[1024,288]{0,1:T(8,128)(2,1)} %param.24) | copy-start | bytes 1769476
  843.2 47.2 %copy-start.41 = (f32[16,2]{0,1:T(2,128)S(1)}, f32[16,2]{0,1:T(2,128)}, u32[]{:S(2)}) copy-start(f32[16,2]{0,1:T(2,128)} %param.32) | copy-start | bytes 388
  843.2 57.4 %copy-start.22 = (bf16[16,4096]{1,0:T(8,128)(2,1)S(1)}, bf16[16,4096]{1,0:T(8,128)(2,1)}, u32[]{:S(2)}) copy-start(bf16[16,4096]{1,0:T(8,128)(2,1)} %reduce-scatter.3.cloned.1.call-done) | copy-start | bytes 393220
  883.3 17.2 %all-to-all-start.1 = ((bf16[16,4,4096]{2,1,0:T(4,128)(2,1)}), bf16[16,4,4096]{2,1,0:T(4,128)(2,1)S(1)}, u32[]{:S(2)}, u32[]{:S(2)}) async-start(bf16[16,4,4096]{2,1,0:T(4,128)(2,1)} %reshape.81), calls=%async_computation.3 | async-start | bytes 1048576 | tf_op jit(solution)/shard_map/all_to_all | solution.py:128
  (21 other events, 86.6 us)
Sparse Core Ops, SparseCore 0:
  9.1 25.7 all-gather.4
  37.0 111.3 all-gather.6
  163.4 60.1 all-reduce.29
  225.7 77.5 all-gather.8
  726.4 40.3 reduce-scatter.2
  787.2 29.2 all-gather.10
  843.4 37.8 reduce-scatter.4
where the time goes:
time: 924 us; the launch traced here: 909 us
  waiting for transfers between devices  327 us (35%)
  local copies, waits for them, and re-layouts  289 us (31%)
  other arithmetic  109 us (12%)
  starting transfers between devices  94.2 us (10%)
  matrix products  44.8 us (5%)
  blocking collectives  30.9 us (3%)
  between operations  14 us (2%)
    pad x24, local copies, waits for them, and re-layouts, per_device(): lax.associative_scan(combine_states, (decay, source), axis=0)  267 us
    all_gather x1, waiting for transfers between devices, per_device(): lax.all_gather(in_weight, 'seq', axis=1, tiled=True)  112 us
    ppermute x16, starting transfers between devices, from_behind(): return lax.ppermute(block, axis, route)  86.9 us
    psum x1, waiting for transfers between devices, per_device(): lax.psum(partial_value[:, :RANK].astype(jnp.bfloat16), 'expert')  44.8 us
    reduce_scatter x1, waiting for transfers between devices, per_device(): lax.psum_scatter(terms.astype(jnp.bfloat16), 'expert', scatter_dimension=...  39.7 us
    reduce_scatter x1, waiting for transfers between devices, per_device(): lax.psum_scatter(jnp.dot(act, w_down[0], preferred_element_type=jnp.float...  38 us
    add x12, other arithmetic, combine_states(): return (earlier[0] * later[0], later[0] * earlier[1] + later[1])  34.6 us
    add x12, other arithmetic, per_device(): lax.associative_scan(combine_states, (decay, source), axis=0)  33.2 us
  transfers between devices with their start and end apart: 24, of which 23 were waited for; matrix products, arithmetic and copies ran while one was open for 42% of the time, Pallas kernels for 0%

commit v1 on v0

--- a/solution.py
+++ b/solution.py
@@ -101,9 +101,9 @@
     capacity = max(2, 4 * rows // n_seq)
     slots_all = n_seq * capacity
     flat_ids = expert_ids.reshape(-1)
-    onehot = (flat_ids[:, None] == jnp.arange(n_seq, dtype=jnp.int32)[None, :]).astype(jnp.int32)
-    before = jnp.cumsum(onehot, axis=0) - onehot
-    slot = jnp.sum(before * onehot, axis=1)
+    order = jnp.arange(flat_ids.shape[0], dtype=jnp.int32)
+    same = (flat_ids[:, None] == flat_ids[None, :]) & (order[None, :] < order[:, None])
+    slot = jnp.sum(same.astype(jnp.int32), axis=1)
     target = flat_ids * capacity + slot
     places = target[:, None] == jnp.arange(slots_all, dtype=jnp.int32)[None, :]
     dispatch_mat = jnp.any(places.reshape(rows, TOP, slots_all), axis=1).astype(jnp.bfloat16)

time: 924 us -> 926 us (level)
  transfers between devices with their start and end apart: 24 -> 24, of which waited for: 23 -> 23; matrix products, arithmetic and copies ran while one was open for 42% -> 43% of each run, Pallas kernels for 0% -> 0%
where the time goes in v1:
time: 926 us; the launch traced here: 910 us
  waiting for transfers between devices  327 us (35%)
  local copies, waits for them, and re-layouts  290 us (31%)
  other arithmetic  109 us (12%)
  starting transfers between devices  94.1 us (10%)
  matrix products  44.8 us (5%)
  blocking collectives  30.8 us (3%)
  between operations  14 us (2%)
    pad x24, local copies, waits for them, and re-layouts, per_device(): lax.associative_scan(combine_states, (decay, source), axis=0)  268 us
    all_gather x1, waiting for transfers between devices, per_device(): lax.all_gather(in_weight, 'seq', axis=1, tiled=True)  112 us
    ppermute x16, starting transfers between devices, from_behind(): return lax.ppermute(block, axis, route)  86.9 us
    psum x1, waiting for transfers between devices, per_device(): lax.psum(partial_value[:, :RANK].astype(jnp.bfloat16), 'expert')  44.8 us
    reduce_scatter x1, waiting for transfers between devices, per_device(): lax.psum_scatter(terms.astype(jnp.bfloat16), 'expert', scatter_dimension=...  39.9 us
    reduce_scatter x1, waiting for transfers between devices, per_device(): lax.psum_scatter(jnp.dot(act, w_down[0], preferred_element_type=jnp.float...  38 us
    add x12, other arithmetic, combine_states(): return (earlier[0] * later[0], later[0] * earlier[1] + later[1])  34.6 us
    add x12, other arithmetic, per_device(): lax.associative_scan(combine_states, (decay, source), axis=0)  33.2 us
  transfers between devices with their start and end apart: 24, of which 23 were waited for; matrix products, arithmetic and copies ran while one was open for 43% of the time, Pallas kernels for 0%

profile of v1, /device:TPU:0, one launch (start us, length us, event | category | flops | bytes accessed | tf_op | source)
XLA Modules:
  0.0 910.1 jit_solution(3287583702979538523)
XLA Ops:
  8.9 26.0 %all-gather.5.cloned.1.call-done = bf16[128,4096]{1,0:T(8,128)(2,1)} async-done(((bf16[16,4096]{1,0:T(8,128)(2,1)}), bf16[128,4096]{1,0:T(8,128)(2,1)}) %all-gather.5.cloned.1.call-update) | async-done | bytes 1048592 | tf_op jit(solution)/shard_map/all_gather | solution.py:49
  36.5 111.9 %all-gather.7.cloned.1.call-done = bf16[2,4096,1024]{2,1,0:T(8,128)(2,1)} async-done(((bf16[2,256,1024]{2,1,0:T(8,128)(2,1)}), bf16[2,4096,1024]{2,1,0:T(8,128)(2,1)}) %all-gather.7.cloned.1.call-update) | async-done | bytes 16777232 | tf_op jit(solution)/shard_map/all_gather | solution.py:55
  148.4 8.5 fusion.20
  163.9 14.0 %psum.14 = bf16[128,32]{0,1:T(8,128)(2,1)S(1)} all-reduce(bf16[128,32]{0,1:T(8,128)(2,1)S(1)} %slice.341), channel_id=1, replica_groups=mesh['seq'=16,'expert'=8] {'expert'}, use_global_device_ids=true, to_apply=%region_1.2 | all-reduce | flops 4096 | bytes 16384 | tf_op jit(solution)/shard_map/psum | solution.py:69
  178.7 44.8 %all-reduce.30.cloned.1.call-done = bf16[128,256]{0,1:T(8,128)(2,1)} async-done(((bf16[128,256]{0,1:T(8,128)(2,1)}), bf16[128,256]{0,1:T(8,128)(2,1)}) %all-reduce.30.cloned.1.call-update) | async-done | bytes 65552 | tf_op jit(solution)/shard_map/psum | solution.py:68
  233.5 10.9 %slice_add_fusion = (f32[64,16,1024]{2,1,0:T(8,128)S(1)}, f32[64,16,1024]{2,1,0:T(8,128)}) fusion(f32[128,16,1024]{2,1,0:T(8,128)} %copy-done.3, f32[128,16,1024]{2,1,0:T(8,128)} %copy-done.2), kind=kLoop, calls=%fused_computation.19 | loop fusion | flops 3145728 | bytes 25165824 | tf_op jit(solution)/shard_map/add | solution.py:24
  308.6 7.0 pad.108
  315.6 10.2 %pad.109 = f32[32,16,1024]{2,1,0:T(8,128)} pad(f32[16,16,1024]{2,1,0:T(8,128)} %add.263, f32[]{:T(128)} %constant.11.clone.1), padding=1_0_1x0_0_0x0_0_0 | pad | bytes 3145732 | tf_op jit(solution)/shard_map/pad | solution.py:78
  325.8 10.1 %pad.95 = f32[32,16,1024]{2,1,0:T(8,128)} pad(f32[16,16,1024]{2,1,0:T(8,128)} %add.253, f32[]{:T(128)} %constant.11.clone.1), padding=1_0_1x0_0_0x0_0_0 | pad | bytes 3145732 | tf_op jit(solution)/shard_map/pad | solution.py:78
  338.2 10.2 %pad.94 = f32[32,16,1024]{2,1,0:T(8,128)} pad(f32[16,16,1024]{2,1,0:T(8,128)} %pad_maximum_fusion.4, f32[]{:T(128)} %constant.11.clone.1), padding=0_1_1x0_0_0x0_0_0 | pad | bytes 3145732 | tf_op jit(solution)/shard_map/pad | solution.py:78
  348.4 4.3 add.255
  355.7 5.0 fusion.16
  362.3 18.7 %pad.96 = f32[64,16,1024]{2,1,0:T(8,128)} pad(f32[32,16,1024]{2,1,0:T(8,128)} %pad_maximum_fusion.2, f32[]{:T(128)} %constant.11.clone.1), padding=0_1_1x0_0_0x0_0_0 | pad | bytes 6291460 | tf_op jit(solution)/shard_map/pad | solution.py:78
  381.0 12.1 %pad.97 = f32[64,16,1024]{2,1,0:T(8,128)} pad(f32[32,16,1024]{2,1,0:T(8,128)S(1)} %copy-done.16, f32[]{:T(128)} %constant.11.clone.1), padding=1_0_1x0_0_0x0_0_0 | pad | bytes 6291460 | tf_op jit(solution)/shard_map/pad | solution.py:78
  393.1 6.9 add.257
  400.0 35.8 %pad.99 = f32[128,16,1024]{2,1,0:T(8,128)} pad(f32[64,16,1024]{2,1,0:T(8,128)} %add.257, f32[]{:T(128)} %constant.11.clone.1), padding=1_0_1x0_0_0x0_0_0 | pad | bytes 12582916 | tf_op jit(solution)/shard_map/pad | solution.py:78
  437.2 18.7 %pad.110 = f32[64,16,1024]{2,1,0:T(8,128)} pad(f32[32,16,1024]{2,1,0:T(8,128)} %pad_maximum_fusion.3, f32[]{:T(128)} %constant.11.clone.1), padding=0_1_1x0_0_0x0_0_0 | pad | bytes 6291460 | tf_op jit(solution)/shard_map/pad | solution.py:78
  455.9 12.1 %pad.111 = f32[64,16,1024]{2,1,0:T(8,128)} pad(f32[32,16,1024]{2,1,0:T(8,128)S(1)} %copy-done.15, f32[]{:T(128)} %constant.11.clone.1), padding=1_0_1x0_0_0x0_0_0 | pad | bytes 6291460 | tf_op jit(solution)/shard_map/pad | solution.py:78
  468.0 7.1 add.265
  476.6 7.6 fusion.12
  486.7 35.8 %pad.98 = f32[128,16,1024]{2,1,0:T(8,128)} pad(f32[64,16,1024]{2,1,0:T(8,128)} %pad_maximum_fusion, f32[]{:T(128)} %constant.11.clone.1), padding=0_1_1x0_0_0x0_0_0 | pad | bytes 12582916 | tf_op jit(solution)/shard_map/pad | solution.py:78
  522.5 35.7 %pad.113 = f32[128,16,1024]{2,1,0:T(8,128)} pad(f32[64,16,1024]{2,1,0:T(8,128)} %add.265, f32[]{:T(128)} %constant.11.clone.1), padding=1_0_1x0_0_0x0_0_0 | pad | bytes 12582916 | tf_op jit(solution)/shard_map/pad | solution.py:78
  558.2 4.8 pad_maximum_fusion.1
  563.0 35.6 %pad.112 = f32[128,16,1024]{2,1,0:T(8,128)} pad(f32[64,16,1024]{2,1,0:T(8,128)} %pad_maximum_fusion.1, f32[]{:T(128)} %constant.11.clone.1), padding=0_1_1x0_0_0x0_0_0 | pad | bytes 12582916 | tf_op jit(solution)/shard_map/pad | solution.py:78
  600.4 107.7 %while.11 = (s32[]{:T(128)}, f32[16,1024]{1,0:T(8,128)S(1)}, f32[16,1024]{1,0:T(8,128)S(1)}, f32[16,1024]{1,0:T(8,128)S(1)}, s32[]{:T(128)}, /*index=5*/s32[]{:T(128)}) while((s32[]{:T(128)}, f32[16,1024]{1,0:T(8,128)S(1)}, f32[16,1024]{1,0:T(8,128)S(1)}, f32[16,1024]{1,0:T(8,128)S(1)}, s32[]{:T(128)}, /*index=5*/s32[]{:T(128)}) %tuple.47), condition=%wide.region_4.5_spmd.clone, body=%wide.region_3.4_spmd.clone.sunk | while | flops 81923 | bytes 458871 | solution.py:87
  605.5 4.2 collective-permute-start
  611.3 4.3 collective-permute-start
  617.3 4.2 collective-permute-start
  628.9 5.6 collective-permute-start
  636.1 6.5 collective-permute-start
  644.2 6.5 collective-permute-start
  652.3 6.3 collective-permute-start
  660.3 6.3 collective-permute-start
  668.2 6.3 collective-permute-start
  676.3 6.2 collective-permute-start
  684.1 6.3 collective-permute-start
  692.1 6.5 collective-permute-start
  700.2 6.3 collective-permute-start
  708.1 14.0 %multiply_reduce_fusion = f32[128,1024]{1,0:T(8,128)S(1)} fusion(f32[128,16,1024]{2,1,0:T(8,128)} %pad.112, f32[128,16,1024]{2,1,0:T(8,128)} %pad.113, f32[128,16,1024]{2,1,0:T(8,128)} %pad.98, f32[128,16,1024]{2,1,0:T(8,128)} %pad.99, f32[16,1024]{1,0:T(8,128)S(1)} %get-tuple-element.27, f32[128,16]{1,0:T(8,128)S(1)} %copy-done.28), kind=kLoop, calls=%fused_computation.3 | loop fusion | flops 12451840 | bytes 34152448 | tf_op jit(solution)/shard_map/reduce_sum | solution.py:89
  722.2 5.7 convolution_convert_fusion
  728.6 39.9 %reduce-scatter.3.cloned.1.call-done = bf16[16,4096]{1,0:T(8,128)(2,1)} async-done(((bf16[128,4096]{1,0:T(8,128)(2,1)}), bf16[16,4096]{1,0:T(8,128)(2,1)}) %reduce-scatter.3.cloned.1.call-update) | async-done | bytes 131088 | tf_op jit(solution)/shard_map/reduce_scatter | solution.py:96
  771.0 16.8 %all_to_all.10 = bf16[16,4,4096]{2,1,0:T(4,128)(2,1)S(1)} all-to-all(bf16[16,4,4096]{2,1,0:T(4,128)(2,1)S(1)} %reshape.79), channel_id=1, replica_groups=mesh['seq'=16,'expert'=8] {'seq'}, dimensions={0} | all-to-all | bytes 1048576 | tf_op jit(solution)/shard_map/all_to_all | solution.py:113
  788.8 29.3 %all-gather.11.cloned.1.call-done = bf16[8,64,4096]{2,1,0:T(8,128)(2,1)} async-done(((bf16[1,64,4096]{2,1,0:T(8,128)(2,1)}), bf16[8,64,4096]{2,1,0:T(8,128)(2,1)}) %all-gather.11.cloned.1.call-update) | async-done | bytes 4194320 | tf_op jit(solution)/shard_map/all_gather | solution.py:116
  818.1 10.1 %fusion.6 = f32[512,896]{1,0:T(8,128)} fusion(bf16[512,4096]{1,0:T(8,128)(2,1)} %bitcast.51, bf16[1,4096,896]{2,1,0:T(8,128)(2,1)} %param.33), kind=kOutput, calls=%fused_computation.9 | convolution fusion | flops 3758096384 | bytes 13369344 | tf_op jit(solution)/shard_map/dot_general | solution.py:119
  828.2 16.6 %fusion.8 = bf16[512,4096]{1,0:T(8,128)(2,1)} fusion(bf16[1,896,4096]{2,1,0:T(8,128)(2,1)} %param.35, f32[512,896]{1,0:T(8,128)} %fusion.6, bf16[512,4096]{1,0:T(8,128)(2,1)} %bitcast.52, bf16[1,4096,896]{2,1,0:T(8,128)(2,1)} %param.34), kind=kOutput, calls=%fused_computation.11 | convolution fusion | flops 7521042432 | bytes 24903680 | tf_op jit(solution)/shard_map/dot_general | solution.py:123
  844.9 38.0 %reduce-scatter.5.cloned.1.call-done = bf16[64,4096]{1,0:T(8,128)(2,1)} async-done(((bf16[512,4096]{1,0:T(8,128)(2,1)}), bf16[64,4096]{1,0:T(8,128)(2,1)}) %reduce-scatter.5.cloned.1.call-update) | async-done | bytes 524304 | tf_op jit(solution)/shard_map/reduce_scatter | solution.py:122
  885.0 7.0 all-to-all-start.1
  892.1 10.1 %all-to-all-done.1 = bf16[16,4,4096]{2,1,0:T(4,128)(2,1)S(1)} async-done(((bf16[16,4,4096]{2,1,0:T(4,128)(2,1)}), bf16[16,4,4096]{2,1,0:T(4,128)(2,1)S(1)}, u32[]{:S(2)}, u32[]{:S(2)}) %all-to-all-start.1) | async-done | bytes 524320 | tf_op jit(solution)/shard_map/all_to_all | solution.py:128
  (239 shorter events, 139.0 us)
Async XLA Ops:
  6.5 155.7 %copy-start = (bf16[1024,288]{0,1:T(8,128)(2,1)S(1)}, bf16[1024,288]{0,1:T(8,128)(2,1)}, u32[]{:S(2)}) copy-start(bf16[1024,288]{0,1:T(8,128)(2,1)} %param.24) | copy-start | bytes 1769476
  6.5 28.4 %all-gather.5.cloned.1.call-start = ((), (), s32[]{:S(2)}) async-start(), calls=%async_computation.4 | async-start | bytes 1179648 | tf_op jit(solution)/shard_map/all_gather | solution.py:49
  7.3 141.1 %all-gather.7.cloned.1.call-start = ((), (), s32[]{:S(2)}) async-start(), calls=%async_computation.5 | async-start | bytes 17825792 | tf_op jit(solution)/shard_map/all_gather | solution.py:55
  8.0 215.6 %all-reduce.30.cloned.1.call-start = ((), (), s32[]{:S(2)}) async-start(), calls=%async_computation.6 | async-start | bytes 131072 | tf_op jit(solution)/shard_map/psum | solution.py:68
  36.4 125.5 %copy-start.39 = (f32[1024]{0:T(1024)S(1)}, f32[1024]{0:T(1024)}, u32[]{:S(2)}) copy-start(f32[1024]{0:T(1024)} %param.23) | copy-start | bytes 12292
  36.4 187.1 %copy-start.42 = (bf16[256,1024]{1,0:T(8,128)(2,1)S(1)}, bf16[256,1024]{1,0:T(8,128)(2,1)}, u32[]{:S(2)}) copy-start(bf16[256,1024]{1,0:T(8,128)(2,1)} %param.25) | copy-start | bytes 1572868
  36.4 187.1 %copy-start.43 = (f32[1024]{0:T(1024)S(1)}, f32[1024]{0:T(1024)}, u32[]{:S(2)}) copy-start(f32[1024]{0:T(1024)} %param.26) | copy-start | bytes 12292
  156.9 68.0 %copy-start.37 = (f32[16,1024]{1,0:T(8,128)S(1)}, f32[16,1024]{1,0:T(8,128)}, u32[]{:S(2)}) copy-start(f32[16,1024]{1,0:T(8,128)} %param.27) | copy-start | bytes 196612
  156.9 5.0 collective-permute-start.1
  162.2 64.8 %copy-start.23 = (bf16[128,1024]{1,0:T(8,128)(2,1)}, bf16[128,1024]{1,0:T(8,128)(2,1)S(1)}, u32[]{:S(2)}) copy-start(bf16[128,1024]{1,0:T(8,128)(2,1)S(1)} %multiply_convert_fusion.1) | copy-start | bytes 786436
  163.2 558.9 %all-gather.9.cloned.1.call-start = ((), (), s32[]{:S(2)}) async-start(), calls=%async_computation.7 | async-start | bytes 8912896 | tf_op jit(solution)/shard_map/all_gather | solution.py:93
  163.8 604.6 %reduce-scatter.3.cloned.1.call-start = ((), (), s32[]{:S(2)}) async-start(), calls=%async_computation.8 | async-start | bytes 1179648 | tf_op jit(solution)/shard_map/reduce_scatter | solution.py:96
  280.4 8.3 copy-start.36
  288.7 8.3 copy-start.20
  308.6 27.3 %copy-start.33 = (f32[1,16,1024]{2,1,0:T(8,128)S(1)}, f32[1,16,1024]{2,1,0:T(8,128)}, u32[]{:S(2)}) copy-start(f32[1,16,1024]{2,1,0:T(8,128)} %slice.347) | copy-start | bytes 196612
  362.3 18.7 %copy-start.16 = (f32[32,16,1024]{2,1,0:T(8,128)S(1)}, f32[32,16,1024]{2,1,0:T(8,128)}, u32[]{:S(2)}) copy-start(f32[32,16,1024]{2,1,0:T(8,128)} %add.255) | copy-start | bytes 6291460
  400.0 35.8 %copy-start.17 = (f32[31,16,1024]{2,1,0:T(8,128)S(1)}, f32[31,16,1024]{2,1,0:T(8,128)}, u32[]{:S(2)}) copy-start(f32[31,16,1024]{2,1,0:T(8,128)} %get-tuple-element.56) | copy-start | bytes 6094852
  400.0 35.8 %copy-start.31 = (f32[1,16,1024]{2,1,0:T(8,128)S(1)}, f32[1,16,1024]{2,1,0:T(8,128)}, u32[]{:S(2)}) copy-start(f32[1,16,1024]{2,1,0:T(8,128)} %slice.369) | copy-start | bytes 196612
  437.2 18.7 %copy-start.15 = (f32[32,16,1024]{2,1,0:T(8,128)S(1)}, f32[32,16,1024]{2,1,0:T(8,128)}, u32[]{:S(2)}) copy-start(f32[32,16,1024]{2,1,0:T(8,128)} %add.264) | copy-start | bytes 6291460
  468.0 8.6 copy-start.6
  522.5 35.8 %copy-start.29 = (f32[1,16,1024]{2,1,0:T(8,128)S(1)}, f32[1,16,1024]{2,1,0:T(8,128)}, u32[]{:S(2)}) copy-start(f32[1,16,1024]{2,1,0:T(8,128)} %slice.368) | copy-start | bytes 196612
  563.0 145.1 %copy-start.28 = (f32[128,16]{1,0:T(8,128)S(1)}, f32[128,16]{1,0:T(8,128)}, u32[]{:S(2)}) copy-start(f32[128,16]{1,0:T(8,128)} %copy.42) | copy-start | bytes 24580
  600.5 5.0 collective-permute-start
  605.5 5.8 collective-permute-start
  611.3 5.9 collective-permute-start
  617.3 5.8 collective-permute-start
  623.1 5.8 collective-permute-start
  628.9 7.2 collective-permute-start
  636.1 8.1 collective-permute-start
  644.2 8.1 collective-permute-start
  652.3 7.9 collective-permute-start
  660.3 7.9 collective-permute-start
  668.2 8.0 collective-permute-start
  676.3 7.8 collective-permute-start
  684.1 7.9 collective-permute-start
  692.1 8.1 collective-permute-start
  700.2 7.9 collective-permute-start
  708.1 14.1 %copy-start.19 = (f32[128,2,1024]{2,0,1:T(8,128)S(1)}, f32[128,2,1024]{2,0,1:T(8,128)}, u32[]{:S(2)}) copy-start(f32[128,2,1024]{2,0,1:T(8,128)} %copy-done.18) | copy-start | bytes 3145732
  708.1 14.1 %copy-start.24 = (bf16[128,1024]{1,0:T(8,128)(2,1)S(1)}, bf16[128,1024]{1,0:T(8,128)(2,1)}, u32[]{:S(2)}) copy-start(bf16[128,1024]{1,0:T(8,128)(2,1)} %copy-done.23) | copy-start | bytes 786436
  708.1 14.1 %copy-start.44 = (f32[1024]{0:T(1024)S(1)}, f32[1024]{0:T(1024)}, u32[]{:S(2)}) copy-start(f32[1024]{0:T(1024)} %param.28) | copy-start | bytes 12292
  722.1 46.4 %copy-start.21 = (bf16[16,4096]{1,0:T(8,128)(2,1)S(1)}, bf16[16,4096]{1,0:T(8,128)(2,1)}, u32[]{:S(2)}) copy-start(bf16[16,4096]{1,0:T(8,128)(2,1)} %param.19) | copy-start | bytes 393220
  722.1 47.4 %copy-start.38 = (f32[4096]{0:T(1024)S(1)}, f32[4096]{0:T(1024)}, u32[]{:S(2)}) copy-start(f32[4096]{0:T(1024)} %param.30) | copy-start | bytes 49156
  727.9 90.2 %all-gather.11.cloned.1.call-start = ((), (), s32[]{:S(2)}) async-start(), calls=%async_computation.9 | async-start | bytes 4718592 | tf_op jit(solution)/shard_map/all_gather | solution.py:116
  788.8 94.2 %reduce-scatter.5.cloned.1.call-start = ((), (), s32[]{:S(2)}) async-start(), calls=%async_computation.10 | async-start | bytes 4718592 | tf_op jit(solution)/shard_map/reduce_scatter | solution.py:122
  828.2 75.1 %copy-start.1 = (bf16[1024,288]{0,1:T(8,128)(2,1)S(1)}, bf16[1024,288]{0,1:T(8,128)(2,1)}, u32[]{:S(2)}) copy-start(bf16[1024,288]{0,1:T(8,128)(2,1)} %param.24) | copy-start | bytes 1769476
  844.9 47.2 %copy-start.41 = (f32[16,2]{0,1:T(2,128)S(1)}, f32[16,2]{0,1:T(2,128)}, u32[]{:S(2)}) copy-start(f32[16,2]{0,1:T(2,128)} %param.32) | copy-start | bytes 388
  844.9 57.4 %copy-start.22 = (bf16[16,4096]{1,0:T(8,128)(2,1)S(1)}, bf16[16,4096]{1,0:T(8,128)(2,1)}, u32[]{:S(2)}) copy-start(bf16[16,4096]{1,0:T(8,128)(2,1)} %reduce-scatter.3.cloned.1.call-done) | copy-start | bytes 393220
  885.0 17.2 %all-to-all-start.1 = ((bf16[16,4,4096]{2,1,0:T(4,128)(2,1)}), bf16[16,4,4096]{2,1,0:T(4,128)(2,1)S(1)}, u32[]{:S(2)}, u32[]{:S(2)}) async-start(bf16[16,4,4096]{2,1,0:T(4,128)(2,1)} %reshape.82), calls=%async_computation.3 | async-start | bytes 1048576 | tf_op jit(solution)/shard_map/all_to_all | solution.py:128
  (21 other events, 86.8 us)
Sparse Core Ops, SparseCore 0:
  9.1 25.7 all-gather.4
  37.0 111.3 all-gather.6
  163.4 60.1 all-reduce.29
  225.7 77.5 all-gather.8
  728.0 40.3 reduce-scatter.2
  788.9 29.2 all-gather.10
  845.0 37.8 reduce-scatter.4

commit v2 on v1

--- a/solution.py
+++ b/solution.py
@@ -1,7 +1,14 @@
+import functools
+
 import jax
 import jax.numpy as jnp
 from jax import lax
+from jax.experimental import pallas as pl
+from jax.experimental.pallas import tpu as pltpu
 from jax.sharding import PartitionSpec as P
+
+MESH = pl.DeviceIdType.MESH
+VMEM_LIMIT = 56 * 2**20
 
 STATE = 16
 CONV = 4
@@ -20,8 +27,113 @@
     return wide * lax.rsqrt(jnp.mean(wide * wide, axis=-1, keepdims=True) + 1e-05) * gain
 
 
-def combine_states(earlier, later):
-    return (earlier[0] * later[0], later[0] * earlier[1] + later[1])
+def gather_kernel(axis, n, x_ref, o_ref, send_sems, recv_sems, local_sem):
+    me = lax.axis_index(axis)
+    barrier = pltpu.get_barrier_semaphore()
+    for d in range(1, n):
+        pl.semaphore_signal(
+            barrier, inc=1, device_id={axis: lax.rem(me + d, n)}, device_id_type=MESH
+        )
+    pl.semaphore_wait(barrier, n - 1)
+    own = pltpu.make_async_copy(x_ref, o_ref.at[me], local_sem)
+    own.start()
+    sent = []
+    for d in range(1, n):
+        copy = pltpu.make_async_remote_copy(
+            src_ref=x_ref,
+            dst_ref=o_ref.at[me],
+            send_sem=send_sems.at[d],
+            recv_sem=recv_sems.at[d],
+            device_id={axis: lax.rem(me + d, n)},
+            device_id_type=MESH,
+        )
+        copy.start()
+        sent.append(copy)
+    own.wait()
+    for d in range(1, n):
+        pltpu.make_async_remote_copy(
+            src_ref=x_ref,
+            dst_ref=o_ref.at[lax.rem(me + n - d, n)],
+            send_sem=send_sems.at[d],
+            recv_sem=recv_sems.at[d],
+            device_id={axis: lax.rem(me + d, n)},
+            device_id_type=MESH,
+        ).wait_recv()
+    for copy in sent:
+        copy.wait_send()
+
+
+def direct_gather(x, axis, collective_id):
+    n = lax.axis_size(axis)
+    return pl.pallas_call(
+        functools.partial(gather_kernel, axis, n),
+        out_shape=jax.ShapeDtypeStruct((n, *x.shape), x.dtype),
+        in_specs=[pl.BlockSpec(memory_space=pltpu.VMEM)],
+        out_specs=pl.BlockSpec(memory_space=pltpu.VMEM),
+        scratch_shapes=[
+            pltpu.SemaphoreType.DMA((n,)),
+            pltpu.SemaphoreType.DMA((n,)),
+            pltpu.SemaphoreType.DMA,
+        ],
+        compiler_params=pltpu.CompilerParams(
+            collective_id=collective_id, has_side_effects=True, vmem_limit_bytes=VMEM_LIMIT
+        ),
+    )(x)
+
+
+def lanes_of(value, width):
+    return jnp.concatenate([value] * (width // 128), axis=1)
+
+
+def first_pass(low_ref, weight_ref, bias_ref, inner_ref, a_ref, b_ref, step_ref, out_ref, u_ref):
+    tokens, width = inner_ref.shape
+    for at in range(0, width, 256):
+        cols = pl.ds(at, 256)
+        raw = jnp.dot(low_ref[...], weight_ref[:, cols], preferred_element_type=jnp.float32)
+        raw = raw + bias_ref[:, cols]
+        step = jnp.maximum(raw, 0.0) + jnp.log1p(jnp.exp(-jnp.abs(raw)))
+        step_ref[:, cols] = step
+        u_ref[:, cols] = step * inner_ref[:, cols].astype(jnp.float32)
+    rate = a_ref[...]
+
+    def group(g, state):
+        base = pl.multiple_of(g * 8, 8)
+        step8 = step_ref[pl.ds(base, 8), :]
+        u8 = u_ref[pl.ds(base, 8), :]
+        for r in range(8):
+            decay = jnp.exp(-(step8[r : r + 1, :] * rate))
+            state = decay * state + lanes_of(b_ref[base + r], width) * u8[r : r + 1, :]
+        return state
+
+    final = lax.fori_loop(0, tokens // 8, group, jnp.zeros_like(rate))
+    out_ref[:STATE, :] = final
+    out_ref[STATE : STATE + 8, :] = jnp.broadcast_to(
+        jnp.sum(step_ref[...], axis=0, keepdims=True), (8, width)
+    )
+
+
+def second_pass(step_ref, inner_ref, a_ref, b_ref, c_ref, start_ref, skip_ref, z_ref, out_ref, u_ref):
+    tokens, width = inner_ref.shape
+    u_ref[...] = step_ref[...] * inner_ref[...].astype(jnp.float32)
+    rate = a_ref[...]
+
+    def group(g, state):
+        base = pl.multiple_of(g * 8, 8)
+        step8 = step_ref[pl.ds(base, 8), :]
+        u8 = u_ref[pl.ds(base, 8), :]
+        rows = []
+        for r in range(8):
+            decay = jnp.exp(-(step8[r : r + 1, :] * rate))
+            state = decay * state + lanes_of(b_ref[base + r], width) * u8[r : r + 1, :]
+            rows.append(jnp.sum(lanes_of(c_ref[base + r], width) * state, axis=0, keepdims=True))
+        u_ref[pl.ds(base, 8), :] = jnp.concatenate(rows, axis=0)
+        return state
+
+    lax.fori_loop(0, tokens // 8, group, start_ref[...])
+    z = z_ref[...]
+    out_ref[...] = (
+        (u_ref[...] + skip_ref[...] * inner_ref[...].astype(jnp.float32)) * (z / (1.0 + jnp.exp(-z)))
+    ).astype(out_ref.dtype)
 
 
 def per_device(
@@ -64,30 +176,34 @@
         conv = conv + conv_weight[tap] * padded[tap : tap + local_tok]
     inner = jax.nn.silu(conv).astype(jnp.bfloat16)
     partial_value = jnp.dot(inner, xproj_weight, preferred_element_type=jnp.float32)
-    low_part, edge_part = (
-        lax.psum(partial_value[:, :RANK].astype(jnp.bfloat16), "expert").astype(jnp.float32),
-        lax.psum(partial_value[:, RANK:].astype(jnp.bfloat16), "expert").astype(jnp.float32),
-    )
-    dt_low = low_part.astype(jnp.bfloat16)
-    bmat = edge_part[:, :STATE]
-    cmat = edge_part[:, STATE:]
-    step = jax.nn.softplus(jnp.dot(dt_low, dt_weight, preferred_element_type=jnp.float32) + dt_bias)
-    inner_f = inner.astype(jnp.float32)
-    decay = jnp.exp(-step[:, None, :] * a_rate[None, :, :])
-    source = bmat[:, :, None] * (step * inner_f)[:, None, :]
-    cumulative, states = lax.associative_scan(combine_states, (decay, source), axis=0)
-    total = cumulative[-1]
-    final = states[-1]
-
-    def relay(turn, incoming):
-        return from_behind((total * incoming + final).astype(jnp.bfloat16), "seq", 1).astype(
-            jnp.float32
-        )
-
-    arriving = lax.fori_loop(0, n_seq - 1, relay, jnp.zeros_like(final))
-    states = states + cumulative * arriving[None, :, :]
-    readout = jnp.sum(cmat[:, :, None] * states, axis=1)
-    gated = ((readout + skip_d * inner_f) * jax.nn.silu(zpart)).astype(jnp.bfloat16)
+    proj = jnp.sum(
+        direct_gather(partial_value.astype(jnp.bfloat16), "expert", 1).astype(jnp.float32), axis=0
+    )
+    dt_low = proj[:, :RANK].astype(jnp.bfloat16)
+    width = inner.shape[1]
+    bmat = jnp.broadcast_to(proj[:, RANK : RANK + STATE, None], (local_tok, STATE, 128))
+    cmat = jnp.broadcast_to(proj[:, RANK + STATE :, None], (local_tok, STATE, 128))
+    step, local_end = pl.pallas_call(
+        first_pass,
+        out_shape=(
+            jax.ShapeDtypeStruct((local_tok, width), jnp.float32),
+            jax.ShapeDtypeStruct((STATE + 8, width), jnp.float32),
+        ),
+        scratch_shapes=[pltpu.VMEM((local_tok, width), jnp.float32)],
+        compiler_params=pltpu.CompilerParams(vmem_limit_bytes=VMEM_LIMIT),
+    )(dt_low, dt_weight, dt_bias[None, :], inner, a_rate, bmat)
+    ends = direct_gather(local_end, "seq", 2)
+    me = lax.axis_index("seq")
+    start = jnp.zeros_like(a_rate)
+    for block in range(n_seq - 1):
+        after = jnp.exp(-a_rate * ends[block, STATE : STATE + 1]) * start + ends[block, :STATE]
+        start = jnp.where(block < me, after, start)
+    gated = pl.pallas_call(
+        second_pass,
+        out_shape=jax.ShapeDtypeStruct((local_tok, width), jnp.bfloat16),
+        scratch_shapes=[pltpu.VMEM((local_tok, width), jnp.float32)],
+        compiler_params=pltpu.CompilerParams(vmem_limit_bytes=VMEM_LIMIT),
+    )(step, inner, a_rate, bmat, cmat, start, skip_d[None, :], zpart)
     terms = jnp.dot(
         gated,
         lax.all_gather(out_weight, "seq", axis=1, tiled=True),

time: 926 us -> 426 us (0.46); the launches traced: 910 us -> 426 us
  local copies, waits for them, and re-layouts: 290 us -> 10.6 us
  other arithmetic: 109 us -> 6.67 us
  starting transfers between devices: 94.1 us -> 10.8 us
  waiting for transfers between devices: 327 us -> 260 us
  Pallas kernels: 0 us -> 63.9 us
  blocking collectives: 30.8 us -> 16.9 us
    pad x24 -> x0, local copies, waits for them, and re-layouts: 268 us -> none  [per_device(): lax.associative_scan(combine_states, (decay, source), axis=0)]
    ppermute x16 -> x1, starting transfers between devices: 86.9 us -> 3.39 us  [from_behind(): return lax.ppermute(block, axis, route)]
    add x24 -> x0, other arithmetic: 67.8 us -> none  [the longest x12 34.6 us: combine_states(): return (earlier[0] * later[0], later[0] * earlier[1] + later[1])]
    pallas_call x0 -> x4, Pallas kernels: none -> 63.9 us  [the longest x2 52.8 us: direct_gather(): pl.pallas_call(functools.partial(gather_kernel, axis, n), out_shape=jax.S...]
    psum x1 -> x0, waiting for transfers between devices: 44.8 us -> none  [per_device(): lax.psum(partial_value[:, :RANK].astype(jnp.bfloat16), 'expert')]
    ppermute x16 -> x1, waiting for transfers between devices: 25.2 us -> 0.54 us  [from_behind(): return lax.ppermute(block, axis, route)]
    concatenate x12 -> x0, other arithmetic: 18.9 us -> none  [per_device(): lax.associative_scan(combine_states, (decay, source), axis=0)]
    psum x1 -> x0, blocking collectives: 14 us -> none  [per_device(): lax.psum(partial_value[:, RANK:].astype(jnp.bfloat16), 'expert')]
  transfers between devices with their start and end apart: 24 -> 8, of which waited for: 23 -> 8; matrix products, arithmetic and copies ran while one was open for 43% -> 5% of each run, Pallas kernels for 0% -> 15%
where the time goes in v2:
time: 426 us
  waiting for transfers between devices  260 us (61%)
  Pallas kernels  63.9 us (15%)
  matrix products  43.5 us (10%)
  blocking collectives  16.9 us (4%)
  between operations  13.7 us (3%)
  starting transfers between devices  10.8 us (3%)
  local copies, waits for them, and re-layouts  10.6 us (2%)
  other arithmetic  6.67 us (2%)
    all_gather x1, waiting for transfers between devices, per_device(): lax.all_gather(in_weight, 'seq', axis=1, tiled=True)  112 us
    pallas_call x2, Pallas kernels, direct_gather(): pl.pallas_call(functools.partial(gather_kernel, axis, n), out_shape=jax.S...  52.8 us
    reduce_scatter x1, waiting for transfers between devices, per_device(): lax.psum_scatter(jnp.dot(act, w_down[0], preferred_element_type=jnp.float...  38 us
    reduce_scatter x1, waiting for transfers between devices, per_device(): lax.psum_scatter(terms.astype(jnp.bfloat16), 'expert', scatter_dimension=...  30.5 us
    all_gather x1, waiting for transfers between devices, per_device(): lax.all_gather(received.reshape(1, slots_all, dim), 'expert', axis=0, til...  29.1 us
    all_gather x1, waiting for transfers between devices, per_device(): group = lax.all_gather(tokens, 'expert', axis=0, tiled=True)  25.2 us
    all_to_all x1, blocking collectives, per_device(): lax.all_to_all(send.reshape(n_seq, capacity, dim), 'seq', split_axis=0, c...  16.9 us
    dot_general x1, matrix products, per_device(): jnp.dot(act, w_down[0], preferred_element_type=jnp.float32)  16.6 us
  transfers between devices with their start and end apart: 8, of which 8 were waited for; matrix products, arithmetic and copies ran while one was open for 5% of the time, Pallas kernels for 15%

profile of v2, /device:TPU:0, one launch (start us, length us, event | category | flops | bytes accessed | tf_op | source)
XLA Modules:
  0.0 425.7 jit_solution(530944131733962238)
XLA Ops:
  6.5 0.7 all-gather.5.cloned.1.call-update
  7.3 0.7 all-gather.7.cloned.1.call-update
  8.1 0.7 all-gather.9.cloned.1.call-update
  8.8 0.9 fusion.57
  9.7 25.2 %all-gather.5.cloned.1.call-done = bf16[128,4096]{1,0:T(8,128)(2,1)} async-done(((bf16[16,4096]{1,0:T(8,128)(2,1)}), bf16[128,4096]{1,0:T(8,128)(2,1)}) %all-gather.5.cloned.1.call-update) | async-done | bytes 1048592 | tf_op jit(solution)/shard_map/all_gather | solution.py:161
  34.9 1.5 fusion.10
  36.4 112.0 %all-gather.7.cloned.1.call-done = bf16[2,4096,1024]{2,1,0:T(8,128)(2,1)} async-done(((bf16[2,256,1024]{2,1,0:T(8,128)(2,1)}), bf16[2,4096,1024]{2,1,0:T(8,128)(2,1)}) %all-gather.7.cloned.1.call-update) | async-done | bytes 16777232 | tf_op jit(solution)/shard_map/all_gather | solution.py:167
  148.4 8.5 %fusion.16 = f32[128,2,1024]{2,0,1:T(8,128)S(1)} fusion(bf16[2,4096,1024]{2,1,0:T(8,128)(2,1)} %all-gather.7.cloned.1.call-done, bf16[128,4096]{1,0:T(8,128)(2,1)} %all-gather.5.cloned.1.call-done, f32[4096]{0:T(1024)} %param.18, f32[128]{0:T(128)S(1)} %add_rsqrt_fusion.1), kind=kOutput, calls=%fused_computation.20 | convolution fusion | flops 2149580800 | bytes 18891264 | tf_op jit(solution)/shard_map/td,kdc->tkc/dot_general | solution.py:164
  156.9 3.4 collective-permute-start
  160.3 0.9 slice_bitcast_fusion
  161.2 0.5 collective-permute-done
  161.7 0.4 multiply_convert_fusion.1.inner_ref
  162.1 0.3 convolution_convert_fusion.2
  162.4 0.8 copy.38.x_ref
  163.2 14.0 %shard_map.163 = bf16[8,128,288]{2,1,0:T(8,128)(2,1)} custom-call(bf16[128,288]{1,0:T(8,128)(2,1)} %copy.38.x_ref), custom_call_target="tpu_custom_call" | custom-call | tf_op jit(solution)/shard_map/pallas_call | solution.py:68
  177.2 1.3 convert_reduce_fusion
  178.5 0.6 slice.241.low_ref
  179.1 0.1 fusion.56
  179.2 1.3 broadcast_in_dim.19.b_ref
  180.5 4.8 %shard_map.164 = (f32[128,1024]{1,0:T(8,128)}, f32[24,1024]{1,0:T(8,128)}) custom-call(bf16[128,256]{1,0:T(8,128)(2,1)} %slice.241.low_ref, bf16[256,1024]{1,0:T(8,128)(2,1)} %weight_ref.1, f32[1,1024]{1,0:T(1,128)} %bitcast.163, bf16[128,1024]{1,0:T(8,128)(2,1)} %copy-done.2, f32[16,1024]{1,0:T(8,128)} %a_ref.3, f32[128,16,128]{2,1,0:T(8,128)} %broadcast_in_dim.19.b_ref), custom_call_target="tpu_custom_call" | custom-call | tf_op jit(solution)/shard_map/pallas_call | solution.py:186
  185.3 38.8 %shard_map.165 = f32[16,24,1024]{2,1,0:T(8,128)} custom-call(f32[24,1024]{1,0:T(8,128)} %get-tuple-element.8.x_ref), custom_call_target="tpu_custom_call" | custom-call | tf_op jit(solution)/shard_map/pallas_call | solution.py:68
  224.1 1.0 fusion.55
  225.2 2.1 fusion.37.start_ref
  227.3 1.3 broadcast_in_dim.20.c_ref
  228.6 6.3 %shard_map.166 = bf16[128,1024]{1,0:T(8,128)(2,1)} custom-call(f32[128,1024]{1,0:T(8,128)} %get-tuple-element.7.step_ref, bf16[128,1024]{1,0:T(8,128)(2,1)} %copy-done.2, f32[16,1024]{1,0:T(8,128)} %a_ref.3, f32[128,16,128]{2,1,0:T(8,128)} %broadcast_in_dim.19.b_ref, f32[128,16,128]{2,1,0:T(8,128)} %broadcast_in_dim.20.c_ref, f32[16,1024]{1,0:T(8,128)} %fusion.37.start_ref, ...), custom_call_target="tpu_custom_call" | custom-call | tf_op jit(solution)/shard_map/pallas_call | solution.py:201
  235.0 12.0 %all-gather.9.cloned.1.call-done = bf16[1024,4096]{1,0:T(8,128)(2,1)} async-done(((bf16[1024,256]{1,0:T(8,128)(2,1)}), bf16[1024,4096]{1,0:T(8,128)(2,1)}) %all-gather.9.cloned.1.call-update) | async-done | bytes 8388624 | tf_op jit(solution)/shard_map/all_gather | solution.py:209
  247.0 5.7 %convolution_convert_fusion = bf16[128,4096]{1,0:T(8,128)(2,1)} fusion(bf16[128,1024]{1,0:T(8,128)(2,1)} %shard_map.166, bf16[1024,4096]{1,0:T(8,128)(2,1)} %all-gather.9.cloned.1.call-done), kind=kOutput, calls=%fused_computation.7 | convolution fusion | flops 1074266112 | bytes 9699328 | tf_op jit(solution)/shard_map/dot_general | solution.py:207
  252.8 0.1 copy.39
  252.9 0.1 eq.30
  253.0 0.2 convert_reduce_fusion.1
  253.1 0.1 reduce_sum.50
  253.2 0.1 copy.40
  253.4 30.5 %reduce-scatter.3.cloned.1.call-done = bf16[16,4096]{1,0:T(8,128)(2,1)} async-done(((bf16[128,4096]{1,0:T(8,128)(2,1)}), bf16[16,4096]{1,0:T(8,128)(2,1)}) %reduce-scatter.3.cloned.1.call-update) | async-done | bytes 131088 | tf_op jit(solution)/shard_map/reduce_scatter | solution.py:212
  283.9 1.1 fusion.31
  285.0 1.3 convolution_convert_fusion.1
  286.2 0.2 reshape.87
  286.4 16.9 %all_to_all.10 = bf16[16,4,4096]{2,1,0:T(4,128)(2,1)S(1)} all-to-all(bf16[16,4,4096]{2,1,0:T(4,128)(2,1)S(1)} %reshape.87), channel_id=1, replica_groups=mesh['seq'=16,'expert'=8] {'seq'}, dimensions={0} | all-to-all | bytes 1048576 | tf_op jit(solution)/shard_map/all_to_all | solution.py:229
  303.4 0.9 reshape.88
  304.3 0.2 reduce-scatter.5.cloned.1.call-start
  304.6 29.1 %all-gather.11.cloned.1.call-done = bf16[8,64,4096]{2,1,0:T(8,128)(2,1)} async-done(((bf16[1,64,4096]{2,1,0:T(8,128)(2,1)}), bf16[8,64,4096]{2,1,0:T(8,128)(2,1)}) %all-gather.11.cloned.1.call-update) | async-done | bytes 4194320 | tf_op jit(solution)/shard_map/all_gather | solution.py:232
  333.7 10.1 %fusion.4 = f32[512,896]{1,0:T(8,128)} fusion(bf16[512,4096]{1,0:T(8,128)(2,1)} %bitcast.165, bf16[1,4096,896]{2,1,0:T(8,128)(2,1)} %param.31), kind=kOutput, calls=%fused_computation.4 | convolution fusion | flops 3758096384 | bytes 13369344 | tf_op jit(solution)/shard_map/dot_general | solution.py:235
  343.8 16.6 %fusion.6 = bf16[512,4096]{1,0:T(8,128)(2,1)} fusion(bf16[1,896,4096]{2,1,0:T(8,128)(2,1)} %param.33, f32[512,896]{1,0:T(8,128)} %fusion.4, bf16[512,4096]{1,0:T(8,128)(2,1)} %bitcast.166, bf16[1,4096,896]{2,1,0:T(8,128)(2,1)} %param.32), kind=kOutput, calls=%fused_computation.6 | convolution fusion | flops 7521042432 | bytes 24903680 | tf_op jit(solution)/shard_map/dot_general | solution.py:239
  360.5 38.0 %reduce-scatter.5.cloned.1.call-done = bf16[64,4096]{1,0:T(8,128)(2,1)} async-done(((bf16[512,4096]{1,0:T(8,128)(2,1)}), bf16[64,4096]{1,0:T(8,128)(2,1)}) %reduce-scatter.5.cloned.1.call-update) | async-done | bytes 524304 | tf_op jit(solution)/shard_map/reduce_scatter | solution.py:238
  398.5 2.0 reshape.90
  400.5 7.1 %all-to-all-start.1 = ((bf16[16,4,4096]{2,1,0:T(4,128)(2,1)}), bf16[16,4,4096]{2,1,0:T(4,128)(2,1)S(1)}, u32[]{:S(2)}, u32[]{:S(2)}) async-start(bf16[16,4,4096]{2,1,0:T(4,128)(2,1)} %reshape.90), calls=%async_computation.3 | async-start | bytes 1048576 | tf_op jit(solution)/shard_map/all_to_all | solution.py:244
  407.7 10.1 %all-to-all-done.1 = bf16[16,4,4096]{2,1,0:T(4,128)(2,1)S(1)} async-done(((bf16[16,4,4096]{2,1,0:T(4,128)(2,1)}), bf16[16,4,4096]{2,1,0:T(4,128)(2,1)S(1)}, u32[]{:S(2)}, u32[]{:S(2)}) %all-to-all-start.1) | async-done | bytes 524320 | tf_op jit(solution)/shard_map/all_to_all | solution.py:244
  417.7 0.1 reshape.91
  417.9 1.0 fusion.9
  (34 shorter events, 0.4 us)
Async XLA Ops:
  6.5 155.5 %copy-start = (bf16[1024,288]{0,1:T(8,128)(2,1)S(1)}, bf16[1024,288]{0,1:T(8,128)(2,1)}, u32[]{:S(2)}) copy-start(bf16[1024,288]{0,1:T(8,128)(2,1)} %param.22) | copy-start | bytes 1769476
  6.5 28.4 %all-gather.5.cloned.1.call-start = ((), (), s32[]{:S(2)}) async-start(), calls=%async_computation.4 | async-start | bytes 1179648 | tf_op jit(solution)/shard_map/all_gather | solution.py:161
  7.3 141.1 %all-gather.7.cloned.1.call-start = ((), (), s32[]{:S(2)}) async-start(), calls=%async_computation.5 | async-start | bytes 17825792 | tf_op jit(solution)/shard_map/all_gather | solution.py:167
  8.0 239.0 %all-gather.9.cloned.1.call-start = ((), (), s32[]{:S(2)}) async-start(), calls=%async_computation.6 | async-start | bytes 8912896 | tf_op jit(solution)/shard_map/all_gather | solution.py:209
  8.7 275.2 %reduce-scatter.3.cloned.1.call-start = ((), (), s32[]{:S(2)}) async-start(), calls=%async_computation.7 | async-start | bytes 1179648 | tf_op jit(solution)/shard_map/reduce_scatter | solution.py:212
  36.4 125.3 %copy-start.7 = (f32[1024]{0:T(1024)S(1)}, f32[1024]{0:T(1024)}, u32[]{:S(2)}) copy-start(f32[1024]{0:T(1024)} %param.21) | copy-start | bytes 12292
  156.9 4.8 %collective-permute-start = (f32[3,1024]{1,0:T(4,128)S(1)}, f32[3,1024]{1,0:T(4,128)S(1)}, u32[]{:S(2)}, u32[]{:S(2)}) collective-permute-start(f32[3,1024]{1,0:T(4,128)S(1)} %slice_bitcast_fusion.2), channel_id=1, source_target_pairs={{0,8},{8,16},{16,24},{24,32},{32,40},{40,48},{48,56},{56,64},{64,7... | collective-permute-start | bytes 36872 | tf_op jit(solution)/shard_map/ppermute | solution.py:22
  162.1 18.4 %copy-start.2 = (bf16[128,1024]{1,0:T(8,128)(2,1)}, bf16[128,1024]{1,0:T(8,128)(2,1)S(1)}, u32[]{:S(2)}) copy-start(bf16[128,1024]{1,0:T(8,128)(2,1)S(1)} %multiply_convert_fusion.1.inner_ref) | copy-start | bytes 786436
  162.1 63.1 %copy-start.5 = (f32[16,1024]{1,0:T(8,128)S(1)}, f32[16,1024]{1,0:T(8,128)}, u32[]{:S(2)}) copy-start(f32[16,1024]{1,0:T(8,128)} %a_ref.3) | copy-start | bytes 196612
  234.9 17.8 %copy-start.8 = (s32[16,2]{0,1:T(2,128)S(1)}, s32[16,2]{0,1:T(2,128)}, u32[]{:S(2)}) copy-start(s32[16,2]{0,1:T(2,128)} %param.29) | copy-start | bytes 388
  234.9 49.0 %copy-start.3 = (bf16[16,4096]{1,0:T(8,128)(2,1)S(1)}, bf16[16,4096]{1,0:T(8,128)(2,1)}, u32[]{:S(2)}) copy-start(bf16[16,4096]{1,0:T(8,128)(2,1)} %param.17) | copy-start | bytes 393220
  234.9 50.0 %copy-start.6 = (f32[4096]{0:T(1024)S(1)}, f32[4096]{0:T(1024)}, u32[]{:S(2)}) copy-start(f32[4096]{0:T(1024)} %param.28) | copy-start | bytes 49156
  252.7 81.0 %all-gather.11.cloned.1.call-start = ((), (), s32[]{:S(2)}) async-start(), calls=%async_computation.8 | async-start | bytes 4718592 | tf_op jit(solution)/shard_map/all_gather | solution.py:232
  304.3 94.1 %reduce-scatter.5.cloned.1.call-start = ((), (), s32[]{:S(2)}) async-start(), calls=%async_computation.9 | async-start | bytes 4718592 | tf_op jit(solution)/shard_map/reduce_scatter | solution.py:238
  343.8 75.0 %copy-start.1 = (bf16[1024,288]{0,1:T(8,128)(2,1)S(1)}, bf16[1024,288]{0,1:T(8,128)(2,1)}, u32[]{:S(2)}) copy-start(bf16[1024,288]{0,1:T(8,128)(2,1)} %param.22) | copy-start | bytes 1769476
  360.4 47.1 %copy-start.9 = (f32[16,2]{0,1:T(2,128)S(1)}, f32[16,2]{0,1:T(2,128)}, u32[]{:S(2)}) copy-start(f32[16,2]{0,1:T(2,128)} %param.30) | copy-start | bytes 388
  360.4 57.4 %copy-start.4 = (bf16[16,4096]{1,0:T(8,128)(2,1)S(1)}, bf16[16,4096]{1,0:T(8,128)(2,1)}, u32[]{:S(2)}) copy-start(bf16[16,4096]{1,0:T(8,128)(2,1)} %reduce-scatter.3.cloned.1.call-done) | copy-start | bytes 393220
  400.5 17.2 %all-to-all-start.1 = ((bf16[16,4,4096]{2,1,0:T(4,128)(2,1)}), bf16[16,4,4096]{2,1,0:T(4,128)(2,1)S(1)}, u32[]{:S(2)}, u32[]{:S(2)}) async-start(bf16[16,4,4096]{2,1,0:T(4,128)(2,1)} %reshape.90), calls=%async_computation.3 | async-start | bytes 1048576 | tf_op jit(solution)/shard_map/all_to_all | solution.py:244
Sparse Core Ops, SparseCore 0:
  9.1 25.7 all-gather.4
  37.0 111.3 all-gather.6
  150.5 96.4 all-gather.8
  252.9 31.0 reduce-scatter.2
  304.5 29.1 all-gather.10
  360.6 37.8 reduce-scatter.4

commit v3 on v2

--- a/solution.py
+++ b/solution.py
@@ -79,6 +79,251 @@
             collective_id=collective_id, has_side_effects=True, vmem_limit_bytes=VMEM_LIMIT
         ),
     )(x)
+
+
+def ring_of(axis_seq, kind):
+    z, y = axis_seq // 4, axis_seq % 4
+    if kind == 0:
+        return y, lambda d: z * 4 + (y + d) % 4
+    return z, lambda d: ((z + d) % 4) * 4 + y
+
+
+def remote(src, dst, sems, index, target):
+    return pltpu.make_async_remote_copy(
+        src_ref=src,
+        dst_ref=dst,
+        send_sem=sems[0].at[index],
+        recv_sem=sems[1].at[index],
+        device_id=target,
+        device_id_type=MESH,
+    )
+
+
+def greet(targets):
+    barrier = pltpu.get_barrier_semaphore()
+    for target in targets:
+        pl.semaphore_signal(barrier, inc=1, device_id=target, device_id_type=MESH)
+    pl.semaphore_wait(barrier, len(targets))
+
+
+def expert_ring(e):
+    return (e ^ 1, (e + 2) % 8, (e + 6) % 8)
+
+
+def project_kernel(
+    tok_ref, gain_ref, w_ref, x_ref, z_ref,
+    n_ref, t_ref, g_ref, p_ref, relay_ref, in_ref,
+    ws, wr, ts, tr, xs, xr, rs, rr, local_sems,
+):
+    s = lax.axis_index("seq")
+    e = lax.axis_index("expert")
+    at_y, along_y = ring_of(s, 0)
+    at_z, along_z = ring_of(s, 1)
+    sib, nxt, prv = expert_ring(e)
+    gather = ((at_y, along_y), (at_z, along_z))
+    reduce = ((at_z, along_z), (at_y, along_y))
+    seq = lambda index: {"seq": index}
+    exp = lambda index: {"expert": index}
+    greet(
+        [seq(along_y(d)) for d in (1, 2, 3)]
+        + [seq(along_z(d)) for d in (1, 2, 3)]
+        + [exp(sib), exp(nxt), exp(prv)]
+    )
+    half = w_ref.shape[1] // 2
+    halves = (pl.ds(0, half), pl.ds(half, half))
+    sent, own = [], []
+    for k, (at, along) in enumerate(gather):
+        for m, (h, d) in enumerate(((0, 1), (1, 3), (1, 1), (0, 3))):
+            copy = remote(
+                w_ref.at[k, halves[h]], g_ref.at[k, at, halves[h]], (ws, wr), k * 6 + m, seq(along(d))
+            )
+            copy.start()
+            sent.append(copy)
+        copy = pltpu.make_async_copy(w_ref.at[k], g_ref.at[k, at], local_sems.at[k])
+        copy.start()
+        own.append(copy)
+    wide = tok_ref[...].astype(jnp.float32)
+    scale = lax.rsqrt(jnp.mean(wide * wide, axis=-1, keepdims=True) + 1e-05)
+    normed = (wide * scale * gain_ref[...]).astype(jnp.bfloat16)
+    for q in range(4):
+        n_ref[0, q] = normed[:, q * 1024 : (q + 1) * 1024]
+        for r in range(4):
+            n_ref[1, q, :, r * 256 : (r + 1) * 256] = normed[:, (r * 4 + q) * 256 : (r * 4 + q + 1) * 256]
+    mine = pl.ds(pl.multiple_of(e * 16, 16), 16)
+    for k, (at, along) in enumerate(reduce):
+        for d in (2, 1, 3):
+            copy = remote(
+                n_ref.at[k, (at + d) % 4], t_ref.at[k, at, mine], (ts, tr), k * 4 + d, seq(along(d))
+            )
+            copy.start()
+            sent.append(copy)
+        copy = pltpu.make_async_copy(n_ref.at[k, at], t_ref.at[k, at, mine], local_sems.at[2 + k])
+        copy.start()
+        own.append(copy)
+    for copy in own:
+        copy.wait()
+    rows_of = lambda index: pl.ds(pl.multiple_of(index * 16, 16), 16)
+
+    def pass_on(k, m, index, part, target):
+        span = (slice(None), slice(0, 2), slice(2, 4))[part]
+        block = t_ref.at[k, span, rows_of(index)]
+        copy = remote(block, block, (xs, xr), k * 9 + m, exp(target))
+        copy.start()
+        sent.append(copy)
+
+    def arrive(k, m, index, part):
+        span = (slice(None), slice(0, 2), slice(2, 4))[part]
+        block = t_ref.at[k, span, rows_of(index)]
+        remote(block, block, (xs, xr), k * 9 + m, exp(sib)).wait_recv()
+
+    for k, (at, along) in enumerate(reduce):
+        for d in (1, 3, 2):
+            remote(
+                n_ref.at[k, at], t_ref.at[k, (at + 4 - d) % 4, mine], (ts, tr), k * 4 + d, seq(along(d))
+            ).wait_recv()
+        pass_on(k, 0, e, 0, nxt)
+        pass_on(k, 1, e, 0, prv)
+        pass_on(k, 2, e, 0, sib)
+    for k, (at, along) in enumerate(gather):
+        remote(
+            w_ref.at[k, halves[0]], g_ref.at[k, (at + 3) % 4, halves[0]], (ws, wr), k * 6, seq(along(1))
+        ).wait_recv()
+        block = g_ref.at[k, (at + 3) % 4, halves[0]]
+        copy = remote(block, block, (ws, wr), k * 6 + 4, seq(along(1)))
+        copy.start()
+        sent.append(copy)
+        remote(
+            w_ref.at[k, halves[1]], g_ref.at[k, (at + 1) % 4, halves[1]], (ws, wr), k * 6 + 1, seq(along(3))
+        ).wait_recv()
+        block = g_ref.at[k, (at + 1) % 4, halves[1]]
+        copy = remote(block, block, (ws, wr), k * 6 + 5, seq(along(3)))
+        copy.start()
+        sent.append(copy)
+    far = (e + 4) % 8
+    for k in range(2):
+        arrive(k, 0, prv, 0)
+        pass_on(k, 3, prv, 1, nxt)
+        pass_on(k, 4, prv, 0, sib)
+        arrive(k, 1, nxt, 0)
+        pass_on(k, 5, nxt, 2, prv)
+        pass_on(k, 6, nxt, 0, sib)
+    for k in range(2):
+        arrive(k, 3, far, 1)
+        pass_on(k, 7, far, 1, sib)
+        arrive(k, 5, far, 2)
+        pass_on(k, 8, far, 2, sib)
+    for k in range(2):
+        arrive(k, 2, e ^ 1, 0)
+        arrive(k, 4, prv ^ 1, 0)
+        arrive(k, 6, nxt ^ 1, 0)
+        arrive(k, 7, far ^ 1, 1)
+        arrive(k, 8, far ^ 1, 2)
+    top, low = pl.ds(0, 64), pl.ds(64, 64)
+    outs = (x_ref, z_ref)
+
+    def product(k, block, put):
+        def tile(c, carry):
+            cols = pl.ds(pl.multiple_of(c * 256, 256), 256)
+            rows = t_ref[k, block]
+            total = jnp.zeros((rows.shape[0], 256), jnp.float32)
+            for q in range(4):
+                total = total + jnp.dot(
+                    rows[:, q * 256 : (q + 1) * 256],
+                    g_ref[k, q, :, cols],
+                    preferred_element_type=jnp.float32,
+                )
+            put(cols, total)
+            return carry
+
+        lax.fori_loop(0, 4, tile, 0)
+
+    def push(k, m, src, dst, target):
+        copy = remote(src, dst, (rs, rr), k * 6 + m, seq(target))
+        copy.start()
+        sent.append(copy)
+
+    def landed(k, m, dst, target):
+        remote(dst, dst, (rs, rr), k * 6 + m, seq(target)).wait_recv()
+
+    for k, (at, along) in enumerate(gather):
+        later = (at + 3) % 4
+        for m, (h, o) in enumerate(((0, 3), (1, 1), (1, 3), (0, 1))):
+            if m >= 2:
+                remote(
+                    w_ref.at[k, halves[h]], g_ref.at[k, (at + o) % 4, halves[h]], (ws, wr), k * 6 + m, seq(along(1))
+                ).wait_recv()
+        for m, h in ((4, 0), (5, 1)):
+            remote(
+                w_ref.at[k, halves[h]], g_ref.at[k, (at + 2) % 4, halves[h]], (ws, wr), k * 6 + m, seq(along(1))
+            ).wait_recv()
+        del later
+        at, along = reduce[k]
+        for d in (2, 1, 3):
+
+            def put(cols, total, k=k, d=d):
+                p_ref[k, d - 1, :, cols] = total.astype(jnp.bfloat16)
+
+            product(k, (at + d) % 4, put)
+            if d == 2:
+                push(k, 0, p_ref.at[k, 1, top], relay_ref.at[k, 0], along(1))
+                push(k, 1, p_ref.at[k, 1, low], relay_ref.at[k, 1], along(3))
+            if d == 1:
+                push(k, 2, p_ref.at[k, 0, low], in_ref.at[k, 0, low], along(1))
+            if d == 3:
+                push(k, 3, p_ref.at[k, 2, top], in_ref.at[k, 1, top], along(3))
+
+        def keep(cols, total, k=k):
+            outs[k][:, cols] = total
+
+        product(k, at, keep)
+    for k, (at, along) in enumerate(reduce):
+        landed(k, 0, relay_ref.at[k, 0], along(1))
+        p_ref[k, 0, top] = (
+            p_ref[k, 0, top].astype(jnp.float32) + relay_ref[k, 0].astype(jnp.float32)
+        ).astype(jnp.bfloat16)
+        push(k, 4, p_ref.at[k, 0, top], in_ref.at[k, 0, top], along(1))
+        landed(k, 1, relay_ref.at[k, 1], along(3))
+        p_ref[k, 2, low] = (
+            p_ref[k, 2, low].astype(jnp.float32) + relay_ref[k, 1].astype(jnp.float32)
+        ).astype(jnp.bfloat16)
+        push(k, 5, p_ref.at[k, 2, low], in_ref.at[k, 1, low], along(3))
+    for k, (at, along) in enumerate(reduce):
+        landed(k, 2, in_ref.at[k, 0, low], along(1))
+        landed(k, 3, in_ref.at[k, 1, top], along(3))
+        landed(k, 4, in_ref.at[k, 0, top], along(1))
+        landed(k, 5, in_ref.at[k, 1, low], along(3))
+        outs[k][...] = outs[k][...] + (in_ref[k, 0].astype(jnp.float32) + in_ref[k, 1].astype(jnp.float32))
+    for copy in sent:
+        copy.wait_send()
+
+
+def project(tokens, gain, weight, collective_id):
+    width = weight.shape[2]
+    out = jax.ShapeDtypeStruct((128, width), jnp.float32)
+    dma = pltpu.SemaphoreType.DMA
+    return pl.pallas_call(
+        project_kernel,
+        out_shape=(out, out),
+        in_specs=[
+            pl.BlockSpec(memory_space=pltpu.VMEM),
+            pl.BlockSpec(memory_space=pltpu.VMEM),
+            pl.BlockSpec(memory_space=pltpu.VMEM),
+        ],
+        out_specs=[pl.BlockSpec(memory_space=pltpu.VMEM)] * 2,
+        scratch_shapes=[
+            pltpu.VMEM((2, 4, 16, 1024), jnp.bfloat16),
+            pltpu.VMEM((2, 4, 128, 1024), jnp.bfloat16),
+            pltpu.VMEM((2, 4, 256, width), jnp.bfloat16),
+            pltpu.VMEM((2, 3, 128, width), jnp.bfloat16),
+            pltpu.VMEM((2, 2, 64, width), jnp.bfloat16),
+            pltpu.VMEM((2, 2, 128, width), jnp.bfloat16),
+            dma((12,)), dma((12,)), dma((8,)), dma((8,)), dma((18,)), dma((18,)), dma((12,)), dma((12,)),
+            dma((4,)),
+        ],
+        compiler_params=pltpu.CompilerParams(
+            collective_id=collective_id, has_side_effects=True, vmem_limit_bytes=VMEM_LIMIT
+        ),
+    )(tokens, gain[None, :], weight)
 
 
 def lanes_of(value, width):
@@ -158,17 +403,8 @@
     rows, dim = tokens.shape
     n_seq = lax.axis_size("seq")
     n_exp = lax.axis_size("expert")
-    group = lax.all_gather(tokens, "expert", axis=0, tiled=True)
-    local_tok = group.shape[0]
-    normed = rms_norm(group, gain_mamba).astype(jnp.bfloat16)
-    both = jnp.einsum(
-        "td,kdc->tkc",
-        normed,
-        lax.all_gather(in_weight, "seq", axis=1, tiled=True),
-        preferred_element_type=jnp.float32,
-    )
-    xpart = both[:, 0]
-    zpart = both[:, 1]
+    xpart, zpart = project(tokens, gain_mamba, in_weight, 3)
+    local_tok = xpart.shape[0]
     edge = from_behind(xpart[local_tok - (CONV - 1) :], "seq", 1)
     padded = jnp.concatenate([edge, xpart], axis=0)
     conv = conv_bias

time: 426 us -> 316 us (0.74)
  waiting for transfers between devices: 260 us -> 109 us
  Pallas kernels: 63.9 us -> 113 us
  matrix products: 43.5 us -> 35.1 us
    all_gather x2 -> x0, waiting for transfers between devices: 137 us -> none  [the longest x1 112 us: per_device(): lax.all_gather(in_weight, 'seq', axis=1, tiled=True)]
    pallas_call x0 -> x1, Pallas kernels: none -> 57.2 us  [project(): pl.pallas_call(project_kernel, out_shape=(out, out), in_specs=[pl.BlockSp...]
    all_gather x1, waiting for transfers between devices: 12 us -> 0.02 us  [per_device(): lax.all_gather(out_weight, 'seq', axis=1, tiled=True)]
    dot_general x1 -> x0, matrix products: 8.5 us -> none  [per_device(): jnp.einsum('td,kdc->tkc', normed, lax.all_gather(in_weight, 'seq', axis=1...]
    pallas_call x2, Pallas kernels: 52.8 us -> 44.3 us  [direct_gather(): pl.pallas_call(functools.partial(gather_kernel, axis, n), out_shape=jax.S...]
  transfers between devices with their start and end apart: 8 -> 6, of which waited for: 8 -> 5; matrix products, arithmetic and copies ran while one was open for 5% -> 4% of each run, Pallas kernels for 15% -> 36%
where the time goes in v3:
time: 316 us; the launch traced here: 315 us
  Pallas kernels  113 us (36%)
  waiting for transfers between devices  109 us (34%)
  matrix products  35.1 us (11%)
  blocking collectives  16.9 us (5%)
  between operations  13.3 us (4%)
  starting transfers between devices  11.1 us (4%)
  local copies, waits for them, and re-layouts  10.5 us (3%)
  other arithmetic  6.99 us (2%)
    pallas_call x1, Pallas kernels, project(): pl.pallas_call(project_kernel, out_shape=(out, out), in_specs=[pl.BlockSp...  57.2 us
    pallas_call x2, Pallas kernels, direct_gather(): pl.pallas_call(functools.partial(gather_kernel, axis, n), out_shape=jax.S...  44.3 us
    reduce_scatter x1, waiting for transfers between devices, per_device(): lax.psum_scatter(jnp.dot(act, w_down[0], preferred_element_type=jnp.float...  37.9 us
    reduce_scatter x1, waiting for transfers between devices, per_device(): lax.psum_scatter(terms.astype(jnp.bfloat16), 'expert', scatter_dimension=...  30.3 us
    all_gather x1, waiting for transfers between devices, per_device(): lax.all_gather(received.reshape(1, slots_all, dim), 'expert', axis=0, til...  29.1 us
    all_to_all x1, blocking collectives, per_device(): lax.all_to_all(send.reshape(n_seq, capacity, dim), 'seq', split_axis=0, c...  16.9 us
    dot_general x1, matrix products, per_device(): jnp.dot(act, w_down[0], preferred_element_type=jnp.float32)  16.6 us
    dot_general x1, matrix products, per_device(): gate = jnp.dot(pooled, w_gate[0], preferred_element_type=jnp.float32)  10.1 us
  transfers between devices with their start and end apart: 6, of which 5 were waited for; matrix products, arithmetic and copies ran while one was open for 4% of the time, Pallas kernels for 36%

profile of v3, /device:TPU:0, one launch (start us, length us, event | category | flops | bytes accessed | tf_op | source)
XLA Modules:
  0.0 315.4 jit_solution(10762795844283578983)
XLA Ops:
  6.5 0.7 all-gather.3.cloned.1.call-update
  7.3 0.0 reduce-scatter.3.cloned.1.call-start
  7.3 57.2 %shard_map.163 = (f32[128,1024]{1,0:T(8,128)}, f32[128,1024]{1,0:T(8,128)}) custom-call(bf16[16,4096]{1,0:T(8,128)(2,1)} %tok_ref.1, f32[1,4096]{1,0:T(1,128)} %bitcast.135, bf16[2,256,1024]{2,1,0:T(8,128)(2,1)} %w_ref.1), custom_call_target="tpu_custom_call" | custom-call | tf_op jit(solution)/shard_map/pallas_call | solution.py:304
  64.6 0.8 slice.125
  65.3 3.7 %collective-permute-start = (f32[3,1024]{1,0:T(4,128)S(1)}, f32[3,1024]{1,0:T(4,128)S(1)}, u32[]{:S(2)}, u32[]{:S(2)}) collective-permute-start(f32[3,1024]{1,0:T(4,128)S(1)} %slice.125), channel_id=1, source_target_pairs={{0,8},{8,16},{16,24},{24,32},{32,40},{40,48},{48,56},{56,64},{64,7... | collective-permute-start | bytes 36872 | tf_op jit(solution)/shard_map/ppermute | solution.py:22
  69.0 0.9 fusion.49
  70.0 0.5 collective-permute-done
  70.5 2.2 multiply_convert_fusion.1.inner_ref
  72.7 0.3 convolution_convert_fusion.2
  73.0 0.8 copy.38.x_ref
  73.8 14.7 %shard_map.164 = bf16[8,128,288]{2,1,0:T(8,128)(2,1)} custom-call(bf16[128,288]{1,0:T(8,128)(2,1)} %copy.38.x_ref), custom_call_target="tpu_custom_call" | custom-call | tf_op jit(solution)/shard_map/pallas_call | solution.py:68
  88.4 1.3 convert_reduce_fusion
  89.7 0.6 slice.222.low_ref
  90.4 0.1 fusion.48
  90.4 1.3 broadcast_in_dim.22.b_ref
  91.8 4.8 %shard_map.165 = (f32[128,1024]{1,0:T(8,128)}, f32[24,1024]{1,0:T(8,128)}) custom-call(bf16[128,256]{1,0:T(8,128)(2,1)} %slice.222.low_ref, bf16[256,1024]{1,0:T(8,128)(2,1)} %weight_ref.1, f32[1,1024]{1,0:T(1,128)} %bitcast.155, bf16[128,1024]{1,0:T(8,128)(2,1)} %copy-done.1, f32[16,1024]{1,0:T(8,128)} %a_ref.3, f32[128,16,128]{2,1,0:T(8,128)} %broadcast_in_dim.22.b_ref), custom_call_target="tpu_custom_call" | custom-call | tf_op jit(solution)/shard_map/pallas_call | solution.py:422
  96.6 29.7 %shard_map.166 = f32[16,24,1024]{2,1,0:T(8,128)} custom-call(f32[24,1024]{1,0:T(8,128)} %get-tuple-element.11.x_ref), custom_call_target="tpu_custom_call" | custom-call | tf_op jit(solution)/shard_map/pallas_call | solution.py:68
  126.3 1.0 fusion.47
  127.3 2.1 fusion.29.start_ref
  129.4 1.4 broadcast_in_dim.46.c_ref
  130.8 6.3 %shard_map.167 = bf16[128,1024]{1,0:T(8,128)(2,1)} custom-call(f32[128,1024]{1,0:T(8,128)} %get-tuple-element.10.step_ref, bf16[128,1024]{1,0:T(8,128)(2,1)} %copy-done.1, f32[16,1024]{1,0:T(8,128)} %a_ref.3, f32[128,16,128]{2,1,0:T(8,128)} %broadcast_in_dim.22.b_ref, f32[128,16,128]{2,1,0:T(8,128)} %broadcast_in_dim.46.c_ref, f32[16,1024]{1,0:T(8,128)} %fusion.29.start_ref, ...), custom_call_target="tpu_custom_call" | custom-call | tf_op jit(solution)/shard_map/pallas_call | solution.py:437
  137.1 0.0 all-gather.3.cloned.1.call-done
  137.1 5.8 %convolution_convert_fusion = bf16[128,4096]{1,0:T(8,128)(2,1)} fusion(bf16[128,1024]{1,0:T(8,128)(2,1)} %shard_map.167, bf16[1024,4096]{1,0:T(8,128)(2,1)} %all-gather.3.cloned.1.call-done), kind=kOutput, calls=%fused_computation.7 | convolution fusion | flops 1074266112 | bytes 9699328 | tf_op jit(solution)/shard_map/dot_general | solution.py:443
  143.0 0.0 reduce-scatter.3.cloned.1.call-update
  143.0 0.0 all-gather.5.cloned.1.call-start
  143.1 0.1 copy.39
  143.1 0.1 eq.30
  143.2 0.2 convert_reduce_fusion.1
  143.4 0.1 reduce_sum.40
  143.5 0.1 copy.40
  143.6 0.1 fusion.44
  143.7 30.3 %reduce-scatter.3.cloned.1.call-done = bf16[16,4096]{1,0:T(8,128)(2,1)} async-done(((bf16[128,4096]{1,0:T(8,128)(2,1)}), bf16[16,4096]{1,0:T(8,128)(2,1)}) %reduce-scatter.3.cloned.1.call-update) | async-done | bytes 131088 | tf_op jit(solution)/shard_map/reduce_scatter | solution.py:448
  174.0 1.1 fusion.23
  175.1 1.3 convolution_convert_fusion.1
  176.3 0.2 reshape.77
  176.5 16.9 %all_to_all.10 = bf16[16,4,4096]{2,1,0:T(4,128)(2,1)S(1)} all-to-all(bf16[16,4,4096]{2,1,0:T(4,128)(2,1)S(1)} %reshape.77), channel_id=1, replica_groups=mesh['seq'=16,'expert'=8] {'seq'}, dimensions={0} | all-to-all | bytes 1048576 | tf_op jit(solution)/shard_map/all_to_all | solution.py:465
  193.4 0.9 reshape.78
  194.4 0.2 reduce-scatter.5.cloned.1.call-start
  194.6 29.1 %all-gather.5.cloned.1.call-done = bf16[8,64,4096]{2,1,0:T(8,128)(2,1)} async-done(((bf16[1,64,4096]{2,1,0:T(8,128)(2,1)}), bf16[8,64,4096]{2,1,0:T(8,128)(2,1)}) %all-gather.5.cloned.1.call-update) | async-done | bytes 4194320 | tf_op jit(solution)/shard_map/all_gather | solution.py:468
  223.8 10.1 %fusion.4 = f32[512,896]{1,0:T(8,128)} fusion(bf16[512,4096]{1,0:T(8,128)(2,1)} %bitcast.157, bf16[1,4096,896]{2,1,0:T(8,128)(2,1)} %param.31), kind=kOutput, calls=%fused_computation.4 | convolution fusion | flops 3758096384 | bytes 13369344 | tf_op jit(solution)/shard_map/dot_general | solution.py:471
  233.9 16.6 %fusion.6 = bf16[512,4096]{1,0:T(8,128)(2,1)} fusion(bf16[1,896,4096]{2,1,0:T(8,128)(2,1)} %param.33, f32[512,896]{1,0:T(8,128)} %fusion.4, bf16[512,4096]{1,0:T(8,128)(2,1)} %bitcast.158, bf16[1,4096,896]{2,1,0:T(8,128)(2,1)} %param.32), kind=kOutput, calls=%fused_computation.6 | convolution fusion | flops 7521042432 | bytes 24903680 | tf_op jit(solution)/shard_map/dot_general | solution.py:475
  250.5 37.9 %reduce-scatter.5.cloned.1.call-done = bf16[64,4096]{1,0:T(8,128)(2,1)} async-done(((bf16[512,4096]{1,0:T(8,128)(2,1)}), bf16[64,4096]{1,0:T(8,128)(2,1)}) %reduce-scatter.5.cloned.1.call-update) | async-done | bytes 524304 | tf_op jit(solution)/shard_map/reduce_scatter | solution.py:474
  288.4 2.0 reshape.80
  290.4 7.1 %all-to-all-start.1 = ((bf16[16,4,4096]{2,1,0:T(4,128)(2,1)}), bf16[16,4,4096]{2,1,0:T(4,128)(2,1)S(1)}, u32[]{:S(2)}, u32[]{:S(2)}) async-start(bf16[16,4,4096]{2,1,0:T(4,128)(2,1)} %reshape.80), calls=%async_computation.3 | async-start | bytes 1048576 | tf_op jit(solution)/shard_map/all_to_all | solution.py:480
  297.6 0.1 select_reduce_fusion
  297.7 10.1 %all-to-all-done.1 = bf16[16,4,4096]{2,1,0:T(4,128)(2,1)S(1)} async-done(((bf16[16,4,4096]{2,1,0:T(4,128)(2,1)}), bf16[16,4,4096]{2,1,0:T(4,128)(2,1)S(1)}, u32[]{:S(2)}, u32[]{:S(2)}) %all-to-all-start.1) | async-done | bytes 524320 | tf_op jit(solution)/shard_map/all_to_all | solution.py:480
  307.7 0.1 reshape.81
  307.8 1.0 fusion.9
  (21 shorter events, 0.1 us)
Async XLA Ops:
  6.5 66.1 %copy-start = (bf16[1024,288]{0,1:T(8,128)(2,1)S(1)}, bf16[1024,288]{0,1:T(8,128)(2,1)}, u32[]{:S(2)}) copy-start(bf16[1024,288]{0,1:T(8,128)(2,1)} %param.22) | copy-start | bytes 1769476
  6.5 130.6 %all-gather.3.cloned.1.call-start = ((), (), s32[]{:S(2)}) async-start(), calls=%async_computation.4 | async-start | bytes 8912896 | tf_op jit(solution)/shard_map/all_gather | solution.py:445
  7.3 166.7 %reduce-scatter.3.cloned.1.call-start = ((), (), s32[]{:S(2)}) async-start(), calls=%async_computation.5 | async-start | bytes 1179648 | tf_op jit(solution)/shard_map/reduce_scatter | solution.py:448
  65.3 5.2 %collective-permute-start = (f32[3,1024]{1,0:T(4,128)S(1)}, f32[3,1024]{1,0:T(4,128)S(1)}, u32[]{:S(2)}, u32[]{:S(2)}) collective-permute-start(f32[3,1024]{1,0:T(4,128)S(1)} %slice.125), channel_id=1, source_target_pairs={{0,8},{8,16},{16,24},{24,32},{32,40},{40,48},{48,56},{56,64},{64,7... | collective-permute-start | bytes 36872 | tf_op jit(solution)/shard_map/ppermute | solution.py:22
  72.7 19.1 %copy-start.1 = (bf16[128,1024]{1,0:T(8,128)(2,1)}, bf16[128,1024]{1,0:T(8,128)(2,1)S(1)}, u32[]{:S(2)}) copy-start(bf16[128,1024]{1,0:T(8,128)(2,1)S(1)} %multiply_convert_fusion.1.inner_ref) | copy-start | bytes 786436
  72.7 54.6 %copy-start.4 = (f32[16,1024]{1,0:T(8,128)S(1)}, f32[16,1024]{1,0:T(8,128)}, u32[]{:S(2)}) copy-start(f32[16,1024]{1,0:T(8,128)} %a_ref.3) | copy-start | bytes 196612
  137.1 6.0 %copy-start.6 = (s32[16,2]{0,1:T(2,128)S(1)}, s32[16,2]{0,1:T(2,128)}, u32[]{:S(2)}) copy-start(s32[16,2]{0,1:T(2,128)} %param.29) | copy-start | bytes 388
  137.1 36.9 %copy-start.2 = (bf16[16,4096]{1,0:T(8,128)(2,1)S(1)}, bf16[16,4096]{1,0:T(8,128)(2,1)}, u32[]{:S(2)}) copy-start(bf16[16,4096]{1,0:T(8,128)(2,1)} %tok_ref.1) | copy-start | bytes 393220
  137.1 38.0 %copy-start.5 = (f32[4096]{0:T(1024)S(1)}, f32[4096]{0:T(1024)}, u32[]{:S(2)}) copy-start(f32[4096]{0:T(1024)} %param.28) | copy-start | bytes 49156
  143.0 80.8 %all-gather.5.cloned.1.call-start = ((), (), s32[]{:S(2)}) async-start(), calls=%async_computation.6 | async-start | bytes 4718592 | tf_op jit(solution)/shard_map/all_gather | solution.py:468
  194.4 94.0 %reduce-scatter.5.cloned.1.call-start = ((), (), s32[]{:S(2)}) async-start(), calls=%async_computation.7 | async-start | bytes 4718592 | tf_op jit(solution)/shard_map/reduce_scatter | solution.py:474
  250.5 47.1 %copy-start.7 = (f32[16,2]{0,1:T(2,128)S(1)}, f32[16,2]{0,1:T(2,128)}, u32[]{:S(2)}) copy-start(f32[16,2]{0,1:T(2,128)} %param.30) | copy-start | bytes 388
  250.5 57.4 %copy-start.3 = (bf16[16,4096]{1,0:T(8,128)(2,1)S(1)}, bf16[16,4096]{1,0:T(8,128)(2,1)}, u32[]{:S(2)}) copy-start(bf16[16,4096]{1,0:T(8,128)(2,1)} %reduce-scatter.3.cloned.1.call-done) | copy-start | bytes 393220
  290.4 17.3 %all-to-all-start.1 = ((bf16[16,4,4096]{2,1,0:T(4,128)(2,1)}), bf16[16,4,4096]{2,1,0:T(4,128)(2,1)S(1)}, u32[]{:S(2)}, u32[]{:S(2)}) async-start(bf16[16,4,4096]{2,1,0:T(4,128)(2,1)} %reshape.80), calls=%async_computation.3 | async-start | bytes 1048576 | tf_op jit(solution)/shard_map/all_to_all | solution.py:480
Sparse Core Ops, SparseCore 0:
  9.5 88.1 all-gather.2
  143.1 30.8 reduce-scatter.2
  194.5 29.1 all-gather.4
  250.6 37.7 reduce-scatter.4

commit v4 on v3

--- a/solution.py
+++ b/solution.py
@@ -14,71 +14,6 @@
 CONV = 4
 RANK = 256
 TOP = 2
-
-
-def from_behind(block, axis, distance):
-    devices = range(lax.axis_size(axis))
-    route = [(i - distance, i) for i in devices if i - distance in devices]
-    return lax.ppermute(block, axis, route)
-
-
-def rms_norm(values, gain):
-    wide = values.astype(jnp.float32)
-    return wide * lax.rsqrt(jnp.mean(wide * wide, axis=-1, keepdims=True) + 1e-05) * gain
-
-
-def gather_kernel(axis, n, x_ref, o_ref, send_sems, recv_sems, local_sem):
-    me = lax.axis_index(axis)
-    barrier = pltpu.get_barrier_semaphore()
-    for d in range(1, n):
-        pl.semaphore_signal(
-            barrier, inc=1, device_id={axis: lax.rem(me + d, n)}, device_id_type=MESH
-        )
-    pl.semaphore_wait(barrier, n - 1)
-    own = pltpu.make_async_copy(x_ref, o_ref.at[me], local_sem)
-    own.start()
-    sent = []
-    for d in range(1, n):
-        copy = pltpu.make_async_remote_copy(
-            src_ref=x_ref,
-            dst_ref=o_ref.at[me],
-            send_sem=send_sems.at[d],
-            recv_sem=recv_sems.at[d],
-            device_id={axis: lax.rem(me + d, n)},
-            device_id_type=MESH,
-        )
-        copy.start()
-        sent.append(copy)
-    own.wait()
-    for d in range(1, n):
-        pltpu.make_async_remote_copy(
-            src_ref=x_ref,
-            dst_ref=o_ref.at[lax.rem(me + n - d, n)],
-            send_sem=send_sems.at[d],
-            recv_sem=recv_sems.at[d],
-            device_id={axis: lax.rem(me + d, n)},
-            device_id_type=MESH,
-        ).wait_recv()
-    for copy in sent:
-        copy.wait_send()
-
-
-def direct_gather(x, axis, collective_id):
-    n = lax.axis_size(axis)
-    return pl.pallas_call(
-        functools.partial(gather_kernel, axis, n),
-        out_shape=jax.ShapeDtypeStruct((n, *x.shape), x.dtype),
-        in_specs=[pl.BlockSpec(memory_space=pltpu.VMEM)],
-        out_specs=pl.BlockSpec(memory_space=pltpu.VMEM),
-        scratch_shapes=[
-            pltpu.SemaphoreType.DMA((n,)),
-            pltpu.SemaphoreType.DMA((n,)),
-            pltpu.SemaphoreType.DMA,
-        ],
-        compiler_params=pltpu.CompilerParams(
-            collective_id=collective_id, has_side_effects=True, vmem_limit_bytes=VMEM_LIMIT
-        ),
-    )(x)
 
 
 def ring_of(axis_seq, kind):
@@ -326,59 +261,471 @@
     )(tokens, gain[None, :], weight)
 
 
+def mailbox(sems, sent):
+    def send(i, src, dst, target):
+        copy = remote(src, dst, sems, i, target)
+        copy.start()
+        sent.append(copy)
+
+    def land(i, dst):
+        remote(dst, dst, sems, i, {"expert": lax.axis_index("expert") ^ 1}).wait_recv()
+
+    return send, land
+
+
+def ring_gather_open(send, base, block, at, to):
+    for m, (h, d) in enumerate(((0, 1), (1, 3), (1, 1), (0, 3))):
+        send(base + m, block(at, h), block(at, h), to(d))
+
+
+def ring_gather_pass(send, land, base, block, at, to):
+    for m, h, o, d in ((0, 0, 3, 1), (1, 1, 1, 3)):
+        ref = block((at + o) % 4, h)
+        land(base + m, ref)
+        send(base + 4 + m, ref, ref, to(d))
+
+
+def expert_gather(send, land, base, block, e):
+    sib, nxt, prv = expert_ring(e)
+    far = (e + 4) % 8
+    to = lambda index: {"expert": index}
+
+    def pass_on(m, index, h, target):
+        ref = block(index, h)
+        send(base + m, ref, ref, to(target))
+
+    pass_on(0, e, None, nxt)
+    pass_on(1, e, None, prv)
+    pass_on(2, e, None, sib)
+    land(base + 0, block(prv, None))
+    pass_on(3, prv, 0, nxt)
+    pass_on(4, prv, None, sib)
+    land(base + 1, block(nxt, None))
+    pass_on(5, nxt, 1, prv)
+    pass_on(6, nxt, None, sib)
+    land(base + 3, block(far, 0))
+    pass_on(7, far, 0, sib)
+    land(base + 5, block(far, 1))
+    pass_on(8, far, 1, sib)
+    land(base + 2, block(sib, None))
+    land(base + 4, block(prv ^ 1, None))
+    land(base + 6, block(nxt ^ 1, None))
+    land(base + 7, block(far ^ 1, 0))
+    land(base + 8, block(far ^ 1, 1))
+
+
+def expert_reduce(send, land, base, src, e, sib_ref, p_ref, relay_ref, in_ref):
+    sib, nxt, prv = expert_ring(e)
+    to = lambda index: {"expert": index}
+    wide = lambda value: value.astype(jnp.float32)
+    half = (pl.ds(0, 32), pl.ds(32, 32))
+    for d in (2, 1, 3, 0):
+        send(base + d, src(((e + 2 * d) % 8) ^ 1), sib_ref.at[d], to(sib))
+    for d in (2, 1, 3):
+        land(base + d, sib_ref.at[d])
+        p_ref[d - 1] = (wide(src((e + 2 * d) % 8)[...]) + wide(sib_ref[d])).astype(jnp.bfloat16)
+        if d == 2:
+            send(base + 4, p_ref.at[1, half[0]], relay_ref.at[0], to(nxt))
+            send(base + 5, p_ref.at[1, half[1]], relay_ref.at[1], to(prv))
+        if d == 1:
+            send(base + 6, p_ref.at[0, half[1]], in_ref.at[0, half[1]], to(nxt))
+        if d == 3:
+            send(base + 7, p_ref.at[2, half[0]], in_ref.at[1, half[0]], to(prv))
+    land(base + 4, relay_ref.at[0])
+    p_ref[0, half[0]] = (wide(p_ref[0, half[0]]) + wide(relay_ref[0])).astype(jnp.bfloat16)
+    send(base + 8, p_ref.at[0, half[0]], in_ref.at[0, half[0]], to(nxt))
+    land(base + 5, relay_ref.at[1])
+    p_ref[2, half[1]] = (wide(p_ref[2, half[1]]) + wide(relay_ref[1])).astype(jnp.bfloat16)
+    send(base + 9, p_ref.at[2, half[1]], in_ref.at[1, half[1]], to(prv))
+    land(base + 0, sib_ref.at[0])
+    total = wide(src(e)[...]) + wide(sib_ref[0])
+    land(base + 6, in_ref.at[0, half[1]])
+    land(base + 7, in_ref.at[1, half[0]])
+    land(base + 8, in_ref.at[0, half[0]])
+    land(base + 9, in_ref.at[1, half[1]])
+    return total + (wide(in_ref[0]) + wide(in_ref[1]))
+
+
+def swap_blocks(send, land, base, out_ref, got_ref, s):
+    for d in (10, 5, 6, 7, 9, 11, 13, 14, 15, 8, 2, 1, 3, 4, 12):
+        to = (s + d) % 16
+        send(base + d, out_ref.at[to], got_ref.at[s], {"seq": to})
+    got_ref[s] = out_ref[s]
+    for d in range(1, 16):
+        land(base + d, got_ref.at[(s + 16 - d) % 16])
+
+
+def all_partners(s, e):
+    return [{"seq": (s + d) % 16} for d in range(1, 16)] + [{"expert": i} for i in expert_ring(e)]
+
+
+def mix_kernel(
+    gated_ref, w_ref, tok_ref, gain_ref, place_ref, order_ref, resid_ref, pool_ref,
+    gg_ref, t_ref, sib_ref, p_ref, relay_ref, in_ref, u_ref, v_ref, n_ref, out_ref, got_ref,
+    gs, gr, es, er, ys, yr, ds, dr, xs, xr,
+):
+    s = lax.axis_index("seq")
+    e = lax.axis_index("expert")
+    at, along = ring_of(s, 0)
+    to = lambda d: {"seq": along(d)}
+    greet(all_partners(s, e))
+    sent = []
+    gsend, gland = mailbox((gs, gr), sent)
+    esend, eland = mailbox((es, er), sent)
+    ysend, yland = mailbox((ys, yr), sent)
+    dsend, dland = mailbox((ds, dr), sent)
+    xsend, xland = mailbox((xs, xr), sent)
+    gg_ref[at] = gated_ref[...]
+    span = (pl.ds(0, 64), pl.ds(64, 64))
+    block = lambda i, h: gg_ref.at[i, span[h]]
+    ring_gather_open(gsend, 0, block, at, to)
+
+    def product(y):
+        def tile(q, carry):
+            total = jnp.dot(gg_ref[y], w_ref[q], preferred_element_type=jnp.float32)
+            rows = pl.ds(pl.multiple_of(y * 16, 16), 16)
+            cols = pl.ds(pl.multiple_of(q * 256, 256), 256)
+            t_ref[:, rows, cols] = total.astype(jnp.bfloat16).reshape(8, 16, 256)
+            return carry
+
+        lax.fori_loop(0, 4, tile, 0)
+
+    product(at)
+    ring_gather_pass(gsend, gland, 0, block, at, to)
+    gland(2, block((at + 3) % 4, 1))
+    product((at + 3) % 4)
+    gland(3, block((at + 1) % 4, 0))
+    product((at + 1) % 4)
+    gland(4, block((at + 2) % 4, 0))
+    gland(5, block((at + 2) % 4, 1))
+    product((at + 2) % 4)
+    total = expert_reduce(
+        esend, eland, 0, lambda i: t_ref.at[i], e, sib_ref, p_ref, relay_ref, in_ref
+    )
+    for y in range(4):
+        u_ref[y] = total[y * 16 : (y + 1) * 16].astype(jnp.bfloat16)
+    for d in (2, 1, 3):
+        ysend(d, u_ref.at[(at + d) % 4], v_ref.at[at], to(d))
+    v_ref[at] = u_ref[at]
+    for d in (1, 3, 2):
+        yland(d, v_ref.at[(at + 4 - d) % 4])
+    mixer = jnp.concatenate(
+        [v_ref[y][:, z * 256 : (z + 1) * 256] for z in range(4) for y in range(4)], axis=1
+    )
+    resid = (tok_ref[...].astype(jnp.float32) + mixer.astype(jnp.float32)).astype(jnp.bfloat16)
+    resid_ref[...] = resid
+    wide = resid.astype(jnp.float32)
+    scale = lax.rsqrt(jnp.mean(wide * wide, axis=-1, keepdims=True) + 1e-05)
+    normed = (wide * scale * gain_ref[...]).astype(jnp.bfloat16)
+    for q in range(4):
+        n_ref[q * 16 : (q + 1) * 16] = normed[:, q * 1024 : (q + 1) * 1024]
+    out_ref[...] = (
+        jnp.dot(place_ref[...], n_ref[...], preferred_element_type=jnp.float32)
+        .astype(jnp.bfloat16)
+        .reshape(16, 16, 1024)
+    )
+    swap_blocks(dsend, dland, 0, out_ref, got_ref, s)
+    rows = jnp.dot(
+        order_ref[...], got_ref[...].reshape(256, 1024), preferred_element_type=jnp.float32
+    ).astype(jnp.bfloat16)
+    for q in range(4):
+        pool_ref[e, :, q * 1024 : (q + 1) * 1024] = rows[q * 64 : (q + 1) * 64]
+    whole = (pl.ds(0, 32), pl.ds(32, 32))
+    expert_gather(
+        xsend, xland, 0, lambda i, h: pool_ref.at[i] if h is None else pool_ref.at[i, whole[h]], e
+    )
+    for copy in sent:
+        copy.wait_send()
+
+
+def mix(gated, weight, tokens, gain, place, order, collective_id):
+    dma = pltpu.SemaphoreType.DMA
+    bf16 = jnp.bfloat16
+    return pl.pallas_call(
+        mix_kernel,
+        out_shape=(
+            jax.ShapeDtypeStruct((16, 4096), bf16),
+            jax.ShapeDtypeStruct((8, 64, 4096), bf16),
+        ),
+        in_specs=[pl.BlockSpec(memory_space=pltpu.VMEM)] * 6,
+        out_specs=[pl.BlockSpec(memory_space=pltpu.VMEM)] * 2,
+        scratch_shapes=[
+            pltpu.VMEM((4, 128, 1024), bf16),
+            pltpu.VMEM((8, 64, 1024), bf16),
+            pltpu.VMEM((4, 64, 1024), bf16),
+            pltpu.VMEM((3, 64, 1024), bf16),
+            pltpu.VMEM((2, 32, 1024), bf16),
+            pltpu.VMEM((2, 64, 1024), bf16),
+            pltpu.VMEM((4, 16, 1024), bf16),
+            pltpu.VMEM((4, 16, 1024), bf16),
+            pltpu.VMEM((64, 1024), bf16),
+            pltpu.VMEM((16, 16, 1024), bf16),
+            pltpu.VMEM((16, 16, 1024), bf16),
+            dma((6,)), dma((6,)), dma((10,)), dma((10,)), dma((4,)), dma((4,)),
+            dma((16,)), dma((16,)), dma((9,)), dma((9,)),
+        ],
+        compiler_params=pltpu.CompilerParams(
+            collective_id=collective_id, has_side_effects=True, vmem_limit_bytes=VMEM_LIMIT
+        ),
+    )(gated, weight, tokens, gain[None, :], place, order)
+
+
+def finish_kernel(
+    terms_ref, resid_ref, back_ref, weigh_ref, o_ref,
+    sib_ref, p_ref, relay_ref, in_ref, stack_ref, out_ref, got_ref,
+    es, er, ds, dr,
+):
+    s = lax.axis_index("seq")
+    e = lax.axis_index("expert")
+    greet(all_partners(s, e))
+    sent = []
+    esend, eland = mailbox((es, er), sent)
+    dsend, dland = mailbox((ds, dr), sent)
+    total = expert_reduce(
+        esend, eland, 0, lambda i: terms_ref.at[i], e, sib_ref, p_ref, relay_ref, in_ref
+    ).astype(jnp.bfloat16)
+    for q in range(4):
+        stack_ref[q * 64 : (q + 1) * 64] = total[:, q * 1024 : (q + 1) * 1024]
+    out_ref[...] = (
+        jnp.dot(back_ref[...], stack_ref[...], preferred_element_type=jnp.float32)
+        .astype(jnp.bfloat16)
+        .reshape(16, 16, 1024)
+    )
+    swap_blocks(dsend, dland, 0, out_ref, got_ref, s)
+    values = got_ref[...].reshape(256, 1024)
+    moe = jnp.dot(weigh_ref[0], values, preferred_element_type=jnp.float32) + jnp.dot(
+        weigh_ref[1], values, preferred_element_type=jnp.float32
+    )
+    for q in range(4):
+        cols = slice(q * 1024, (q + 1) * 1024)
+        o_ref[:, cols] = (
+            resid_ref[:, cols].astype(jnp.float32) + moe[q * 16 : (q + 1) * 16]
+        ).astype(jnp.bfloat16)
+    for copy in sent:
+        copy.wait_send()
+
+
+def finish(terms, resid, back, weigh, collective_id):
+    dma = pltpu.SemaphoreType.DMA
+    bf16 = jnp.bfloat16
+    return pl.pallas_call(
+        finish_kernel,
+        out_shape=jax.ShapeDtypeStruct((16, 4096), bf16),
+        in_specs=[pl.BlockSpec(memory_space=pltpu.VMEM)] * 4,
+        out_specs=pl.BlockSpec(memory_space=pltpu.VMEM),
+        scratch_shapes=[
+            pltpu.VMEM((4, 64, 4096), bf16),
+            pltpu.VMEM((3, 64, 4096), bf16),
+            pltpu.VMEM((2, 32, 4096), bf16),
+            pltpu.VMEM((2, 64, 4096), bf16),
+            pltpu.VMEM((256, 1024), bf16),
+            pltpu.VMEM((16, 16, 1024), bf16),
+            pltpu.VMEM((16, 16, 1024), bf16),
+            dma((10,)), dma((10,)), dma((16,)), dma((16,)),
+        ],
+        compiler_params=pltpu.CompilerParams(
+            collective_id=collective_id, has_side_effects=True, vmem_limit_bytes=VMEM_LIMIT
+        ),
+    )(terms, resid, back, weigh)
+
+
 def lanes_of(value, width):
     return jnp.concatenate([value] * (width // 128), axis=1)
 
 
-def first_pass(low_ref, weight_ref, bias_ref, inner_ref, a_ref, b_ref, step_ref, out_ref, u_ref):
-    tokens, width = inner_ref.shape
+def split_sum(value):
+    top = value.astype(jnp.bfloat16)
+    low = (value - top.astype(jnp.float32)).astype(jnp.bfloat16)
+    width = value.shape[1]
+    return jnp.concatenate(
+        [jnp.broadcast_to(top.astype(jnp.float32), (8, width)), jnp.broadcast_to(low.astype(jnp.float32), (8, width))],
+        axis=0,
+    ).astype(jnp.bfloat16)
+
+
+def read_end(ref, index):
+    final = ref[index, :STATE].astype(jnp.float32)
+    rows = ref[index, STATE:].astype(jnp.float32)
+    return final, rows[0:1] + rows[8:9]
+
+
+def scan_kernel(
+    x_ref, z_ref, taps_ref, cbias_ref, xproj_ref, dtw_ref, dtb_ref, a_ref, skip_ref, w_ref,
+    out_ref, g_ref,
+    pad_ref, inner_ref, part_ref, rbox_ref, proj_ref, b_ref, c_ref, step_ref, u_ref, ybox_ref, zbox_ref, zmsg_ref,
+    ws, wr, as_, ar, bs, br, ys, yr, zs, zr, edge_s, edge_r, local_sem,
+):
+    s = lax.axis_index("seq")
+    e = lax.axis_index("expert")
+    at_y, along_y = ring_of(s, 0)
+    at_z, along_z = ring_of(s, 1)
+    tokens, width = x_ref.shape
+    greet(
+        [{"expert": (e + d) % 8} for d in range(1, 8)]
+        + [{"seq": (s + 1) % 16}, {"seq": (s + 15) % 16}]
+        + [{"seq": along_y(d)} for d in (1, 2, 3)]
+        + [{"seq": along_z(d)} for d in (1, 2, 3)]
+    )
+    sent = []
+    wsend, wland = mailbox((ws, wr), sent)
+    asend, aland = mailbox((as_, ar), sent)
+    bsend, bland = mailbox((bs, br), sent)
+    ysend, yland = mailbox((ys, yr), sent)
+    zsend, zland = mailbox((zs, zr), sent)
+    esend, eland = mailbox((edge_s, edge_r), sent)
+    esend(0, x_ref.at[pl.ds(tokens - 8, 8)], pad_ref.at[pl.ds(0, 8)], {"seq": (s + 1) % 16})
+    own = pltpu.make_async_copy(w_ref, g_ref.at[at_z], local_sem)
+    own.start()
+    half = w_ref.shape[0] // 2
+    span = (pl.ds(0, half), pl.ds(half, half))
+    block = lambda i, h: g_ref.at[i, span[h]]
+    to_z = lambda d: {"seq": along_z(d)}
+    own.wait()
+    ring_gather_open(wsend, 0, block, at_z, to_z)
+    pad_ref[8:] = x_ref[...]
+    eland(0, pad_ref.at[pl.ds(0, 8)])
+    pad_ref[:8] = jnp.where(s > 0, pad_ref[:8], 0.0)
+    part = jnp.zeros((tokens, xproj_ref.shape[1]), jnp.float32)
     for at in range(0, width, 256):
-        cols = pl.ds(at, 256)
-        raw = jnp.dot(low_ref[...], weight_ref[:, cols], preferred_element_type=jnp.float32)
-        raw = raw + bias_ref[:, cols]
+        cols = slice(at, at + 256)
+        conv = jnp.broadcast_to(cbias_ref[:, cols], (tokens, 256))
+        for tap in range(CONV):
+            conv = conv + taps_ref[tap : tap + 1, cols] * pad_ref[5 + tap : 5 + tap + tokens, cols]
+        inner = (conv / (1.0 + jnp.exp(-conv))).astype(jnp.bfloat16)
+        inner_ref[:, cols] = inner
+        part = part + jnp.dot(inner, xproj_ref[cols, :], preferred_element_type=jnp.float32)
+    part_ref[...] = part.astype(jnp.bfloat16).reshape(8, tokens // 8, part.shape[1])
+    for d in (4, 5, 3, 2, 6, 1, 7):
+        to = (e + d) % 8
+        asend(d, part_ref.at[to], rbox_ref.at[e], {"expert": to})
+    rbox_ref[e] = part_ref[e]
+    for d in range(1, 8):
+        aland(d, rbox_ref.at[(e + 8 - d) % 8])
+    proj_ref[e] = jnp.sum(rbox_ref[...].astype(jnp.float32), axis=0)
+    for d in (4, 5, 3, 2, 6, 1, 7):
+        bsend(d, proj_ref.at[e], proj_ref.at[e], {"expert": (e + d) % 8})
+    ring_gather_pass(wsend, wland, 0, block, at_z, to_z)
+    for d in range(1, 8):
+        bland(d, proj_ref.at[(e + 8 - d) % 8])
+    low = proj_ref[:, :, :RANK].reshape(tokens, RANK).astype(jnp.bfloat16)
+    for at in range(0, width, 256):
+        cols = slice(at, at + 256)
+        raw = jnp.dot(low, dtw_ref[:, cols], preferred_element_type=jnp.float32) + dtb_ref[:, cols]
         step = jnp.maximum(raw, 0.0) + jnp.log1p(jnp.exp(-jnp.abs(raw)))
         step_ref[:, cols] = step
         u_ref[:, cols] = step * inner_ref[:, cols].astype(jnp.float32)
+    same = lax.broadcasted_iota(jnp.int32, (1, STATE, STATE), 1) == lax.broadcasted_iota(
+        jnp.int32, (1, STATE, STATE), 2
+    )
+
+    def spread(i, carry):
+        rows = pl.ds(pl.multiple_of(i * 16, 16), 16)
+        for ref, at in ((b_ref, RANK), (c_ref, RANK + STATE)):
+            values = proj_ref[i][:, at : at + STATE]
+            column = jnp.sum(jnp.where(same, values[:, None, :], 0.0), axis=-1, keepdims=True)
+            ref[rows] = jnp.broadcast_to(column, (16, STATE, 128))
+        return carry
+
+    lax.fori_loop(0, 8, spread, 0)
     rate = a_ref[...]
 
-    def group(g, state):
+    def advance(state, step8, u8, r, t):
+        decay = jnp.exp(-(step8[r : r + 1, :] * rate))
+        return decay * state + lanes_of(b_ref[t], width) * u8[r : r + 1, :]
+
+    def first(g, state):
         base = pl.multiple_of(g * 8, 8)
         step8 = step_ref[pl.ds(base, 8), :]
         u8 = u_ref[pl.ds(base, 8), :]
         for r in range(8):
-            decay = jnp.exp(-(step8[r : r + 1, :] * rate))
-            state = decay * state + lanes_of(b_ref[base + r], width) * u8[r : r + 1, :]
+            state = advance(state, step8, u8, r, base + r)
         return state
 
-    final = lax.fori_loop(0, tokens // 8, group, jnp.zeros_like(rate))
-    out_ref[:STATE, :] = final
-    out_ref[STATE : STATE + 8, :] = jnp.broadcast_to(
-        jnp.sum(step_ref[...], axis=0, keepdims=True), (8, width)
-    )
-
-
-def second_pass(step_ref, inner_ref, a_ref, b_ref, c_ref, start_ref, skip_ref, z_ref, out_ref, u_ref):
-    tokens, width = inner_ref.shape
-    u_ref[...] = step_ref[...] * inner_ref[...].astype(jnp.float32)
-    rate = a_ref[...]
-
-    def group(g, state):
+    final = lax.fori_loop(0, tokens // 8, first, jnp.zeros_like(rate))
+    ybox_ref[at_y, :STATE] = final.astype(jnp.bfloat16)
+    ybox_ref[at_y, STATE:] = split_sum(jnp.sum(step_ref[...], axis=0, keepdims=True))
+    for d in (2, 1, 3):
+        ysend(d, ybox_ref.at[at_y], ybox_ref.at[at_y], {"seq": along_y(d)})
+    for d in (1, 3, 2):
+        yland(d, ybox_ref.at[(at_y + 4 - d) % 4])
+    plane = jnp.zeros_like(rate)
+    total = jnp.zeros((1, width), jnp.float32)
+    for y in range(4):
+        end, summed = read_end(ybox_ref, y)
+        plane = jnp.exp(-(summed * rate)) * plane + end
+        total = total + summed
+    zmsg_ref[:STATE] = plane.astype(jnp.bfloat16)
+    zmsg_ref[STATE:] = split_sum(total)
+    for d in (2, 1, 3):
+        zsend(d, zmsg_ref, zbox_ref.at[at_z], to_z(d))
+    zbox_ref[at_z] = zmsg_ref[...]
+    for d in (1, 3, 2):
+        zland(d, zbox_ref.at[(at_z + 4 - d) % 4])
+    start = jnp.zeros_like(rate)
+    for ref, at in ((zbox_ref, at_z), (ybox_ref, at_y)):
+        for i in range(3):
+            end, summed = read_end(ref, i)
+            start = jnp.where(i < at, jnp.exp(-(summed * rate)) * start + end, start)
+
+    def second(g, state):
         base = pl.multiple_of(g * 8, 8)
         step8 = step_ref[pl.ds(base, 8), :]
         u8 = u_ref[pl.ds(base, 8), :]
         rows = []
         for r in range(8):
-            decay = jnp.exp(-(step8[r : r + 1, :] * rate))
-            state = decay * state + lanes_of(b_ref[base + r], width) * u8[r : r + 1, :]
+            state = advance(state, step8, u8, r, base + r)
             rows.append(jnp.sum(lanes_of(c_ref[base + r], width) * state, axis=0, keepdims=True))
         u_ref[pl.ds(base, 8), :] = jnp.concatenate(rows, axis=0)
         return state
 
-    lax.fori_loop(0, tokens // 8, group, start_ref[...])
-    z = z_ref[...]
-    out_ref[...] = (
-        (u_ref[...] + skip_ref[...] * inner_ref[...].astype(jnp.float32)) * (z / (1.0 + jnp.exp(-z)))
-    ).astype(out_ref.dtype)
+    lax.fori_loop(0, tokens // 8, second, start)
+    for at in range(0, width, 256):
+        cols = slice(at, at + 256)
+        z = z_ref[:, cols]
+        out_ref[:, cols] = (
+            (u_ref[:, cols] + skip_ref[:, cols] * inner_ref[:, cols].astype(jnp.float32))
+            * (z / (1.0 + jnp.exp(-z)))
+        ).astype(jnp.bfloat16)
+    for m, h, o in ((2, 1, 3), (3, 0, 1), (4, 0, 2), (5, 1, 2)):
+        wland(m, block((at_z + o) % 4, h))
+    for copy in sent:
+        copy.wait_send()
+
+
+def scan(x, z, taps, conv_bias, xproj, dt_weight, dt_bias, rate, skip, weight, collective_id):
+    dma = pltpu.SemaphoreType.DMA
+    tokens, width = x.shape
+    bf16, f32 = jnp.bfloat16, jnp.float32
+    return pl.pallas_call(
+        scan_kernel,
+        out_shape=(
+            jax.ShapeDtypeStruct((tokens, width), bf16),
+            jax.ShapeDtypeStruct((4, *weight.shape), bf16),
+        ),
+        in_specs=[pl.BlockSpec(memory_space=pltpu.VMEM)] * 10,
+        out_specs=[pl.BlockSpec(memory_space=pltpu.VMEM)] * 2,
+        scratch_shapes=[
+            pltpu.VMEM((tokens + 8, width), f32),
+            pltpu.VMEM((tokens, width), bf16),
+            pltpu.VMEM((8, 16, xproj.shape[1]), bf16),
+            pltpu.VMEM((8, 16, xproj.shape[1]), bf16),
+            pltpu.VMEM((8, 16, xproj.shape[1]), f32),
+            pltpu.VMEM((tokens, STATE, 128), f32),
+            pltpu.VMEM((tokens, STATE, 128), f32),
+            pltpu.VMEM((tokens, width), f32),
+            pltpu.VMEM((tokens, width), f32),
+            pltpu.VMEM((4, 2 * STATE, width), bf16),
+            pltpu.VMEM((4, 2 * STATE, width), bf16),
+            pltpu.VMEM((2 * STATE, width), bf16),
+            dma((6,)), dma((6,)), dma((8,)), dma((8,)), dma((8,)), dma((8,)),
+            dma((4,)), dma((4,)), dma((4,)), dma((4,)), dma((1,)), dma((1,)), dma,
+        ],
+        compiler_params=pltpu.CompilerParams(
+            collective_id=collective_id, has_side_effects=True, vmem_limit_bytes=VMEM_LIMIT
+        ),
+    )(
+        x, z, taps, conv_bias[None, :], xproj, dt_weight, dt_bias[None, :], rate, skip[None, :], weight
+    )
 
 
 def per_device(
@@ -404,52 +751,9 @@
     n_seq = lax.axis_size("seq")
     n_exp = lax.axis_size("expert")
     xpart, zpart = project(tokens, gain_mamba, in_weight, 3)
-    local_tok = xpart.shape[0]
-    edge = from_behind(xpart[local_tok - (CONV - 1) :], "seq", 1)
-    padded = jnp.concatenate([edge, xpart], axis=0)
-    conv = conv_bias
-    for tap in range(CONV):
-        conv = conv + conv_weight[tap] * padded[tap : tap + local_tok]
-    inner = jax.nn.silu(conv).astype(jnp.bfloat16)
-    partial_value = jnp.dot(inner, xproj_weight, preferred_element_type=jnp.float32)
-    proj = jnp.sum(
-        direct_gather(partial_value.astype(jnp.bfloat16), "expert", 1).astype(jnp.float32), axis=0
-    )
-    dt_low = proj[:, :RANK].astype(jnp.bfloat16)
-    width = inner.shape[1]
-    bmat = jnp.broadcast_to(proj[:, RANK : RANK + STATE, None], (local_tok, STATE, 128))
-    cmat = jnp.broadcast_to(proj[:, RANK + STATE :, None], (local_tok, STATE, 128))
-    step, local_end = pl.pallas_call(
-        first_pass,
-        out_shape=(
-            jax.ShapeDtypeStruct((local_tok, width), jnp.float32),
-            jax.ShapeDtypeStruct((STATE + 8, width), jnp.float32),
-        ),
-        scratch_shapes=[pltpu.VMEM((local_tok, width), jnp.float32)],
-        compiler_params=pltpu.CompilerParams(vmem_limit_bytes=VMEM_LIMIT),
-    )(dt_low, dt_weight, dt_bias[None, :], inner, a_rate, bmat)
-    ends = direct_gather(local_end, "seq", 2)
-    me = lax.axis_index("seq")
-    start = jnp.zeros_like(a_rate)
-    for block in range(n_seq - 1):
-        after = jnp.exp(-a_rate * ends[block, STATE : STATE + 1]) * start + ends[block, :STATE]
-        start = jnp.where(block < me, after, start)
-    gated = pl.pallas_call(
-        second_pass,
-        out_shape=jax.ShapeDtypeStruct((local_tok, width), jnp.bfloat16),
-        scratch_shapes=[pltpu.VMEM((local_tok, width), jnp.float32)],
-        compiler_params=pltpu.CompilerParams(vmem_limit_bytes=VMEM_LIMIT),
-    )(step, inner, a_rate, bmat, cmat, start, skip_d[None, :], zpart)
-    terms = jnp.dot(
-        gated,
-        lax.all_gather(out_weight, "seq", axis=1, tiled=True),
-        preferred_element_type=jnp.float32,
-    )
-    mixer = lax.psum_scatter(
-        terms.astype(jnp.bfloat16), "expert", scatter_dimension=0, tiled=True
-    ).astype(jnp.float32)
-    resid = (tokens.astype(jnp.float32) + mixer).astype(jnp.bfloat16)
-    normed2 = rms_norm(resid, gain_moe).astype(jnp.bfloat16)
+    gated, mixer_weight = scan(
+        xpart, zpart, conv_weight, conv_bias, xproj_weight, dt_weight, dt_bias, a_rate, skip_d, out_weight, 1
+    )
     capacity = max(2, 4 * rows // n_seq)
     slots_all = n_seq * capacity
     flat_ids = expert_ids.reshape(-1)
@@ -458,32 +762,26 @@
     slot = jnp.sum(same.astype(jnp.int32), axis=1)
     target = flat_ids * capacity + slot
     places = target[:, None] == jnp.arange(slots_all, dtype=jnp.int32)[None, :]
-    dispatch_mat = jnp.any(places.reshape(rows, TOP, slots_all), axis=1).astype(jnp.bfloat16)
-    send = jnp.einsum(
-        "rp,rd->pd", dispatch_mat, normed2, preferred_element_type=jnp.float32
-    ).astype(jnp.bfloat16)
-    received = lax.all_to_all(
-        send.reshape(n_seq, capacity, dim), "seq", split_axis=0, concat_axis=0, tiled=True
-    )
-    pooled = lax.all_gather(
-        received.reshape(1, slots_all, dim), "expert", axis=0, tiled=True
-    ).reshape(n_exp * slots_all, dim)
+    eye = jnp.eye(4, dtype=jnp.float32)
+    by_row = places.reshape(rows, TOP, n_seq, capacity)
+    chosen = jnp.any(by_row, axis=1).astype(jnp.float32)
+    place = jnp.einsum("rpi,qk->pqikr", chosen, eye).reshape(4 * slots_all, 4 * rows).astype(jnp.bfloat16)
+    weighting = jnp.sum(
+        jnp.where(by_row, gate_weights[:, :, None, None], 0.0), axis=1
+    )
+    weigh = (eye[:, None, None, :, None] * weighting[None, :, :, None, :]).reshape(4 * rows, 4 * slots_all)
+    weigh_top = weigh.astype(jnp.bfloat16)
+    weigh = jnp.stack([weigh_top, (weigh - weigh_top.astype(jnp.float32)).astype(jnp.bfloat16)])
+    line = jnp.arange(4 * slots_all, dtype=jnp.int32)
+    moved = (line // 4 % 4) * slots_all + line // 16 * 4 + line % 4
+    back = (moved[:, None] == line[None, :]).astype(jnp.bfloat16)
+    resid, pooled = mix(gated, mixer_weight, tokens, gain_moe, place, back.T, 4)
+    pooled = pooled.reshape(n_exp * slots_all, dim)
     gate = jnp.dot(pooled, w_gate[0], preferred_element_type=jnp.float32)
     upper = jnp.dot(pooled, w_up[0], preferred_element_type=jnp.float32)
     act = (jax.nn.silu(gate) * upper).astype(jnp.bfloat16)
-    outputs = lax.psum_scatter(
-        jnp.dot(act, w_down[0], preferred_element_type=jnp.float32).astype(jnp.bfloat16),
-        "expert",
-        scatter_dimension=0,
-        tiled=True,
-    )
-    returned = lax.all_to_all(
-        outputs.reshape(n_seq, capacity, dim), "seq", split_axis=0, concat_axis=0, tiled=True
-    ).reshape(slots_all, dim)
-    weighting = jnp.where(places, gate_weights.reshape(-1)[:, None], 0.0)
-    weighting = jnp.sum(weighting.reshape(rows, TOP, slots_all), axis=1)
-    moe = jnp.dot(weighting, returned.astype(jnp.float32), precision=lax.Precision.HIGHEST)
-    return (resid.astype(jnp.float32) + moe).astype(jnp.bfloat16)
+    terms = jnp.dot(act, w_down[0], preferred_element_type=jnp.float32).astype(jnp.bfloat16)
+    return finish(terms.reshape(n_exp, slots_all, dim), resid, back, weigh, 5)
 
 
 def solution(mesh):

time: 316 us -> 224 us (0.71)
  waiting for transfers between devices: 109 us -> 0 us
  Pallas kernels: 113 us -> 190 us
  blocking collectives: 16.9 us -> 0 us
  between operations: 13.3 us -> 0.13 us
  starting transfers between devices: 11.1 us -> 0 us
  matrix products: 35.1 us -> 26.3 us
  local copies, waits for them, and re-layouts: 10.5 us -> 5.52 us
  other arithmetic: 6.99 us -> 2.13 us
    pallas_call x4 -> x3, Pallas kernels: 55.4 us -> 138 us  [the longest x1 63.7 us: mix(): pl.pallas_call(mix_kernel, out_shape=(jax.ShapeDtypeStruct((16, 4096), bf...]
    reduce_scatter x2 -> x0, waiting for transfers between devices: 68.2 us -> none  [the longest x1 37.9 us: per_device(): lax.psum_scatter(jnp.dot(act, w_down[0], preferred_element_type=jnp.float...]
    all_gather x2 -> x0, waiting for transfers between devices: 29.2 us -> none  [the longest x1 29.1 us: per_device(): lax.all_gather(received.reshape(1, slots_all, dim), 'expert', axis=0, til...]
    all_to_all x1 -> x0, blocking collectives: 16.9 us -> none  [per_device(): lax.all_to_all(send.reshape(n_seq, capacity, dim), 'seq', split_axis=0, c...]
    all_to_all x1 -> x0, waiting for transfers between devices: 10.1 us -> none  [per_device(): lax.all_to_all(outputs.reshape(n_seq, capacity, dim), 'seq', split_axis=0...]
    dot_general x4 -> x0, matrix products: 8.4 us -> none  [the longest x1 5.85 us: per_device(): jnp.dot(gated, lax.all_gather(out_weight, 'seq', axis=1, tiled=True), pre...]
    all_to_all x1 -> x0, starting transfers between devices: 7.12 us -> none  [per_device(): lax.all_to_all(outputs.reshape(n_seq, capacity, dim), 'seq', split_axis=0...]
    pallas_call x1, Pallas kernels: 57.2 us -> 51.5 us  [project(): pl.pallas_call(project_kernel, out_shape=(out, out), in_specs=[pl.BlockSp...]
  transfers between devices with their start and end apart: 6 -> 0, of which waited for: 5 -> 0; matrix products, arithmetic and copies ran while one was open for 4% -> 0% of each run, Pallas kernels for 36% -> 0%
where the time goes in v4:
time: 224 us
  Pallas kernels  190 us (85%)
  matrix products  26.3 us (12%)
  local copies, waits for them, and re-layouts  5.52 us (2%)
    pallas_call x1, Pallas kernels, mix(): pl.pallas_call(mix_kernel, out_shape=(jax.ShapeDtypeStruct((16, 4096), bf...  63.7 us
    pallas_call x1, Pallas kernels, project(): pl.pallas_call(project_kernel, out_shape=(out, out), in_specs=[pl.BlockSp...  51.5 us
    pallas_call x1, Pallas kernels, finish(): pl.pallas_call(finish_kernel, out_shape=jax.ShapeDtypeStruct((16, 4096),...  38.6 us
    pallas_call x1, Pallas kernels, scan(): pl.pallas_call(scan_kernel, out_shape=(jax.ShapeDtypeStruct((tokens, widt...  36 us
    dot_general x1, matrix products, per_device(): jnp.dot(act, w_down[0], preferred_element_type=jnp.float32)  16.5 us
    dot_general x1, matrix products, per_device(): gate = jnp.dot(pooled, w_gate[0], preferred_element_type=jnp.float32)  9.82 us

profile of v4, /device:TPU:0, one launch (start us, length us, event | category | flops | bytes accessed | tf_op | source)
XLA Modules:
  0.0 223.9 jit_solution(7406054346979982622)
XLA Ops:
  0.0 0.0 copy-start
  0.0 51.5 %shard_map.163 = (f32[128,1024]{1,0:T(8,128)}, f32[128,1024]{1,0:T(8,128)}) custom-call(bf16[16,4096]{1,0:T(8,128)(2,1)} %tok_ref.3, f32[1,4096]{1,0:T(1,128)} %bitcast.29, bf16[2,256,1024]{2,1,0:T(8,128)(2,1)} %w_ref.2), custom_call_target="tpu_custom_call" | custom-call | tf_op jit(solution)/shard_map/pallas_call | solution.py:239
  51.5 2.2 copy.41.xproj_ref
  53.7 36.0 %shard_map.164 = (bf16[128,1024]{1,0:T(8,128)(2,1)}, bf16[4,1024,256]{2,1,0:T(8,128)(2,1)}) custom-call(f32[128,1024]{1,0:T(8,128)} %get-tuple-element.11.x_ref, f32[128,1024]{1,0:T(8,128)} %get-tuple-element.12.z_ref, f32[4,1024]{1,0:T(4,128)} %taps_ref.1, f32[1,1024]{1,0:T(1,128)} %bitcast.31, bf16[1024,288]{1,0:T(8,128)(2,1)} %copy.41.xproj_ref, ...), custom_call_target="tpu_custom_call" | custom-call | tf_op jit(solution)/shard_map/pallas_call | solution.py:699
  89.7 0.0 copy-done
  89.7 0.1 copy.43
  89.8 0.1 eq.68
  89.9 0.2 convert_reduce_fusion
  90.1 0.1 reduce_sum.21
  90.2 0.1 copy.44
  90.3 0.1 compare_reduce_fusion
  90.4 0.1 copy.45
  90.5 0.1 copy.42
  90.6 0.2 fusion.13
  90.8 0.8 convert_element_type.64.place_ref
  91.6 0.8 fusion.15
  92.3 63.7 %shard_map.165 = (bf16[16,4096]{1,0:T(8,128)(2,1)}, bf16[8,64,4096]{2,1,0:T(8,128)(2,1)}) custom-call(bf16[128,1024]{1,0:T(8,128)(2,1)} %get-tuple-element.13.gated_ref, bf16[4,1024,256]{2,1,0:T(8,128)(2,1)} %get-tuple-element.14.w_ref, bf16[16,4096]{1,0:T(8,128)(2,1)} %tok_ref.3, f32[1,4096]{1,0:T(1,128)} %bitcast.30, ...), custom_call_target="tpu_custom_call" | custom-call | tf_op jit(solution)/shard_map/pallas_call | solution.py:444
  156.0 9.8 %fusion.4 = f32[512,896]{1,0:T(8,128)S(1)} fusion(bf16[512,4096]{1,0:T(8,128)(2,1)} %bitcast.34, bf16[1,4096,896]{2,1,0:T(8,128)(2,1)} %param.31), kind=kOutput, calls=%fused_computation.4 | convolution fusion | flops 3758096384 | bytes 13369344 | tf_op jit(solution)/shard_map/dot_general | solution.py:780
  165.8 0.0 copy-start.1
  165.9 16.5 %fusion.6 = bf16[512,4096]{1,0:T(8,128)(2,1)} fusion(bf16[1,896,4096]{2,1,0:T(8,128)(2,1)} %param.33, f32[512,896]{1,0:T(8,128)S(1)} %fusion.4, bf16[512,4096]{1,0:T(8,128)(2,1)} %bitcast.35, bf16[1,4096,896]{2,1,0:T(8,128)(2,1)} %param.32), kind=kOutput, calls=%fused_computation.6 | convolution fusion | flops 7521042432 | bytes 24903680 | tf_op jit(solution)/shard_map/dot_general | solution.py:783
  182.3 0.0 copy-done.1
  182.3 0.1 fusion.16
  182.4 0.1 copy.46
  182.5 0.2 broadcast_multiply_fusion
  182.7 0.3 mul.77
  182.9 0.1 copy.47
  183.0 0.6 pad_maximum_fusion.weigh_ref
  183.7 38.6 %shard_map.166 = bf16[16,4096]{1,0:T(8,128)(2,1)} custom-call(bf16[8,64,4096]{2,1,0:T(8,128)(2,1)} %bitcast.28, bf16[16,4096]{1,0:T(8,128)(2,1)} %get-tuple-element.16.resid_ref, bf16[256,256]{1,0:T(8,128)(2,1)} %get-tuple-element.19.back_ref, bf16[2,64,256]{2,1,0:T(8,128)(2,1)} %pad_maximum_fusion.weigh_ref), custom_call_target="tpu_custom_call" | custom-call | tf_op jit(solution)/shard_map/pallas_call | solution.py:511
  222.3 1.6 copy.50
  (6 shorter events, 0.0 us)
Async XLA Ops:
  0.0 89.7 %copy-start = (s32[16,2]{0,1:T(2,128)S(1)}, s32[16,2]{0,1:T(2,128)}, u32[]{:S(2)}) copy-start(s32[16,2]{0,1:T(2,128)} %param.29) | copy-start | bytes 388
  165.8 16.5 %copy-start.1 = (f32[16,2]{0,1:T(2,128)S(1)}, f32[16,2]{0,1:T(2,128)}, u32[]{:S(2)}) copy-start(f32[16,2]{0,1:T(2,128)} %param.30) | copy-start | bytes 388

commit v5 on v4

--- a/solution.py
+++ b/solution.py
@@ -9,6 +9,7 @@
 
 MESH = pl.DeviceIdType.MESH
 VMEM_LIMIT = 56 * 2**20
+PARTS = 2
 
 STATE = 16
 CONV = 4
@@ -67,13 +68,37 @@
     half = w_ref.shape[1] // 2
     halves = (pl.ds(0, half), pl.ds(half, half))
     sent, own = [], []
+    wide_cols = w_ref.shape[2] // PARTS
+    cols_of = [pl.ds(c * wide_cols, wide_cols) for c in range(PARTS)]
+
+    def open_part(c):
+        for k, (at, along) in enumerate(gather):
+            for m, (h, d) in enumerate(((0, 1), (1, 3), (1, 1), (0, 3))):
+                copy = remote(
+                    w_ref.at[k, halves[h], cols_of[c]],
+                    g_ref.at[k, at, halves[h], cols_of[c]],
+                    (ws, wr),
+                    (k * PARTS + c) * 6 + m,
+                    seq(along(d)),
+                )
+                copy.start()
+                sent.append(copy)
+
+    def land_part(c, k, m, o, h):
+        ref = g_ref.at[k, (gather[k][0] + o) % 4, halves[h], cols_of[c]]
+        remote(ref, ref, (ws, wr), (k * PARTS + c) * 6 + m, seq(gather[k][1](1))).wait_recv()
+        return ref
+
+    def pass_part(c):
+        for k, (at, along) in enumerate(gather):
+            for m, o, h, d in ((0, 3, 0, 1), (1, 1, 1, 3)):
+                ref = land_part(c, k, m, o, h)
+                copy = remote(ref, ref, (ws, wr), (k * PARTS + c) * 6 + 4 + m, seq(along(d)))
+                copy.start()
+                sent.append(copy)
+
+    open_part(0)
     for k, (at, along) in enumerate(gather):
-        for m, (h, d) in enumerate(((0, 1), (1, 3), (1, 1), (0, 3))):
-            copy = remote(
-                w_ref.at[k, halves[h]], g_ref.at[k, at, halves[h]], (ws, wr), k * 6 + m, seq(along(d))
-            )
-            copy.start()
-            sent.append(copy)
         copy = pltpu.make_async_copy(w_ref.at[k], g_ref.at[k, at], local_sems.at[k])
         copy.start()
         own.append(copy)
@@ -119,21 +144,9 @@
         pass_on(k, 0, e, 0, nxt)
         pass_on(k, 1, e, 0, prv)
         pass_on(k, 2, e, 0, sib)
-    for k, (at, along) in enumerate(gather):
-        remote(
-            w_ref.at[k, halves[0]], g_ref.at[k, (at + 3) % 4, halves[0]], (ws, wr), k * 6, seq(along(1))
-        ).wait_recv()
-        block = g_ref.at[k, (at + 3) % 4, halves[0]]
-        copy = remote(block, block, (ws, wr), k * 6 + 4, seq(along(1)))
-        copy.start()
-        sent.append(copy)
-        remote(
-            w_ref.at[k, halves[1]], g_ref.at[k, (at + 1) % 4, halves[1]], (ws, wr), k * 6 + 1, seq(along(3))
-        ).wait_recv()
-        block = g_ref.at[k, (at + 1) % 4, halves[1]]
-        copy = remote(block, block, (ws, wr), k * 6 + 5, seq(along(3)))
-        copy.start()
-        sent.append(copy)
+    pass_part(0)
+    if PARTS > 1:
+        open_part(1)
     far = (e + 4) % 8
     for k in range(2):
         arrive(k, 0, prv, 0)
@@ -156,10 +169,10 @@
     top, low = pl.ds(0, 64), pl.ds(64, 64)
     outs = (x_ref, z_ref)
 
-    def product(k, block, put):
-        def tile(c, carry):
-            cols = pl.ds(pl.multiple_of(c * 256, 256), 256)
-            rows = t_ref[k, block]
+    def product(k, block, c, put):
+        rows = t_ref[k, block]
+        for at in range(c * wide_cols, (c + 1) * wide_cols, 256):
+            cols = pl.ds(at, 256)
             total = jnp.zeros((rows.shape[0], 256), jnp.float32)
             for q in range(4):
                 total = total + jnp.dot(
@@ -168,66 +181,70 @@
                     preferred_element_type=jnp.float32,
                 )
             put(cols, total)
-            return carry
-
-        lax.fori_loop(0, 4, tile, 0)
-
-    def push(k, m, src, dst, target):
-        copy = remote(src, dst, (rs, rr), k * 6 + m, seq(target))
+
+    def push(k, c, m, src, dst, target):
+        copy = remote(src, dst, (rs, rr), (k * PARTS + c) * 6 + m, seq(target))
         copy.start()
         sent.append(copy)
 
-    def landed(k, m, dst, target):
-        remote(dst, dst, (rs, rr), k * 6 + m, seq(target)).wait_recv()
-
-    for k, (at, along) in enumerate(gather):
-        later = (at + 3) % 4
-        for m, (h, o) in enumerate(((0, 3), (1, 1), (1, 3), (0, 1))):
-            if m >= 2:
-                remote(
-                    w_ref.at[k, halves[h]], g_ref.at[k, (at + o) % 4, halves[h]], (ws, wr), k * 6 + m, seq(along(1))
-                ).wait_recv()
-        for m, h in ((4, 0), (5, 1)):
-            remote(
-                w_ref.at[k, halves[h]], g_ref.at[k, (at + 2) % 4, halves[h]], (ws, wr), k * 6 + m, seq(along(1))
-            ).wait_recv()
-        del later
-        at, along = reduce[k]
-        for d in (2, 1, 3):
-
-            def put(cols, total, k=k, d=d):
-                p_ref[k, d - 1, :, cols] = total.astype(jnp.bfloat16)
-
-            product(k, (at + d) % 4, put)
-            if d == 2:
-                push(k, 0, p_ref.at[k, 1, top], relay_ref.at[k, 0], along(1))
-                push(k, 1, p_ref.at[k, 1, low], relay_ref.at[k, 1], along(3))
-            if d == 1:
-                push(k, 2, p_ref.at[k, 0, low], in_ref.at[k, 0, low], along(1))
-            if d == 3:
-                push(k, 3, p_ref.at[k, 2, top], in_ref.at[k, 1, top], along(3))
-
-        def keep(cols, total, k=k):
-            outs[k][:, cols] = total
-
-        product(k, at, keep)
-    for k, (at, along) in enumerate(reduce):
-        landed(k, 0, relay_ref.at[k, 0], along(1))
-        p_ref[k, 0, top] = (
-            p_ref[k, 0, top].astype(jnp.float32) + relay_ref[k, 0].astype(jnp.float32)
-        ).astype(jnp.bfloat16)
-        push(k, 4, p_ref.at[k, 0, top], in_ref.at[k, 0, top], along(1))
-        landed(k, 1, relay_ref.at[k, 1], along(3))
-        p_ref[k, 2, low] = (
-            p_ref[k, 2, low].astype(jnp.float32) + relay_ref[k, 1].astype(jnp.float32)
-        ).astype(jnp.bfloat16)
-        push(k, 5, p_ref.at[k, 2, low], in_ref.at[k, 1, low], along(3))
-    for k, (at, along) in enumerate(reduce):
-        landed(k, 2, in_ref.at[k, 0, low], along(1))
-        landed(k, 3, in_ref.at[k, 1, top], along(3))
-        landed(k, 4, in_ref.at[k, 0, top], along(1))
-        landed(k, 5, in_ref.at[k, 1, low], along(3))
-        outs[k][...] = outs[k][...] + (in_ref[k, 0].astype(jnp.float32) + in_ref[k, 1].astype(jnp.float32))
+    def landed(k, c, m, dst):
+        remote(dst, dst, (rs, rr), (k * PARTS + c) * 6 + m, seq(along_y(1))).wait_recv()
+
+    def multiply(c):
+        here = cols_of[c]
+        for d in (2, 1, 3, 0):
+            for k, (at, along) in enumerate(reduce):
+
+                def put(cols, total, k=k, d=d):
+                    if d:
+                        p_ref[k, d - 1, :, cols] = total.astype(jnp.bfloat16)
+                    else:
+                        outs[k][:, cols] = total
+
+                product(k, (at + d) % 4, c, put)
+                if d == 2:
+                    push(k, c, 0, p_ref.at[k, 1, top, here], relay_ref.at[k, 0, :, here], along(1))
+                    push(k, c, 1, p_ref.at[k, 1, low, here], relay_ref.at[k, 1, :, here], along(3))
+                if d == 1:
+                    push(k, c, 2, p_ref.at[k, 0, low, here], in_ref.at[k, 0, low, here], along(1))
+                if d == 3:
+                    push(k, c, 3, p_ref.at[k, 2, top, here], in_ref.at[k, 1, top, here], along(3))
+
+    def add_on_the_way(c):
+        here = cols_of[c]
+        for k, (at, along) in enumerate(reduce):
+            for m, j, rows, side, d in ((0, 0, top, 0, 1), (1, 2, low, 1, 3)):
+                landed(k, c, m, relay_ref.at[k, m, :, here])
+                p_ref[k, j, rows, here] = (
+                    p_ref[k, j, rows, here].astype(jnp.float32)
+                    + relay_ref[k, m, :, here].astype(jnp.float32)
+                ).astype(jnp.bfloat16)
+                push(k, c, 4 + m, p_ref.at[k, j, rows, here], in_ref.at[k, side, rows, here], along(d))
+
+    def close(c):
+        here = cols_of[c]
+        for k in range(2):
+            landed(k, c, 2, in_ref.at[k, 0, low, here])
+            landed(k, c, 3, in_ref.at[k, 1, top, here])
+            landed(k, c, 4, in_ref.at[k, 0, top, here])
+            landed(k, c, 5, in_ref.at[k, 1, low, here])
+            outs[k][:, here] = outs[k][:, here] + (
+                in_ref[k, 0, :, here].astype(jnp.float32) + in_ref[k, 1, :, here].astype(jnp.float32)
+            )
+
+    for c in range(PARTS):
+        for k in range(2):
+            for m, o, h in ((2, 3, 1), (3, 1, 0), (4, 2, 0), (5, 2, 1)):
+                land_part(c, k, m, o, h)
+        multiply(c)
+        if c + 1 < PARTS:
+            pass_part(c + 1)
+        if c + 2 < PARTS:
+            open_part(c + 2)
+        add_on_the_way(c)
+        if c:
+            close(c - 1)
+    close(PARTS - 1)
     for copy in sent:
         copy.wait_send()
 
@@ -252,7 +269,8 @@
             pltpu.VMEM((2, 3, 128, width), jnp.bfloat16),
             pltpu.VMEM((2, 2, 64, width), jnp.bfloat16),
             pltpu.VMEM((2, 2, 128, width), jnp.bfloat16),
-            dma((12,)), dma((12,)), dma((8,)), dma((8,)), dma((18,)), dma((18,)), dma((12,)), dma((12,)),
+            dma((12 * PARTS,)), dma((12 * PARTS,)), dma((8,)), dma((8,)), dma((18,)), dma((18,)),
+            dma((12 * PARTS,)), dma((12 * PARTS,)),
             dma((4,)),
         ],
         compiler_params=pltpu.CompilerParams(
@@ -283,35 +301,6 @@
         ref = block((at + o) % 4, h)
         land(base + m, ref)
         send(base + 4 + m, ref, ref, to(d))
-
-
-def expert_gather(send, land, base, block, e):
-    sib, nxt, prv = expert_ring(e)
-    far = (e + 4) % 8
-    to = lambda index: {"expert": index}
-
-    def pass_on(m, index, h, target):
-        ref = block(index, h)
-        send(base + m, ref, ref, to(target))
-
-    pass_on(0, e, None, nxt)
-    pass_on(1, e, None, prv)
-    pass_on(2, e, None, sib)
-    land(base + 0, block(prv, None))
-    pass_on(3, prv, 0, nxt)
-    pass_on(4, prv, None, sib)
-    land(base + 1, block(nxt, None))
-    pass_on(5, nxt, 1, prv)
-    pass_on(6, nxt, None, sib)
-    land(base + 3, block(far, 0))
-    pass_on(7, far, 0, sib)
-    land(base + 5, block(far, 1))
-    pass_on(8, far, 1, sib)
-    land(base + 2, block(sib, None))
-    land(base + 4, block(prv ^ 1, None))
-    land(base + 6, block(nxt ^ 1, None))
-    land(base + 7, block(far ^ 1, 0))
-    land(base + 8, block(far ^ 1, 1))
 
 
 def expert_reduce(send, land, base, src, e, sib_ref, p_ref, relay_ref, in_ref):
@@ -359,11 +348,57 @@
     return [{"seq": (s + d) % 16} for d in range(1, 16)] + [{"expert": i} for i in expert_ring(e)]
 
 
+def routing(ids_ref, gates_ref):
+    r_of = lax.broadcasted_iota(jnp.int32, (16, 16), 0)
+    c_of = lax.broadcasted_iota(jnp.int32, (16, 16), 1)
+    across = lambda col: jnp.sum(jnp.where(r_of == c_of, col, 0.0), axis=0, keepdims=True)
+    upright = lambda row: jnp.sum(jnp.where(r_of == c_of, row, 0.0), axis=1, keepdims=True)
+    line = [ids_ref[k : k + 1, :].astype(jnp.float32) for k in range(TOP)]
+    column = [upright(row) for row in line]
+    count = lambda hit: jnp.sum(jnp.where(hit, 1.0, 0.0), axis=1, keepdims=True)
+    before, upto = c_of < r_of, c_of <= r_of
+    slot = [
+        count((column[0] == line[0]) & before) + count((column[0] == line[1]) & before),
+        count((column[1] == line[0]) & upto) + count((column[1] == line[1]) & before),
+    ]
+    target = [column[k] * 4.0 + slot[k] for k in range(TOP)]
+    m = lax.broadcasted_iota(jnp.int32, (256, 64), 0)
+    n = lax.broadcasted_iota(jnp.int32, (256, 64), 1)
+    place = m // 16 * 4 + m % 4
+    hit = jnp.zeros((256, 64), jnp.float32)
+    for k in range(TOP):
+        wide = jnp.concatenate([across(target[k])] * 4, axis=1)
+        hit = hit + jnp.where((place.astype(jnp.float32) == wide) & (m // 4 % 4 == n // 16), 1.0, 0.0)
+    m = lax.broadcasted_iota(jnp.int32, (64, 256), 1)
+    n = lax.broadcasted_iota(jnp.int32, (64, 256), 0)
+    place = m // 16 * 4 + m % 4
+    weigh = jnp.zeros((64, 256), jnp.float32)
+    for k in range(TOP):
+        tall = jnp.concatenate([target[k]] * 4, axis=0)
+        gate = jnp.concatenate([upright(gates_ref[k : k + 1, :])] * 4, axis=0)
+        weigh = weigh + jnp.where((place.astype(jnp.float32) == tall) & (m // 4 % 4 == n // 16), gate, 0.0)
+    top = weigh.astype(jnp.bfloat16)
+    return hit.astype(jnp.bfloat16), top, (weigh - top.astype(jnp.float32)).astype(jnp.bfloat16)
+
+
+def reorder(flip):
+    m = lax.broadcasted_iota(jnp.int32, (256, 256), flip)
+    n = lax.broadcasted_iota(jnp.int32, (256, 256), 1 - flip)
+    return jnp.where(m // 4 % 4 * 64 + m // 16 * 4 + m % 4 == n, 1.0, 0.0).astype(jnp.bfloat16)
+
+
 def mix_kernel(
-    gated_ref, w_ref, tok_ref, gain_ref, place_ref, order_ref, resid_ref, pool_ref,
-    gg_ref, t_ref, sib_ref, p_ref, relay_ref, in_ref, u_ref, v_ref, n_ref, out_ref, got_ref,
-    gs, gr, es, er, ys, yr, ds, dr, xs, xr,
+    gated_ref, w_ref, tok_ref, gain_ref, ids_ref, gates_ref, wg_hbm, wu_hbm, wd_hbm, o_ref,
+    wg_ref, wu_ref, wd_ref, act_ref, pool_ref, part_ref, sib2_ref, p2_ref, relay2_ref, in2_ref, stack_ref,
+    gg_ref, t_ref, sib_ref, p_ref, relay_ref, in_ref, u_ref, v_ref, n_ref, out_ref, got_ref, back_out_ref, back_got_ref, place_ref, order_ref, back_ref, weigh_ref,
+    gs, gr, es, er, ys, yr, ds, dr, xs, xr, rs, rr, bs, br, fetch_sems,
 ):
+    fetches = [
+        pltpu.make_async_copy(src.at[0], dst, fetch_sems.at[i])
+        for i, (src, dst) in enumerate(((wg_hbm, wg_ref), (wu_hbm, wu_ref), (wd_hbm, wd_ref)))
+    ]
+    for fetch in fetches:
+        fetch.start()
     s = lax.axis_index("seq")
     e = lax.axis_index("expert")
     at, along = ring_of(s, 0)
@@ -375,10 +410,16 @@
     ysend, yland = mailbox((ys, yr), sent)
     dsend, dland = mailbox((ds, dr), sent)
     xsend, xland = mailbox((xs, xr), sent)
+    rsend, rland = mailbox((rs, rr), sent)
+    bsend, bland = mailbox((bs, br), sent)
     gg_ref[at] = gated_ref[...]
     span = (pl.ds(0, 64), pl.ds(64, 64))
     block = lambda i, h: gg_ref.at[i, span[h]]
     ring_gather_open(gsend, 0, block, at, to)
+
+    place_ref[...], weigh_ref[0], weigh_ref[1] = routing(ids_ref, gates_ref)
+    back_ref[...] = reorder(0)
+    order_ref[...] = reorder(1)
 
     def product(y):
         def tile(q, carry):
@@ -413,7 +454,6 @@
         [v_ref[y][:, z * 256 : (z + 1) * 256] for z in range(4) for y in range(4)], axis=1
     )
     resid = (tok_ref[...].astype(jnp.float32) + mixer.astype(jnp.float32)).astype(jnp.bfloat16)
-    resid_ref[...] = resid
     wide = resid.astype(jnp.float32)
     scale = lax.rsqrt(jnp.mean(wide * wide, axis=-1, keepdims=True) + 1e-05)
     normed = (wide * scale * gain_ref[...]).astype(jnp.bfloat16)
@@ -430,26 +470,136 @@
     ).astype(jnp.bfloat16)
     for q in range(4):
         pool_ref[e, :, q * 1024 : (q + 1) * 1024] = rows[q * 64 : (q + 1) * 64]
-    whole = (pl.ds(0, 32), pl.ds(32, 32))
-    expert_gather(
-        xsend, xland, 0, lambda i, h: pool_ref.at[i] if h is None else pool_ref.at[i, whole[h]], e
-    )
+    sib, nxt, prv = expert_ring(e)
+    far = (e + 4) % 8
+    chip = lambda d: (e // 2 + d) % 4
+    to_e = lambda index: {"expert": index}
+    f32 = lambda value: value.astype(jnp.float32)
+    half = (pl.ds(0, 32), pl.ds(32, 32))
+
+    def rows_of(index, h):
+        return pool_ref.at[index] if h is None else pool_ref.at[index, half[h]]
+
+    def pass_on(m, index, h, target):
+        ref = rows_of(index, h)
+        xsend(m, ref, ref, to_e(target))
+
+    def experts(c):
+        pair = pl.ds(c * 2, 2)
+        rows = pool_ref[pair].reshape(128, 4096)
+
+        def hidden(cols):
+            gate = jnp.dot(rows, wg_ref[:, cols], preferred_element_type=jnp.float32)
+            upper = jnp.dot(rows, wu_ref[:, cols], preferred_element_type=jnp.float32)
+            act_ref[:, cols] = (gate / (1.0 + jnp.exp(-gate)) * upper).astype(jnp.bfloat16)
+
+        def hidden_tile(i, carry):
+            hidden(pl.ds(pl.multiple_of(i * 256, 256), 256))
+            return carry
+
+        lax.fori_loop(0, 3, hidden_tile, 0)
+        hidden(pl.ds(768, 128))
+        act = act_ref[...]
+
+        def down_tile(i, carry):
+            cols = pl.ds(pl.multiple_of(i * 512, 512), 512)
+            total = jnp.dot(act, wd_ref[:, cols], preferred_element_type=jnp.float32)
+            part_ref[pair, :, cols] = total.astype(jnp.bfloat16).reshape(2, 64, 512)
+            return carry
+
+        lax.fori_loop(0, 8, down_tile, 0)
+
+    def offer(d):
+        rsend(d, part_ref.at[((e + 2 * d) % 8) ^ 1], sib2_ref.at[d], to_e(sib))
+
+    def pair_sum(d):
+        rland(d, sib2_ref.at[d])
+        return f32(part_ref[(e + 2 * d) % 8]) + f32(sib2_ref[d])
+
+    pass_on(0, e, None, nxt)
+    pass_on(1, e, None, prv)
+    pass_on(2, e, None, sib)
+    for fetch in fetches:
+        fetch.wait()
+    xland(2, rows_of(sib, None))
+    experts(chip(0))
+    offer(0)
+    xland(0, rows_of(prv, None))
+    pass_on(3, prv, 0, nxt)
+    pass_on(4, prv, None, sib)
+    xland(1, rows_of(nxt, None))
+    pass_on(5, nxt, 1, prv)
+    pass_on(6, nxt, None, sib)
+    xland(6, rows_of(nxt ^ 1, None))
+    experts(chip(1))
+    offer(1)
+    xland(3, rows_of(far, 0))
+    pass_on(7, far, 0, sib)
+    xland(5, rows_of(far, 1))
+    pass_on(8, far, 1, sib)
+    p2_ref[0] = pair_sum(1).astype(jnp.bfloat16)
+    rsend(6, p2_ref.at[0, half[1]], in2_ref.at[0, half[1]], to_e(nxt))
+    xland(7, rows_of(far ^ 1, 0))
+    xland(8, rows_of(far ^ 1, 1))
+    experts(chip(2))
+    offer(2)
+    xland(4, rows_of(prv ^ 1, None))
+    p2_ref[1] = pair_sum(2).astype(jnp.bfloat16)
+    rsend(4, p2_ref.at[1, half[0]], relay2_ref.at[0], to_e(nxt))
+    rsend(5, p2_ref.at[1, half[1]], relay2_ref.at[1], to_e(prv))
+    experts(chip(3))
+    offer(3)
+    rland(4, relay2_ref.at[0])
+    p2_ref[0, half[0]] = (f32(p2_ref[0, half[0]]) + f32(relay2_ref[0])).astype(jnp.bfloat16)
+    rsend(8, p2_ref.at[0, half[0]], in2_ref.at[0, half[0]], to_e(nxt))
+    p2_ref[2] = pair_sum(3).astype(jnp.bfloat16)
+    rsend(7, p2_ref.at[2, half[0]], in2_ref.at[1, half[0]], to_e(prv))
+    rland(5, relay2_ref.at[1])
+    p2_ref[2, half[1]] = (f32(p2_ref[2, half[1]]) + f32(relay2_ref[1])).astype(jnp.bfloat16)
+    rsend(9, p2_ref.at[2, half[1]], in2_ref.at[1, half[1]], to_e(prv))
+    total = pair_sum(0)
+    rland(6, in2_ref.at[0, half[1]])
+    rland(7, in2_ref.at[1, half[0]])
+    rland(8, in2_ref.at[0, half[0]])
+    rland(9, in2_ref.at[1, half[1]])
+    total = (total + (f32(in2_ref[0]) + f32(in2_ref[1]))).astype(jnp.bfloat16)
+    for q in range(4):
+        stack_ref[q * 64 : (q + 1) * 64] = total[:, q * 1024 : (q + 1) * 1024]
+    part_back = jnp.dot(back_ref[...], stack_ref[...], preferred_element_type=jnp.float32)
+    back_out_ref[...] = part_back.astype(jnp.bfloat16).reshape(16, 16, 1024)
+    swap_blocks(bsend, bland, 0, back_out_ref, back_got_ref, s)
+    values = back_got_ref[...].reshape(256, 1024)
+    moe = jnp.dot(weigh_ref[0], values, preferred_element_type=jnp.float32) + jnp.dot(
+        weigh_ref[1], values, preferred_element_type=jnp.float32
+    )
+    for q in range(4):
+        cols = slice(q * 1024, (q + 1) * 1024)
+        o_ref[:, cols] = (f32(resid[:, cols]) + moe[q * 16 : (q + 1) * 16]).astype(jnp.bfloat16)
     for copy in sent:
         copy.wait_send()
 
 
-def mix(gated, weight, tokens, gain, place, order, collective_id):
+def mix(gated, weight, tokens, gain, ids, gates, w_gate, w_up, w_down, collective_id):
     dma = pltpu.SemaphoreType.DMA
     bf16 = jnp.bfloat16
+    whole = pl.BlockSpec(memory_space=pltpu.VMEM)
     return pl.pallas_call(
         mix_kernel,
-        out_shape=(
-            jax.ShapeDtypeStruct((16, 4096), bf16),
-            jax.ShapeDtypeStruct((8, 64, 4096), bf16),
-        ),
-        in_specs=[pl.BlockSpec(memory_space=pltpu.VMEM)] * 6,
-        out_specs=[pl.BlockSpec(memory_space=pltpu.VMEM)] * 2,
+        out_shape=jax.ShapeDtypeStruct((16, 4096), bf16),
+        in_specs=[whole] * 6 + [pl.BlockSpec(memory_space=pl.ANY)] * 3,
+        out_specs=whole,
         scratch_shapes=[
+            pltpu.VMEM(w_gate.shape[1:], bf16),
+            pltpu.VMEM(w_up.shape[1:], bf16),
+            pltpu.VMEM(w_down.shape[1:], bf16),
+            pltpu.VMEM((128, w_gate.shape[2]), bf16),
+            pltpu.VMEM((8, 64, 4096), bf16),
+            pltpu.VMEM((8, 64, 4096), bf16),
+            pltpu.VMEM((4, 64, 4096), bf16),
+            pltpu.VMEM((3, 64, 4096), bf16),
+            pltpu.VMEM((2, 32, 4096), bf16),
+            pltpu.VMEM((2, 64, 4096), bf16),
+            pltpu.VMEM((256, 1024), bf16),
             pltpu.VMEM((4, 128, 1024), bf16),
             pltpu.VMEM((8, 64, 1024), bf16),
             pltpu.VMEM((4, 64, 1024), bf16),
@@ -461,72 +611,19 @@
             pltpu.VMEM((64, 1024), bf16),
             pltpu.VMEM((16, 16, 1024), bf16),
             pltpu.VMEM((16, 16, 1024), bf16),
+            pltpu.VMEM((16, 16, 1024), bf16),
+            pltpu.VMEM((16, 16, 1024), bf16),
+            pltpu.VMEM((256, 64), bf16),
+            pltpu.VMEM((256, 256), bf16),
+            pltpu.VMEM((256, 256), bf16),
+            pltpu.VMEM((2, 64, 256), bf16),
             dma((6,)), dma((6,)), dma((10,)), dma((10,)), dma((4,)), dma((4,)),
-            dma((16,)), dma((16,)), dma((9,)), dma((9,)),
+            dma((16,)), dma((16,)), dma((9,)), dma((9,)), dma((10,)), dma((10,)), dma((16,)), dma((16,)), dma((3,)),
         ],
         compiler_params=pltpu.CompilerParams(
             collective_id=collective_id, has_side_effects=True, vmem_limit_bytes=VMEM_LIMIT
         ),
-    )(gated, weight, tokens, gain[None, :], place, order)
-
-
-def finish_kernel(
-    terms_ref, resid_ref, back_ref, weigh_ref, o_ref,
-    sib_ref, p_ref, relay_ref, in_ref, stack_ref, out_ref, got_ref,
-    es, er, ds, dr,
-):
-    s = lax.axis_index("seq")
-    e = lax.axis_index("expert")
-    greet(all_partners(s, e))
-    sent = []
-    esend, eland = mailbox((es, er), sent)
-    dsend, dland = mailbox((ds, dr), sent)
-    total = expert_reduce(
-        esend, eland, 0, lambda i: terms_ref.at[i], e, sib_ref, p_ref, relay_ref, in_ref
-    ).astype(jnp.bfloat16)
-    for q in range(4):
-        stack_ref[q * 64 : (q + 1) * 64] = total[:, q * 1024 : (q + 1) * 1024]
-    out_ref[...] = (
-        jnp.dot(back_ref[...], stack_ref[...], preferred_element_type=jnp.float32)
-        .astype(jnp.bfloat16)
-        .reshape(16, 16, 1024)
-    )
-    swap_blocks(dsend, dland, 0, out_ref, got_ref, s)
-    values = got_ref[...].reshape(256, 1024)
-    moe = jnp.dot(weigh_ref[0], values, preferred_element_type=jnp.float32) + jnp.dot(
-        weigh_ref[1], values, preferred_element_type=jnp.float32
-    )
-    for q in range(4):
-        cols = slice(q * 1024, (q + 1) * 1024)
-        o_ref[:, cols] = (
-            resid_ref[:, cols].astype(jnp.float32) + moe[q * 16 : (q + 1) * 16]
-        ).astype(jnp.bfloat16)
-    for copy in sent:
-        copy.wait_send()
-
-
-def finish(terms, resid, back, weigh, collective_id):
-    dma = pltpu.SemaphoreType.DMA
-    bf16 = jnp.bfloat16
-    return pl.pallas_call(
-        finish_kernel,
-        out_shape=jax.ShapeDtypeStruct((16, 4096), bf16),
-        in_specs=[pl.BlockSpec(memory_space=pltpu.VMEM)] * 4,
-        out_specs=pl.BlockSpec(memory_space=pltpu.VMEM),
-        scratch_shapes=[
-            pltpu.VMEM((4, 64, 4096), bf16),
-            pltpu.VMEM((3, 64, 4096), bf16),
-            pltpu.VMEM((2, 32, 4096), bf16),
-            pltpu.VMEM((2, 64, 4096), bf16),
-            pltpu.VMEM((256, 1024), bf16),
-            pltpu.VMEM((16, 16, 1024), bf16),
-            pltpu.VMEM((16, 16, 1024), bf16),
-            dma((10,)), dma((10,)), dma((16,)), dma((16,)),
-        ],
-        compiler_params=pltpu.CompilerParams(
-            collective_id=collective_id, has_side_effects=True, vmem_limit_bytes=VMEM_LIMIT
-        ),
-    )(terms, resid, back, weigh)
+    )(gated, weight, tokens, gain[None, :], ids, gates, w_gate, w_up, w_down)
 
 
 def lanes_of(value, width):
@@ -585,7 +682,7 @@
     pad_ref[8:] = x_ref[...]
     eland(0, pad_ref.at[pl.ds(0, 8)])
     pad_ref[:8] = jnp.where(s > 0, pad_ref[:8], 0.0)
-    part = jnp.zeros((tokens, xproj_ref.shape[1]), jnp.float32)
+    part = jnp.zeros((tokens, xproj_ref.shape[0]), jnp.float32)
     for at in range(0, width, 256):
         cols = slice(at, at + 256)
         conv = jnp.broadcast_to(cbias_ref[:, cols], (tokens, 256))
@@ -593,7 +690,9 @@
             conv = conv + taps_ref[tap : tap + 1, cols] * pad_ref[5 + tap : 5 + tap + tokens, cols]
         inner = (conv / (1.0 + jnp.exp(-conv))).astype(jnp.bfloat16)
         inner_ref[:, cols] = inner
-        part = part + jnp.dot(inner, xproj_ref[cols, :], preferred_element_type=jnp.float32)
+        part = part + lax.dot_general(
+            inner, xproj_ref[:, cols], (((1,), (1,)), ((), ())), preferred_element_type=jnp.float32
+        )
     part_ref[...] = part.astype(jnp.bfloat16).reshape(8, tokens // 8, part.shape[1])
     for d in (4, 5, 3, 2, 6, 1, 7):
         to = (e + d) % 8
@@ -724,7 +823,7 @@
             collective_id=collective_id, has_side_effects=True, vmem_limit_bytes=VMEM_LIMIT
         ),
     )(
-        x, z, taps, conv_bias[None, :], xproj, dt_weight, dt_bias[None, :], rate, skip[None, :], weight
+        x, z, taps, conv_bias[None, :], xproj.T, dt_weight, dt_bias[None, :], rate, skip[None, :], weight
     )
 
 
@@ -747,41 +846,13 @@
     w_up,
     w_down,
 ):
-    rows, dim = tokens.shape
-    n_seq = lax.axis_size("seq")
-    n_exp = lax.axis_size("expert")
     xpart, zpart = project(tokens, gain_mamba, in_weight, 3)
     gated, mixer_weight = scan(
         xpart, zpart, conv_weight, conv_bias, xproj_weight, dt_weight, dt_bias, a_rate, skip_d, out_weight, 1
     )
-    capacity = max(2, 4 * rows // n_seq)
-    slots_all = n_seq * capacity
-    flat_ids = expert_ids.reshape(-1)
-    order = jnp.arange(flat_ids.shape[0], dtype=jnp.int32)
-    same = (flat_ids[:, None] == flat_ids[None, :]) & (order[None, :] < order[:, None])
-    slot = jnp.sum(same.astype(jnp.int32), axis=1)
-    target = flat_ids * capacity + slot
-    places = target[:, None] == jnp.arange(slots_all, dtype=jnp.int32)[None, :]
-    eye = jnp.eye(4, dtype=jnp.float32)
-    by_row = places.reshape(rows, TOP, n_seq, capacity)
-    chosen = jnp.any(by_row, axis=1).astype(jnp.float32)
-    place = jnp.einsum("rpi,qk->pqikr", chosen, eye).reshape(4 * slots_all, 4 * rows).astype(jnp.bfloat16)
-    weighting = jnp.sum(
-        jnp.where(by_row, gate_weights[:, :, None, None], 0.0), axis=1
-    )
-    weigh = (eye[:, None, None, :, None] * weighting[None, :, :, None, :]).reshape(4 * rows, 4 * slots_all)
-    weigh_top = weigh.astype(jnp.bfloat16)
-    weigh = jnp.stack([weigh_top, (weigh - weigh_top.astype(jnp.float32)).astype(jnp.bfloat16)])
-    line = jnp.arange(4 * slots_all, dtype=jnp.int32)
-    moved = (line // 4 % 4) * slots_all + line // 16 * 4 + line % 4
-    back = (moved[:, None] == line[None, :]).astype(jnp.bfloat16)
-    resid, pooled = mix(gated, mixer_weight, tokens, gain_moe, place, back.T, 4)
-    pooled = pooled.reshape(n_exp * slots_all, dim)
-    gate = jnp.dot(pooled, w_gate[0], preferred_element_type=jnp.float32)
-    upper = jnp.dot(pooled, w_up[0], preferred_element_type=jnp.float32)
-    act = (jax.nn.silu(gate) * upper).astype(jnp.bfloat16)
-    terms = jnp.dot(act, w_down[0], preferred_element_type=jnp.float32).astype(jnp.bfloat16)
-    return finish(terms.reshape(n_exp, slots_all, dim), resid, back, weigh, 5)
+    return mix(
+        gated, mixer_weight, tokens, gain_moe, expert_ids.T, gate_weights.T, w_gate, w_up, w_down, 4
+    )
 
 
 def solution(mesh):

time: 224 us -> 189 us (0.84)
  matrix products: 26.3 us -> 0 us
  local copies, waits for them, and re-layouts: 5.52 us -> 1.57 us
  Pallas kernels: 190 us -> 187 us
    dot_general x2 -> x0, matrix products: 26.3 us -> none  [the longest x1 16.5 us: per_device(): jnp.dot(act, w_down[0], preferred_element_type=jnp.float32)]
    pallas_call x1, Pallas kernels: 51.5 us -> 48.1 us  [project(): pl.pallas_call(project_kernel, out_shape=(out, out), in_specs=[pl.BlockSp...]
    unnamed x7 -> x1, local copies, waits for them, and re-layouts: 3.88 us -> 1.57 us
    pallas_call x2 -> x1, Pallas kernels: 102 us -> 102 us  [mix(): pl.pallas_call(mix_kernel, out_shape=jax.ShapeDtypeStruct((16, 4096), bf1...]
where the time goes in v5:
time: 189 us; the launch traced here: 188 us
  Pallas kernels  187 us (99%)
    pallas_call x1, Pallas kernels, mix(): pl.pallas_call(mix_kernel, out_shape=jax.ShapeDtypeStruct((16, 4096), bf1...  102 us
    pallas_call x1, Pallas kernels, project(): pl.pallas_call(project_kernel, out_shape=(out, out), in_specs=[pl.BlockSp...  48.1 us
    pallas_call x1, Pallas kernels, scan(): pl.pallas_call(scan_kernel, out_shape=(jax.ShapeDtypeStruct((tokens, widt...  36.2 us

profile of v5, /device:TPU:0, one launch (start us, length us, event | category | flops | bytes accessed | tf_op | source)
XLA Modules:
  0.0 188.2 jit_solution(16001128953322139958)
XLA Ops:
  0.0 48.1 %shard_map.163 = (f32[128,1024]{1,0:T(8,128)}, f32[128,1024]{1,0:T(8,128)}) custom-call(bf16[16,4096]{1,0:T(8,128)(2,1)} %tok_ref.3, f32[1,4096]{1,0:T(1,128)} %bitcast.9, bf16[2,256,1024]{2,1,0:T(8,128)(2,1)} %w_ref.2), custom_call_target="tpu_custom_call" | custom-call | tf_op jit(solution)/shard_map/pallas_call | solution.py:256
  48.1 36.2 %shard_map.164 = (bf16[128,1024]{1,0:T(8,128)(2,1)}, bf16[4,1024,256]{2,1,0:T(8,128)(2,1)}) custom-call(f32[128,1024]{1,0:T(8,128)} %get-tuple-element.9.x_ref, f32[128,1024]{1,0:T(8,128)} %get-tuple-element.10.z_ref, f32[4,1024]{1,0:T(4,128)} %taps_ref.1, f32[1,1024]{1,0:T(1,128)} %bitcast.11, bf16[288,1024]{1,0:T(8,128)(2,1)} %bitcast.8, ...), custom_call_target="tpu_custom_call" | custom-call | tf_op jit(solution)/shard_map/pallas_call | solution.py:798
  84.4 102.2 %shard_map.165 = bf16[16,4096]{1,0:T(8,128)(2,1)} custom-call(bf16[128,1024]{1,0:T(8,128)(2,1)} %get-tuple-element.11.gated_ref, bf16[4,1024,256]{2,1,0:T(8,128)(2,1)} %get-tuple-element.12.w_ref, bf16[16,4096]{1,0:T(8,128)(2,1)} %tok_ref.3, f32[1,4096]{1,0:T(1,128)} %bitcast.10, s32[2,16]{1,0:T(2,128)} %bitcast.14, f32[2,16]{1,0:T(2,128)} %bitcast.15, ...), custom_call_target="tpu_custom_call" | custom-call | tf_op jit(solution)/shard_map/pallas_call | solution.py:586
  186.6 1.6 copy.19

commit v6 on v5

--- a/solution.py
+++ b/solution.py
@@ -335,13 +335,17 @@
     return total + (wide(in_ref[0]) + wide(in_ref[1]))
 
 
-def swap_blocks(send, land, base, out_ref, got_ref, s):
+def swap_send(send, base, v, out_ref, got_ref, s):
+    cols = pl.ds(v * 512, 512)
     for d in (10, 5, 6, 7, 9, 11, 13, 14, 15, 8, 2, 1, 3, 4, 12):
         to = (s + d) % 16
-        send(base + d, out_ref.at[to], got_ref.at[s], {"seq": to})
-    got_ref[s] = out_ref[s]
+        send(base + v * 16 + d, out_ref.at[to, :, cols], got_ref.at[s, :, cols], {"seq": to})
+    got_ref[s, :, cols] = out_ref[s, :, cols]
+
+
+def swap_land(land, base, v, got_ref, s):
     for d in range(1, 16):
-        land(base + d, got_ref.at[(s + 16 - d) % 16])
+        land(base + v * 16 + d, got_ref.at[(s + 16 - d) % 16, :, pl.ds(v * 512, 512)])
 
 
 def all_partners(s, e):
@@ -458,18 +462,14 @@
     scale = lax.rsqrt(jnp.mean(wide * wide, axis=-1, keepdims=True) + 1e-05)
     normed = (wide * scale * gain_ref[...]).astype(jnp.bfloat16)
     for q in range(4):
-        n_ref[q * 16 : (q + 1) * 16] = normed[:, q * 1024 : (q + 1) * 1024]
-    out_ref[...] = (
-        jnp.dot(place_ref[...], n_ref[...], preferred_element_type=jnp.float32)
-        .astype(jnp.bfloat16)
-        .reshape(16, 16, 1024)
-    )
-    swap_blocks(dsend, dland, 0, out_ref, got_ref, s)
-    rows = jnp.dot(
-        order_ref[...], got_ref[...].reshape(256, 1024), preferred_element_type=jnp.float32
-    ).astype(jnp.bfloat16)
-    for q in range(4):
-        pool_ref[e, :, q * 1024 : (q + 1) * 1024] = rows[q * 64 : (q + 1) * 64]
+        for v in range(2):
+            at_col = v * 2048 + q * 512
+            n_ref[q * 16 : (q + 1) * 16, v * 512 : (v + 1) * 512] = normed[:, at_col : at_col + 512]
+    for v in range(2):
+        cols = slice(v * 512, (v + 1) * 512)
+        placed = jnp.dot(place_ref[...], n_ref[:, cols], preferred_element_type=jnp.float32)
+        out_ref[:, :, cols] = placed.astype(jnp.bfloat16).reshape(16, 16, 512)
+        swap_send(dsend, 0, v, out_ref, got_ref, s)
     sib, nxt, prv = expert_ring(e)
     far = (e + 4) % 8
     chip = lambda d: (e // 2 + d) % 4
@@ -477,14 +477,16 @@
     f32 = lambda value: value.astype(jnp.float32)
     half = (pl.ds(0, 32), pl.ds(32, 32))
 
-    def rows_of(index, h):
-        return pool_ref.at[index] if h is None else pool_ref.at[index, half[h]]
-
-    def pass_on(m, index, h, target):
-        ref = rows_of(index, h)
-        xsend(m, ref, ref, to_e(target))
-
-    def experts(c):
+    wide_cols = (pl.ds(0, 2048), pl.ds(2048, 2048))
+
+    def rows_of(index, h, v):
+        return pool_ref.at[index, slice(None) if h is None else half[h], wide_cols[v]]
+
+    def xarrive(m, index, h, v):
+        xland(v * 9 + m, rows_of(index, h, v))
+
+    def experts(d):
+        c = chip(d)
         pair = pl.ds(c * 2, 2)
         rows = pool_ref[pair].reshape(128, 4096)
 
@@ -507,74 +509,109 @@
             part_ref[pair, :, cols] = total.astype(jnp.bfloat16).reshape(2, 64, 512)
             return carry
 
-        lax.fori_loop(0, 8, down_tile, 0)
-
-    def offer(d):
-        rsend(d, part_ref.at[((e + 2 * d) % 8) ^ 1], sib2_ref.at[d], to_e(sib))
-
-    def pair_sum(d):
-        rland(d, sib2_ref.at[d])
-        return f32(part_ref[(e + 2 * d) % 8]) + f32(sib2_ref[d])
-
-    pass_on(0, e, None, nxt)
-    pass_on(1, e, None, prv)
-    pass_on(2, e, None, sib)
+        for v in range(2):
+            lax.fori_loop(v * 4, v * 4 + 4, down_tile, 0)
+            offered = wide_cols[v]
+            rsend(
+                v * 10 + d, part_ref.at[((e + 2 * d) % 8) ^ 1, :, offered], sib2_ref.at[d, :, offered], to_e(sib)
+            )
+
+    def pair_sum(d, v):
+        cols = wide_cols[v]
+        rland(v * 10 + d, sib2_ref.at[d, :, cols])
+        return f32(part_ref[(e + 2 * d) % 8, :, cols]) + f32(sib2_ref[d, :, cols])
+
+    def inbox(side, h, v):
+        return in2_ref.at[side, half[h], wide_cols[v]]
+
+    def add_relay(m, j, h, v):
+        cols = wide_cols[v]
+        rland(v * 10 + 4 + m, relay2_ref.at[m, :, cols])
+        p2_ref[j, half[h], cols] = (f32(p2_ref[j, half[h], cols]) + f32(relay2_ref[m, :, cols])).astype(jnp.bfloat16)
+
+    for v in range(2):
+        swap_land(dland, 0, v, got_ref, s)
+        cols = slice(v * 512, (v + 1) * 512)
+        rows = jnp.dot(
+            order_ref[...], got_ref[:, :, cols].reshape(256, 512), preferred_element_type=jnp.float32
+        ).astype(jnp.bfloat16)
+        for q in range(4):
+            at_col = v * 2048 + q * 512
+            pool_ref[e, :, at_col : at_col + 512] = rows[q * 64 : (q + 1) * 64]
+        for m, target in ((0, nxt), (1, prv), (2, sib)):
+            ref = rows_of(e, None, v)
+            xsend(v * 9 + m, ref, ref, to_e(target))
     for fetch in fetches:
         fetch.wait()
-    xland(2, rows_of(sib, None))
-    experts(chip(0))
-    offer(0)
-    xland(0, rows_of(prv, None))
-    pass_on(3, prv, 0, nxt)
-    pass_on(4, prv, None, sib)
-    xland(1, rows_of(nxt, None))
-    pass_on(5, nxt, 1, prv)
-    pass_on(6, nxt, None, sib)
-    xland(6, rows_of(nxt ^ 1, None))
-    experts(chip(1))
-    offer(1)
-    xland(3, rows_of(far, 0))
-    pass_on(7, far, 0, sib)
-    xland(5, rows_of(far, 1))
-    pass_on(8, far, 1, sib)
-    p2_ref[0] = pair_sum(1).astype(jnp.bfloat16)
-    rsend(6, p2_ref.at[0, half[1]], in2_ref.at[0, half[1]], to_e(nxt))
-    xland(7, rows_of(far ^ 1, 0))
-    xland(8, rows_of(far ^ 1, 1))
-    experts(chip(2))
-    offer(2)
-    xland(4, rows_of(prv ^ 1, None))
-    p2_ref[1] = pair_sum(2).astype(jnp.bfloat16)
-    rsend(4, p2_ref.at[1, half[0]], relay2_ref.at[0], to_e(nxt))
-    rsend(5, p2_ref.at[1, half[1]], relay2_ref.at[1], to_e(prv))
-    experts(chip(3))
-    offer(3)
-    rland(4, relay2_ref.at[0])
-    p2_ref[0, half[0]] = (f32(p2_ref[0, half[0]]) + f32(relay2_ref[0])).astype(jnp.bfloat16)
-    rsend(8, p2_ref.at[0, half[0]], in2_ref.at[0, half[0]], to_e(nxt))
-    p2_ref[2] = pair_sum(3).astype(jnp.bfloat16)
-    rsend(7, p2_ref.at[2, half[0]], in2_ref.at[1, half[0]], to_e(prv))
-    rland(5, relay2_ref.at[1])
-    p2_ref[2, half[1]] = (f32(p2_ref[2, half[1]]) + f32(relay2_ref[1])).astype(jnp.bfloat16)
-    rsend(9, p2_ref.at[2, half[1]], in2_ref.at[1, half[1]], to_e(prv))
-    total = pair_sum(0)
-    rland(6, in2_ref.at[0, half[1]])
-    rland(7, in2_ref.at[1, half[0]])
-    rland(8, in2_ref.at[0, half[0]])
-    rland(9, in2_ref.at[1, half[1]])
-    total = (total + (f32(in2_ref[0]) + f32(in2_ref[1]))).astype(jnp.bfloat16)
-    for q in range(4):
-        stack_ref[q * 64 : (q + 1) * 64] = total[:, q * 1024 : (q + 1) * 1024]
-    part_back = jnp.dot(back_ref[...], stack_ref[...], preferred_element_type=jnp.float32)
-    back_out_ref[...] = part_back.astype(jnp.bfloat16).reshape(16, 16, 1024)
-    swap_blocks(bsend, bland, 0, back_out_ref, back_got_ref, s)
-    values = back_got_ref[...].reshape(256, 1024)
-    moe = jnp.dot(weigh_ref[0], values, preferred_element_type=jnp.float32) + jnp.dot(
-        weigh_ref[1], values, preferred_element_type=jnp.float32
-    )
-    for q in range(4):
-        cols = slice(q * 1024, (q + 1) * 1024)
-        o_ref[:, cols] = (f32(resid[:, cols]) + moe[q * 16 : (q + 1) * 16]).astype(jnp.bfloat16)
+    for v in range(2):
+        xarrive(2, sib, None, v)
+    experts(0)
+    for v in range(2):
+        xarrive(0, prv, None, v)
+        ref = rows_of(prv, 0, v)
+        xsend(v * 9 + 3, ref, ref, to_e(nxt))
+        ref = rows_of(prv, None, v)
+        xsend(v * 9 + 4, ref, ref, to_e(sib))
+        xarrive(1, nxt, None, v)
+        ref = rows_of(nxt, 1, v)
+        xsend(v * 9 + 5, ref, ref, to_e(prv))
+        ref = rows_of(nxt, None, v)
+        xsend(v * 9 + 6, ref, ref, to_e(sib))
+    for v in range(2):
+        xarrive(6, nxt ^ 1, None, v)
+    experts(1)
+    for v in range(2):
+        xarrive(3, far, 0, v)
+        ref = rows_of(far, 0, v)
+        xsend(v * 9 + 7, ref, ref, to_e(sib))
+        xarrive(5, far, 1, v)
+        ref = rows_of(far, 1, v)
+        xsend(v * 9 + 8, ref, ref, to_e(sib))
+    for v in range(2):
+        p2_ref[0, :, wide_cols[v]] = pair_sum(1, v).astype(jnp.bfloat16)
+        rsend(v * 10 + 6, p2_ref.at[0, half[1], wide_cols[v]], inbox(0, 1, v), to_e(nxt))
+    for v in range(2):
+        xarrive(7, far ^ 1, 0, v)
+        xarrive(8, far ^ 1, 1, v)
+    experts(2)
+    for v in range(2):
+        cols = wide_cols[v]
+        p2_ref[1, :, cols] = pair_sum(2, v).astype(jnp.bfloat16)
+        rsend(v * 10 + 4, p2_ref.at[1, half[0], cols], relay2_ref.at[0, :, cols], to_e(nxt))
+        rsend(v * 10 + 5, p2_ref.at[1, half[1], cols], relay2_ref.at[1, :, cols], to_e(prv))
+    for v in range(2):
+        xarrive(4, prv ^ 1, None, v)
+    experts(3)
+    for v in range(2):
+        cols = wide_cols[v]
+        add_relay(0, 0, 0, v)
+        rsend(v * 10 + 8, p2_ref.at[0, half[0], cols], inbox(0, 0, v), to_e(nxt))
+        p2_ref[2, :, cols] = pair_sum(3, v).astype(jnp.bfloat16)
+        rsend(v * 10 + 7, p2_ref.at[2, half[0], cols], inbox(1, 0, v), to_e(prv))
+        add_relay(1, 2, 1, v)
+        rsend(v * 10 + 9, p2_ref.at[2, half[1], cols], inbox(1, 1, v), to_e(prv))
+    for v in range(2):
+        cols = wide_cols[v]
+        total = pair_sum(0, v)
+        for m, side, h in ((6, 0, 1), (7, 1, 0), (8, 0, 0), (9, 1, 1)):
+            rland(v * 10 + m, inbox(side, h, v))
+        total = (total + (f32(in2_ref[0, :, cols]) + f32(in2_ref[1, :, cols]))).astype(jnp.bfloat16)
+        for q in range(4):
+            stack_ref[q * 64 : (q + 1) * 64, v * 512 : (v + 1) * 512] = total[:, q * 512 : (q + 1) * 512]
+        part_back = jnp.dot(
+            back_ref[...], stack_ref[:, v * 512 : (v + 1) * 512], preferred_element_type=jnp.float32
+        )
+        back_out_ref[:, :, v * 512 : (v + 1) * 512] = part_back.astype(jnp.bfloat16).reshape(16, 16, 512)
+        swap_send(bsend, 0, v, back_out_ref, back_got_ref, s)
+    for v in range(2):
+        swap_land(bland, 0, v, back_got_ref, s)
+        values = back_got_ref[:, :, v * 512 : (v + 1) * 512].reshape(256, 512)
+        moe = jnp.dot(weigh_ref[0], values, preferred_element_type=jnp.float32) + jnp.dot(
+            weigh_ref[1], values, preferred_element_type=jnp.float32
+        )
+        for q in range(4):
+            cols = slice(v * 2048 + q * 512, v * 2048 + (q + 1) * 512)
+            o_ref[:, cols] = (f32(resid[:, cols]) + moe[q * 16 : (q + 1) * 16]).astype(jnp.bfloat16)
     for copy in sent:
         copy.wait_send()
 
@@ -618,7 +655,7 @@
             pltpu.VMEM((256, 256), bf16),
             pltpu.VMEM((2, 64, 256), bf16),
             dma((6,)), dma((6,)), dma((10,)), dma((10,)), dma((4,)), dma((4,)),
-            dma((16,)), dma((16,)), dma((9,)), dma((9,)), dma((10,)), dma((10,)), dma((16,)), dma((16,)), dma((3,)),
+            dma((32,)), dma((32,)), dma((18,)), dma((18,)), dma((20,)), dma((20,)), dma((32,)), dma((32,)), dma((3,)),
         ],
         compiler_params=pltpu.CompilerParams(
             collective_id=collective_id, has_side_effects=True, vmem_limit_bytes=VMEM_LIMIT

time: 189 us -> 181 us (0.958)
  Pallas kernels: 187 us -> 179 us
    pallas_call x1, Pallas kernels: 102 us -> 94.6 us  [mix(): pl.pallas_call(mix_kernel, out_shape=jax.ShapeDtypeStruct((16, 4096), bf1...]
where the time goes in v6:
time: 181 us
  Pallas kernels  179 us (99%)
    pallas_call x1, Pallas kernels, mix(): pl.pallas_call(mix_kernel, out_shape=jax.ShapeDtypeStruct((16, 4096), bf1...  94.6 us
    pallas_call x1, Pallas kernels, project(): pl.pallas_call(project_kernel, out_shape=(out, out), in_specs=[pl.BlockSp...  48.1 us
    pallas_call x1, Pallas kernels, scan(): pl.pallas_call(scan_kernel, out_shape=(jax.ShapeDtypeStruct((tokens, widt...  36.2 us

profile of v6, /device:TPU:0, one launch (start us, length us, event | category | flops | bytes accessed | tf_op | source)
XLA Modules:
  0.0 180.6 jit_solution(17204698578461769666)
XLA Ops:
  0.0 48.1 %shard_map.163 = (f32[128,1024]{1,0:T(8,128)}, f32[128,1024]{1,0:T(8,128)}) custom-call(bf16[16,4096]{1,0:T(8,128)(2,1)} %tok_ref.3, f32[1,4096]{1,0:T(1,128)} %bitcast.9, bf16[2,256,1024]{2,1,0:T(8,128)(2,1)} %w_ref.2), custom_call_target="tpu_custom_call" | custom-call | tf_op jit(solution)/shard_map/pallas_call | solution.py:256
  48.1 36.2 %shard_map.164 = (bf16[128,1024]{1,0:T(8,128)(2,1)}, bf16[4,1024,256]{2,1,0:T(8,128)(2,1)}) custom-call(f32[128,1024]{1,0:T(8,128)} %get-tuple-element.9.x_ref, f32[128,1024]{1,0:T(8,128)} %get-tuple-element.10.z_ref, f32[4,1024]{1,0:T(4,128)} %taps_ref.1, f32[1,1024]{1,0:T(1,128)} %bitcast.11, bf16[288,1024]{1,0:T(8,128)(2,1)} %bitcast.8, ...), custom_call_target="tpu_custom_call" | custom-call | tf_op jit(solution)/shard_map/pallas_call | solution.py:835
  84.4 94.6 %shard_map.165 = bf16[16,4096]{1,0:T(8,128)(2,1)} custom-call(bf16[128,1024]{1,0:T(8,128)(2,1)} %get-tuple-element.11.gated_ref, bf16[4,1024,256]{2,1,0:T(8,128)(2,1)} %get-tuple-element.12.w_ref, bf16[16,4096]{1,0:T(8,128)(2,1)} %tok_ref.3, f32[1,4096]{1,0:T(1,128)} %bitcast.10, s32[2,16]{1,0:T(2,128)} %bitcast.14, f32[2,16]{1,0:T(2,128)} %bitcast.15, ...), custom_call_target="tpu_custom_call" | custom-call | tf_op jit(solution)/shard_map/pallas_call | solution.py:623
  179.0 1.6 copy.19

commit v7 on v6

--- a/solution.py
+++ b/solution.py
@@ -35,10 +35,11 @@
     )
 
 
-def greet(targets):
+def greet(targets, meanwhile=lambda: None):
     barrier = pltpu.get_barrier_semaphore()
     for target in targets:
         pl.semaphore_signal(barrier, inc=1, device_id=target, device_id_type=MESH)
+    meanwhile()
     pl.semaphore_wait(barrier, len(targets))
 
 
@@ -60,10 +61,21 @@
     reduce = ((at_z, along_z), (at_y, along_y))
     seq = lambda index: {"seq": index}
     exp = lambda index: {"expert": index}
+
+    def normalise():
+        wide = tok_ref[...].astype(jnp.float32)
+        scale = lax.rsqrt(jnp.mean(wide * wide, axis=-1, keepdims=True) + 1e-05)
+        normed = (wide * scale * gain_ref[...]).astype(jnp.bfloat16)
+        for q in range(4):
+            n_ref[0, q] = normed[:, q * 1024 : (q + 1) * 1024]
+            for r in range(4):
+                n_ref[1, q, :, r * 256 : (r + 1) * 256] = normed[:, (r * 4 + q) * 256 : (r * 4 + q + 1) * 256]
+
     greet(
         [seq(along_y(d)) for d in (1, 2, 3)]
         + [seq(along_z(d)) for d in (1, 2, 3)]
-        + [exp(sib), exp(nxt), exp(prv)]
+        + [exp(sib), exp(nxt), exp(prv)],
+        normalise,
     )
     half = w_ref.shape[1] // 2
     halves = (pl.ds(0, half), pl.ds(half, half))
@@ -102,13 +114,6 @@
         copy = pltpu.make_async_copy(w_ref.at[k], g_ref.at[k, at], local_sems.at[k])
         copy.start()
         own.append(copy)
-    wide = tok_ref[...].astype(jnp.float32)
-    scale = lax.rsqrt(jnp.mean(wide * wide, axis=-1, keepdims=True) + 1e-05)
-    normed = (wide * scale * gain_ref[...]).astype(jnp.bfloat16)
-    for q in range(4):
-        n_ref[0, q] = normed[:, q * 1024 : (q + 1) * 1024]
-        for r in range(4):
-            n_ref[1, q, :, r * 256 : (r + 1) * 256] = normed[:, (r * 4 + q) * 256 : (r * 4 + q + 1) * 256]
     mine = pl.ds(pl.multiple_of(e * 16, 16), 16)
     for k, (at, along) in enumerate(reduce):
         for d in (2, 1, 3):
@@ -155,6 +160,8 @@
         arrive(k, 1, nxt, 0)
         pass_on(k, 5, nxt, 2, prv)
         pass_on(k, 6, nxt, 0, sib)
+    if PARTS > 1:
+        pass_part(1)
     for k in range(2):
         arrive(k, 3, far, 1)
         pass_on(k, 7, far, 1, sib)
@@ -237,7 +244,7 @@
             for m, o, h in ((2, 3, 1), (3, 1, 0), (4, 2, 0), (5, 2, 1)):
                 land_part(c, k, m, o, h)
         multiply(c)
-        if c + 1 < PARTS:
+        if 0 < c < PARTS - 1:
             pass_part(c + 1)
         if c + 2 < PARTS:
             open_part(c + 2)
@@ -694,6 +701,22 @@
     at_y, along_y = ring_of(s, 0)
     at_z, along_z = ring_of(s, 1)
     tokens, width = x_ref.shape
+
+    def convolve(low, high):
+        rows = high - low
+        part = jnp.zeros((rows, xproj_ref.shape[0]), jnp.float32)
+        for at in range(0, width, 256):
+            cols = slice(at, at + 256)
+            conv = jnp.broadcast_to(cbias_ref[:, cols], (rows, 256))
+            for tap in range(CONV):
+                conv = conv + taps_ref[tap : tap + 1, cols] * pad_ref[5 + tap + low : 5 + tap + high, cols]
+            inner = (conv / (1.0 + jnp.exp(-conv))).astype(jnp.bfloat16)
+            inner_ref[low:high, cols] = inner
+            part = part + lax.dot_general(
+                inner, xproj_ref[:, cols], (((1,), (1,)), ((), ())), preferred_element_type=jnp.float32
+            )
+        part_ref[low // 16 : high // 16] = part.astype(jnp.bfloat16).reshape(rows // 16, 16, part.shape[1])
+
     greet(
         [{"expert": (e + d) % 8} for d in range(1, 8)]
         + [{"seq": (s + 1) % 16}, {"seq": (s + 15) % 16}]
@@ -717,20 +740,10 @@
     own.wait()
     ring_gather_open(wsend, 0, block, at_z, to_z)
     pad_ref[8:] = x_ref[...]
+    convolve(16, tokens)
     eland(0, pad_ref.at[pl.ds(0, 8)])
     pad_ref[:8] = jnp.where(s > 0, pad_ref[:8], 0.0)
-    part = jnp.zeros((tokens, xproj_ref.shape[0]), jnp.float32)
-    for at in range(0, width, 256):
-        cols = slice(at, at + 256)
-        conv = jnp.broadcast_to(cbias_ref[:, cols], (tokens, 256))
-        for tap in range(CONV):
-            conv = conv + taps_ref[tap : tap + 1, cols] * pad_ref[5 + tap : 5 + tap + tokens, cols]
-        inner = (conv / (1.0 + jnp.exp(-conv))).astype(jnp.bfloat16)
-        inner_ref[:, cols] = inner
-        part = part + lax.dot_general(
-            inner, xproj_ref[:, cols], (((1,), (1,)), ((), ())), preferred_element_type=jnp.float32
-        )
-    part_ref[...] = part.astype(jnp.bfloat16).reshape(8, tokens // 8, part.shape[1])
+    convolve(0, 16)
     for d in (4, 5, 3, 2, 6, 1, 7):
         to = (e + d) % 8
         asend(d, part_ref.at[to], rbox_ref.at[e], {"expert": to})

time: 181 us -> 177 us (0.978)
  Pallas kernels: 179 us -> 174 us
    pallas_call x1, Pallas kernels: 48.1 us -> 43.8 us  [project(): pl.pallas_call(project_kernel, out_shape=(out, out), in_specs=[pl.BlockSp...]
    pallas_call x1, Pallas kernels: 94.6 us -> 92.7 us  [mix(): pl.pallas_call(mix_kernel, out_shape=jax.ShapeDtypeStruct((16, 4096), bf1...]
where the time goes in v7:
time: 177 us; the launch traced here: 175 us
  Pallas kernels  174 us (98%)
    pallas_call x1, Pallas kernels, mix(): pl.pallas_call(mix_kernel, out_shape=jax.ShapeDtypeStruct((16, 4096), bf1...  92.7 us
    pallas_call x1, Pallas kernels, project(): pl.pallas_call(project_kernel, out_shape=(out, out), in_specs=[pl.BlockSp...  43.8 us
    pallas_call x1, Pallas kernels, scan(): pl.pallas_call(scan_kernel, out_shape=(jax.ShapeDtypeStruct((tokens, widt...  37.1 us

profile of v7, /device:TPU:0, one launch (start us, length us, event | category | flops | bytes accessed | tf_op | source)
XLA Modules:
  0.0 175.3 jit_solution(3998569886564183299)
XLA Ops:
  0.0 43.8 %shard_map.163 = (f32[128,1024]{1,0:T(8,128)}, f32[128,1024]{1,0:T(8,128)}) custom-call(bf16[16,4096]{1,0:T(8,128)(2,1)} %tok_ref.3, f32[1,4096]{1,0:T(1,128)} %bitcast.9, bf16[2,256,1024]{2,1,0:T(8,128)(2,1)} %w_ref.2), custom_call_target="tpu_custom_call" | custom-call | tf_op jit(solution)/shard_map/pallas_call | solution.py:263
  43.8 37.1 %shard_map.164 = (bf16[128,1024]{1,0:T(8,128)(2,1)}, bf16[4,1024,256]{2,1,0:T(8,128)(2,1)}) custom-call(f32[128,1024]{1,0:T(8,128)} %get-tuple-element.9.x_ref, f32[128,1024]{1,0:T(8,128)} %get-tuple-element.10.z_ref, f32[4,1024]{1,0:T(4,128)} %taps_ref.1, f32[1,1024]{1,0:T(1,128)} %bitcast.11, bf16[288,1024]{1,0:T(8,128)(2,1)} %bitcast.8, ...), custom_call_target="tpu_custom_call" | custom-call | tf_op jit(solution)/shard_map/pallas_call | solution.py:848
  80.9 92.7 %shard_map.165 = bf16[16,4096]{1,0:T(8,128)(2,1)} custom-call(bf16[128,1024]{1,0:T(8,128)(2,1)} %get-tuple-element.11.gated_ref, bf16[4,1024,256]{2,1,0:T(8,128)(2,1)} %get-tuple-element.12.w_ref, bf16[16,4096]{1,0:T(8,128)(2,1)} %tok_ref.3, f32[1,4096]{1,0:T(1,128)} %bitcast.10, s32[2,16]{1,0:T(2,128)} %bitcast.14, f32[2,16]{1,0:T(2,128)} %bitcast.15, ...), custom_call_target="tpu_custom_call" | custom-call | tf_op jit(solution)/shard_map/pallas_call | solution.py:630
  173.7 1.6 copy.19

commit v8 on v7

--- a/solution.py
+++ b/solution.py
@@ -428,9 +428,6 @@
     block = lambda i, h: gg_ref.at[i, span[h]]
     ring_gather_open(gsend, 0, block, at, to)
 
-    place_ref[...], weigh_ref[0], weigh_ref[1] = routing(ids_ref, gates_ref)
-    back_ref[...] = reorder(0)
-    order_ref[...] = reorder(1)
 
     def product(y):
         def tile(q, carry):
@@ -442,8 +439,11 @@
 
         lax.fori_loop(0, 4, tile, 0)
 
+    ring_gather_pass(gsend, gland, 0, block, at, to)
     product(at)
-    ring_gather_pass(gsend, gland, 0, block, at, to)
+    place_ref[...], weigh_ref[0], weigh_ref[1] = routing(ids_ref, gates_ref)
+    back_ref[...] = reorder(0)
+    order_ref[...] = reorder(1)
     gland(2, block((at + 3) % 4, 1))
     product((at + 3) % 4)
     gland(3, block((at + 1) % 4, 0))

time: 177 us -> 177 us (level)
  no operation moved by 1% of the time
where the time goes in v8:
time: 177 us; the launch traced here: 175 us
  Pallas kernels  174 us (98%)
    pallas_call x1, Pallas kernels, mix(): pl.pallas_call(mix_kernel, out_shape=jax.ShapeDtypeStruct((16, 4096), bf1...  92.7 us
    pallas_call x1, Pallas kernels, project(): pl.pallas_call(project_kernel, out_shape=(out, out), in_specs=[pl.BlockSp...  43.8 us
    pallas_call x1, Pallas kernels, scan(): pl.pallas_call(scan_kernel, out_shape=(jax.ShapeDtypeStruct((tokens, widt...  37.1 us

profile of v8, /device:TPU:0, one launch (start us, length us, event | category | flops | bytes accessed | tf_op | source)
XLA Modules:
  0.0 175.2 jit_solution(17372480309197857903)
XLA Ops:
  0.0 43.8 %shard_map.163 = (f32[128,1024]{1,0:T(8,128)}, f32[128,1024]{1,0:T(8,128)}) custom-call(bf16[16,4096]{1,0:T(8,128)(2,1)} %tok_ref.3, f32[1,4096]{1,0:T(1,128)} %bitcast.9, bf16[2,256,1024]{2,1,0:T(8,128)(2,1)} %w_ref.2), custom_call_target="tpu_custom_call" | custom-call | tf_op jit(solution)/shard_map/pallas_call | solution.py:263
  43.8 37.1 %shard_map.164 = (bf16[128,1024]{1,0:T(8,128)(2,1)}, bf16[4,1024,256]{2,1,0:T(8,128)(2,1)}) custom-call(f32[128,1024]{1,0:T(8,128)} %get-tuple-element.9.x_ref, f32[128,1024]{1,0:T(8,128)} %get-tuple-element.10.z_ref, f32[4,1024]{1,0:T(4,128)} %taps_ref.1, f32[1,1024]{1,0:T(1,128)} %bitcast.11, bf16[288,1024]{1,0:T(8,128)(2,1)} %bitcast.8, ...), custom_call_target="tpu_custom_call" | custom-call | tf_op jit(solution)/shard_map/pallas_call | solution.py:848
  80.9 92.7 %shard_map.165 = bf16[16,4096]{1,0:T(8,128)(2,1)} custom-call(bf16[128,1024]{1,0:T(8,128)(2,1)} %get-tuple-element.11.gated_ref, bf16[4,1024,256]{2,1,0:T(8,128)(2,1)} %get-tuple-element.12.w_ref, bf16[16,4096]{1,0:T(8,128)(2,1)} %tok_ref.3, f32[1,4096]{1,0:T(1,128)} %bitcast.10, s32[2,16]{1,0:T(2,128)} %bitcast.14, f32[2,16]{1,0:T(2,128)} %bitcast.15, ...), custom_call_target="tpu_custom_call" | custom-call | tf_op jit(solution)/shard_map/pallas_call | solution.py:630
  173.7 1.6 copy.19
